TPU v7x, 128 devices: a whole 4x4x4 slice. The times are simulated.
128 devices in a mesh: seq: 8 (over y, core), tensor: 16 (over z, x).
Axes of the slice: x: 4, y: 4, z: 4, core: 2. Of those that a mesh axis runs over, the one named last changes fastest.
Arguments:
- hidden_rows: bfloat16 [24576, 2560], P(('seq', 'tensor')), may hold values from -6 to 6
- value_weight: bfloat16 [2560, 5120], P(None, 'tensor'), may hold values from -0.125 to 0.125
- gating_weight: bfloat16 [2560, 5120], P(None, 'tensor'), may hold values from -0.125 to 0.125
- state_weight: bfloat16 [2560, 256], replicated, may hold values from -0.125 to 0.125
- step_weight: bfloat16 [2560, 80], P(None, 'tensor'), may hold values from -0.125 to 0.125
- value_kernel: float32 [4, 5120], P(None, 'tensor'), may hold values from -3 to 3
- state_kernel: float32 [4, 256], replicated, may hold values from -3 to 3
- step_bias: float32 [80], P('tensor'), may hold values from -4.5 to -3.5
- decay_log: float32 [80], P('tensor'), may hold values from -10 to 1.5
- skip_scale: float32 [80], P('tensor'), may hold values from 0.1 to 4
- norm_scale: float32 [5120], P('tensor'), may hold values from 0.5 to 1.5
- document_lengths: int32 [16], replicated, may hold values from 1 to 12288, 24576 in all
Outputs:
- layer_out: bfloat16 [24576, 5120], P('seq', 'tensor')
Inputs may be any that keep to these rules, and one draw needn't show every extreme that they name: `document_lengths`: the 16 documents of the pack in order; their lengths sum to 24576.
All inputs are finite; a program needn't handle non-finite values.
Results may differ from a plain program's by a relative error of at most 0.0061.
Values may be sent and summed in bfloat16 or wider, within the bound.
No kernel may reach another device: no remote copies, remote signals or barrier semaphores. Data moves between devices by JAX's collectives and lax.ppermute only.
A program may use at most 128 MiB of HBM per device.

v0:
```python
import jax
import jax.numpy as jnp
from jax import lax
from jax.sharding import PartitionSpec as P

KCONV = 4
Q = 256


def from_behind(array, axis, by):
    length = lax.axis_size(axis)
    pairs = [(i, i + by) for i in range(length) if 0 <= i + by < length]
    return lax.ppermute(array, axis, pairs)


def carried_in(part, axis, combine, identity):
    place = lax.axis_index(axis)
    gathered = jax.tree.map(lambda a: lax.all_gather(a, axis), part)
    state = jax.tree.map(lambda a, e: jnp.zeros_like(a) + jnp.asarray(e, a.dtype), part, identity)

    def one(turn, state):
        return combine(
            state, jax.tree.map(lambda a: lax.dynamic_index_in_dim(a, turn, 0, False), gathered)
        )

    return lax.fori_loop(0, place, one, state)


def document_ids(positions, document_lengths):
    boundary = jnp.cumsum(document_lengths) - document_lengths
    hits = (positions[:, None] >= boundary[None, :]).astype(jnp.int32)
    return jnp.sum(hits, axis=1) - 1


def block_update(carry_state, inputs, skip_scale):
    values, input_map, output_map, step_size, log_decay, documents, before = inputs
    precise = lax.Precision.HIGHEST
    running = jnp.cumsum(log_decay, axis=0)
    index_range = jnp.arange(documents.shape[0])
    allowed = (documents[:, None] == documents[None, :]) & (
        index_range[:, None] >= index_range[None, :]
    )
    spread = running[:, None, :] - running[None, :, :]
    factor = jnp.where(
        allowed[:, :, None], jnp.exp(jnp.where(allowed[:, :, None], spread, 0.0)), 0.0
    )
    scores = jnp.dot(output_map, input_map.T, precision=precise)
    mixing = scores[:, :, None] * factor * step_size[None, :, :]
    inner_part = jnp.einsum("ijh,jhp->ihp", mixing, values, precision=precise)
    carried = (documents == before).astype(jnp.float32)
    entering = jnp.einsum("in,hnp->ihp", output_map, carry_state, precision=precise)
    entering = entering * (carried[:, None] * jnp.exp(running))[:, :, None]
    tail_weight = (
        jnp.where(
            (documents == documents[-1])[:, None], jnp.exp(running[-1][None, :] - running), 0.0
        )
        * step_size
    )
    update = jnp.einsum(
        "jn,jhp->hnp", input_map, values * tail_weight[:, :, None], precision=precise
    )
    passing = carried[-1] * jnp.exp(running[-1])
    new_state = passing[:, None, None] * carry_state + update
    output = inner_part + entering + skip_scale[None, :, None] * values
    return (new_state, output)


def on_device(
    hidden_rows,
    value_weight,
    gating_weight,
    state_weight,
    step_weight,
    value_kernel,
    state_kernel,
    step_bias,
    decay_log,
    skip_scale,
    norm_scale,
    document_lengths,
):
    members = lax.axis_size("tensor")
    row_count = hidden_rows.shape[0] * members
    inner_width = value_weight.shape[1]
    head_count = step_weight.shape[1]
    head_width = inner_width // head_count
    state_count = state_weight.shape[1] // 2
    precise = lax.Precision.HIGHEST
    joined = jnp.concatenate([value_weight, gating_weight, state_weight, step_weight], 1)
    projected = jnp.dot(
        lax.all_gather(hidden_rows, "tensor", axis=0, tiled=True),
        joined,
        preferred_element_type=jnp.float32,
    ).astype(jnp.bfloat16)
    map_raw = projected[:, 2 * inner_width : 2 * inner_width + 2 * state_count]
    step_raw = projected[:, 2 * inner_width + 2 * state_count :]
    value_raw = projected[:, :inner_width]
    gating_raw = projected[:, inner_width : 2 * inner_width]
    raw_inputs = jnp.concatenate([value_raw, map_raw], 1)
    conv_rim = from_behind(raw_inputs[row_count - (KCONV - 1) :], "seq", 1)
    padded = jnp.concatenate([conv_rim, raw_inputs], 0)
    row_offset = lax.axis_index("seq") * row_count
    positions = row_offset + jnp.arange(-(KCONV - 1), row_count, dtype=jnp.int32)
    documents_ext = document_ids(positions, document_lengths)
    documents = documents_ext[KCONV - 1 :]
    kernel = jnp.concatenate([value_kernel, state_kernel], 1)
    row_total = jnp.zeros(raw_inputs.shape, jnp.float32)
    for offset in range(KCONV):
        first_row = KCONV - 1 - offset
        shifted = padded[first_row : first_row + row_count].astype(jnp.float32)
        keep_mask = (documents_ext[first_row : first_row + row_count] == documents).astype(
            jnp.float32
        )
        row_total = row_total + kernel[offset][None, :] * shifted * keep_mask[:, None]
    conv_out = jax.nn.silu(row_total).astype(jnp.bfloat16)
    values = (
        conv_out[:, :inner_width].astype(jnp.float32).reshape(row_count, head_count, head_width)
    )
    input_map = conv_out[:, inner_width : inner_width + state_count].astype(jnp.float32)
    output_map = conv_out[:, inner_width + state_count :].astype(jnp.float32)
    step_size = jax.nn.softplus(step_raw.astype(jnp.float32) + step_bias[None, :])
    log_decay = -jnp.exp(decay_log)[None, :] * step_size
    running = jnp.cumsum(log_decay, axis=0)
    tail_weight = (
        jnp.where(
            (documents == documents[-1])[:, None], jnp.exp(running[-1][None, :] - running), 0.0
        )
        * step_size
    )
    summary = jnp.einsum(
        "rn,rhp->hnp", input_map, values * tail_weight[:, :, None], precision=precise
    )
    passing = (documents[-1] == documents_ext[KCONV - 2]).astype(jnp.float32) * jnp.exp(running[-1])

    def combine(earlier_part, later_part):
        return (
            earlier_part[0] * later_part[0],
            later_part[0][:, None, None] * earlier_part[1] + later_part[1],
        )

    identity = (jnp.ones_like(passing), jnp.zeros_like(summary))
    entering = carried_in((passing, summary), "seq", combine, identity)[1]
    block_count = row_count // Q
    before_all = documents_ext[KCONV - 2 : KCONV - 2 + row_count]
    inputs = (
        values.reshape(block_count, Q, head_count, head_width),
        input_map.reshape(block_count, Q, state_count),
        output_map.reshape(block_count, Q, state_count),
        step_size.reshape(block_count, Q, head_count),
        log_decay.reshape(block_count, Q, head_count),
        documents.reshape(block_count, Q),
        before_all.reshape(block_count, Q)[:, 0],
    )

    def advance(carry_state, block_inputs):
        return block_update(carry_state, block_inputs, skip_scale)

    unused, outputs = lax.scan(advance, entering, inputs)
    ssd_out = outputs.reshape(row_count, inner_width)
    gated_out = ssd_out * jax.nn.silu(gating_raw.astype(jnp.float32))
    row_squares = jnp.sum(gated_out * gated_out, axis=1)
    squares_total = lax.psum(row_squares, "tensor")
    mean_square = squares_total / (inner_width * members)
    return (gated_out * lax.rsqrt(mean_square[:, None] + 1e-05) * norm_scale[None, :]).astype(
        jnp.bfloat16
    )


def solution(mesh):
    in_specs = (
        P(("seq", "tensor"), None),
        P(None, "tensor"),
        P(None, "tensor"),
        P(),
        P(None, "tensor"),
        P(None, "tensor"),
        P(),
        P("tensor"),
        P("tensor"),
        P("tensor"),
        P("tensor"),
        P(),
    )
    out_specs = P("seq", "tensor")
    return jax.shard_map(
        on_device, mesh=mesh, in_specs=in_specs, out_specs=out_specs, check_vma=False
    )
```

profile of v0, /device:TPU:16, one launch (start us, length us, event | category | flops | bytes accessed | tf_op | source)
XLA Modules:
  0.0 574.3 jit_solution(5619878274382889432)
XLA Ops:
  16.7 101.1 %all-gather.5.cloned.1.call-done = bf16[3072,2560]{1,0:T(8,128)(2,1)} async-done(((bf16[192,2560]{1,0:T(8,128)(2,1)}), bf16[3072,2560]{1,0:T(8,128)(2,1)}) %all-gather.5.cloned.1.call-update) | async-done | bytes 15728656 | tf_op jit(solution)/shard_map/all_gather | solution.py:91
  117.8 18.5 %convert_bitcast_fusion = bf16[3072,901]{0,1:T(8,128)(2,1)S(1)} fusion(bf16[3072,2560]{1,0:T(8,128)(2,1)} %all-gather.5.cloned.1.call-done, bf16[2560,5]{0,1:T(8,128)(2,1)} %param.20, bf16[2560,256]{0,1:T(8,128)(2,1)S(1)} %copy.124, bf16[2560,320]{0,1:T(8,128)(2,1)} %param.18, bf16[2560,320]{0,1:T(8,128)(2,1)} %param.17), kind=kOutput, calls=%fused_computation.58 | convolution fusion | flops 14192724992 | bytes 25877504 | tf_op jit(solution)/shard_map/dot_general | solution.py:90
  136.6 2.1 copy-done.3
  140.2 3.6 reduce-window.30
  148.0 2.1 collective-permute-start
  151.8 2.7 collective-permute-done
  154.4 4.9 maximum_maximum_fusion
  159.4 8.3 %multiply_convert_fusion = bf16[3072,576]{0,1:T(8,128)(2,1)S(1)} fusion(bf16[3072,256]{0,1:T(8,128)(2,1)S(1)} %slice.132, bf16[3072,320]{0,1:T(8,128)(2,1)S(1)} %slice.131, bf16[3075,576]{0,1:T(8,128)(2,1)S(1)} %maximum_maximum_fusion, f32[3072]{0:T(1024)S(1)} %copy-done.5, f32[576]{0:T(1024)S(1)} %copy-done.9, f32[3072]{0:T(1024)S(1)} %copy-done.6, ...), kind=kLoop, calls=%fused_computation.57 | loop fusion | flops 38928384 | bytes 17740800 | tf_op jit(solution)/shard_map/convert_element_type | solution.py:115
  170.6 2.7 fusion.61
  173.6 8.3 %all-gather.1 = f32[8,1,5]{2,1,0:T(1,128)S(1)} all-gather(f32[1,1,5]{2,1,0:T(1,128)S(1)} %bitcast.188), channel_id=1, replica_groups=mesh['seq'=8,'tensor'=16] {'seq'}, dimensions={0}, use_global_device_ids=true | all-gather | bytes 180 | tf_op jit(solution)/shard_map/all_gather | solution.py:18
  181.9 5.3 reshape_reshape.3
  187.2 1.7 slice_convert_fusion.1
  191.1 4.8 all-gather.7.cloned.1.call-done
  195.9 5.3 while.24
  201.3 275.0 %while.25 = (s32[]{:T(128)}, f32[5,128,64]{1,2,0:T(8,128)S(1)}, f32[12,256,5,64]{1,0,3,2:T(8,128)}, s32[12,256]{1,0:T(8,128)S(1)}, s32[12]{0:T(128)S(1)}, /*inde...) while((s32[]{:T(128)}, f32[5,128,64]{1,2,0:T(8,128)S(1)}, ...), condition=%wide.region_9.10_spmd, body=%wide.region_6.9_spmd.sunk | while | flops 606476032 | bytes 5385013 | solution.py:158
  209.9 2.0 constant_dynamic-slice_fusion.7
  213.2 1.7 fusion.107
  215.8 8.4 %dynamic_update_slice.5 = f32[12,256,5,64]{1,0,3,2:T(8,128)} dynamic-update-slice(f32[12,256,5,64]{1,0,3,2:T(8,128)} %get-tuple-element.426, f32[1,256,5,64]{1,0,3,2:T(1,128)S(1)} %copy.182, s32[]{:T(128)S(6)} %copy.193, s32[]{:T(128)} %constant.67.clone.1..sunk.1, s32[]{:T(128)} %constant.67.clone.1..sunk.1, s32[]{:T(128)} %constant.67.clone.1..sunk.1) | dynamic-update-slice | bytes 655364 | tf_op jit(solution)/shard_map/while/body/jit(dynamic_update_index_in_dim)/dynamic_update_slice | solution.py:158
  232.8 2.0 constant_dynamic-slice_fusion.7
  236.2 1.7 fusion.107
  238.7 8.4 %dynamic_update_slice.5 = f32[12,256,5,64]{1,0,3,2:T(8,128)} dynamic-update-slice(f32[12,256,5,64]{1,0,3,2:T(8,128)} %get-tuple-element.426, f32[1,256,5,64]{1,0,3,2:T(1,128)S(1)} %copy.182, s32[]{:T(128)S(6)} %copy.193, s32[]{:T(128)} %constant.67.clone.1..sunk.1, s32[]{:T(128)} %constant.67.clone.1..sunk.1, s32[]{:T(128)} %constant.67.clone.1..sunk.1) | dynamic-update-slice | bytes 655364 | tf_op jit(solution)/shard_map/while/body/jit(dynamic_update_index_in_dim)/dynamic_update_slice | solution.py:158
  255.7 2.0 constant_dynamic-slice_fusion.7
  259.1 1.7 fusion.107
  261.6 8.4 %dynamic_update_slice.5 = f32[12,256,5,64]{1,0,3,2:T(8,128)} dynamic-update-slice(f32[12,256,5,64]{1,0,3,2:T(8,128)} %get-tuple-element.426, f32[1,256,5,64]{1,0,3,2:T(1,128)S(1)} %copy.182, s32[]{:T(128)S(6)} %copy.193, s32[]{:T(128)} %constant.67.clone.1..sunk.1, s32[]{:T(128)} %constant.67.clone.1..sunk.1, s32[]{:T(128)} %constant.67.clone.1..sunk.1) | dynamic-update-slice | bytes 655364 | tf_op jit(solution)/shard_map/while/body/jit(dynamic_update_index_in_dim)/dynamic_update_slice | solution.py:158
  278.7 2.0 constant_dynamic-slice_fusion.7
  284.5 8.4 %dynamic_update_slice.5 = f32[12,256,5,64]{1,0,3,2:T(8,128)} dynamic-update-slice(f32[12,256,5,64]{1,0,3,2:T(8,128)} %get-tuple-element.426, f32[1,256,5,64]{1,0,3,2:T(1,128)S(1)} %copy.182, s32[]{:T(128)S(6)} %copy.193, s32[]{:T(128)} %constant.67.clone.1..sunk.1, s32[]{:T(128)} %constant.67.clone.1..sunk.1, s32[]{:T(128)} %constant.67.clone.1..sunk.1) | dynamic-update-slice | bytes 655364 | tf_op jit(solution)/shard_map/while/body/jit(dynamic_update_index_in_dim)/dynamic_update_slice | solution.py:158
  301.6 2.0 constant_dynamic-slice_fusion.7
  304.9 1.7 fusion.107
  307.4 8.4 %dynamic_update_slice.5 = f32[12,256,5,64]{1,0,3,2:T(8,128)} dynamic-update-slice(f32[12,256,5,64]{1,0,3,2:T(8,128)} %get-tuple-element.426, f32[1,256,5,64]{1,0,3,2:T(1,128)S(1)} %copy.182, s32[]{:T(128)S(6)} %copy.193, s32[]{:T(128)} %constant.67.clone.1..sunk.1, s32[]{:T(128)} %constant.67.clone.1..sunk.1, s32[]{:T(128)} %constant.67.clone.1..sunk.1) | dynamic-update-slice | bytes 655364 | tf_op jit(solution)/shard_map/while/body/jit(dynamic_update_index_in_dim)/dynamic_update_slice | solution.py:158
  324.5 2.0 constant_dynamic-slice_fusion.7
  330.3 8.4 %dynamic_update_slice.5 = f32[12,256,5,64]{1,0,3,2:T(8,128)} dynamic-update-slice(f32[12,256,5,64]{1,0,3,2:T(8,128)} %get-tuple-element.426, f32[1,256,5,64]{1,0,3,2:T(1,128)S(1)} %copy.182, s32[]{:T(128)S(6)} %copy.193, s32[]{:T(128)} %constant.67.clone.1..sunk.1, s32[]{:T(128)} %constant.67.clone.1..sunk.1, s32[]{:T(128)} %constant.67.clone.1..sunk.1) | dynamic-update-slice | bytes 655364 | tf_op jit(solution)/shard_map/while/body/jit(dynamic_update_index_in_dim)/dynamic_update_slice | solution.py:158
  347.4 2.0 constant_dynamic-slice_fusion.7
  353.3 8.4 %dynamic_update_slice.5 = f32[12,256,5,64]{1,0,3,2:T(8,128)} dynamic-update-slice(f32[12,256,5,64]{1,0,3,2:T(8,128)} %get-tuple-element.426, f32[1,256,5,64]{1,0,3,2:T(1,128)S(1)} %copy.182, s32[]{:T(128)S(6)} %copy.193, s32[]{:T(128)} %constant.67.clone.1..sunk.1, s32[]{:T(128)} %constant.67.clone.1..sunk.1, s32[]{:T(128)} %constant.67.clone.1..sunk.1) | dynamic-update-slice | bytes 655364 | tf_op jit(solution)/shard_map/while/body/jit(dynamic_update_index_in_dim)/dynamic_update_slice | solution.py:158
  370.3 2.0 constant_dynamic-slice_fusion.7
  376.2 8.4 %dynamic_update_slice.5 = f32[12,256,5,64]{1,0,3,2:T(8,128)} dynamic-update-slice(f32[12,256,5,64]{1,0,3,2:T(8,128)} %get-tuple-element.426, f32[1,256,5,64]{1,0,3,2:T(1,128)S(1)} %copy.182, s32[]{:T(128)S(6)} %copy.193, s32[]{:T(128)} %constant.67.clone.1..sunk.1, s32[]{:T(128)} %constant.67.clone.1..sunk.1, s32[]{:T(128)} %constant.67.clone.1..sunk.1) | dynamic-update-slice | bytes 655364 | tf_op jit(solution)/shard_map/while/body/jit(dynamic_update_index_in_dim)/dynamic_update_slice | solution.py:158
  393.2 2.0 constant_dynamic-slice_fusion.7
  399.1 8.4 %dynamic_update_slice.5 = f32[12,256,5,64]{1,0,3,2:T(8,128)} dynamic-update-slice(f32[12,256,5,64]{1,0,3,2:T(8,128)} %get-tuple-element.426, f32[1,256,5,64]{1,0,3,2:T(1,128)S(1)} %copy.182, s32[]{:T(128)S(6)} %copy.193, s32[]{:T(128)} %constant.67.clone.1..sunk.1, s32[]{:T(128)} %constant.67.clone.1..sunk.1, s32[]{:T(128)} %constant.67.clone.1..sunk.1) | dynamic-update-slice | bytes 655364 | tf_op jit(solution)/shard_map/while/body/jit(dynamic_update_index_in_dim)/dynamic_update_slice | solution.py:158
  416.1 2.0 constant_dynamic-slice_fusion.7
  422.0 8.4 %dynamic_update_slice.5 = f32[12,256,5,64]{1,0,3,2:T(8,128)} dynamic-update-slice(f32[12,256,5,64]{1,0,3,2:T(8,128)} %get-tuple-element.426, f32[1,256,5,64]{1,0,3,2:T(1,128)S(1)} %copy.182, s32[]{:T(128)S(6)} %copy.193, s32[]{:T(128)} %constant.67.clone.1..sunk.1, s32[]{:T(128)} %constant.67.clone.1..sunk.1, s32[]{:T(128)} %constant.67.clone.1..sunk.1) | dynamic-update-slice | bytes 655364 | tf_op jit(solution)/shard_map/while/body/jit(dynamic_update_index_in_dim)/dynamic_update_slice | solution.py:158
  439.1 2.0 constant_dynamic-slice_fusion.7
  444.9 8.4 %dynamic_update_slice.5 = f32[12,256,5,64]{1,0,3,2:T(8,128)} dynamic-update-slice(f32[12,256,5,64]{1,0,3,2:T(8,128)} %get-tuple-element.426, f32[1,256,5,64]{1,0,3,2:T(1,128)S(1)} %copy.182, s32[]{:T(128)S(6)} %copy.193, s32[]{:T(128)} %constant.67.clone.1..sunk.1, s32[]{:T(128)} %constant.67.clone.1..sunk.1, s32[]{:T(128)} %constant.67.clone.1..sunk.1) | dynamic-update-slice | bytes 655364 | tf_op jit(solution)/shard_map/while/body/jit(dynamic_update_index_in_dim)/dynamic_update_slice | solution.py:158
  462.0 2.0 constant_dynamic-slice_fusion.7
  467.8 8.4 %dynamic_update_slice.5 = f32[12,256,5,64]{1,0,3,2:T(8,128)} dynamic-update-slice(f32[12,256,5,64]{1,0,3,2:T(8,128)} %get-tuple-element.426, f32[1,256,5,64]{1,0,3,2:T(1,128)S(1)} %copy.182, s32[]{:T(128)S(6)} %copy.193, s32[]{:T(128)} %constant.67.clone.1..sunk.1, s32[]{:T(128)} %constant.67.clone.1..sunk.1, s32[]{:T(128)} %constant.67.clone.1..sunk.1) | dynamic-update-slice | bytes 655364 | tf_op jit(solution)/shard_map/while/body/jit(dynamic_update_index_in_dim)/dynamic_update_slice | solution.py:158
  476.3 6.1 %copy.146 = f32[40,8,12,256]{3,1,2,0:T(8,128)S(1)} copy(f32[40,8,12,256]{3,2,1,0:T(8,128)} %bitcast.175) | data formatting | bytes 7864320
  482.4 1.9 copy-done
  484.4 3.1 multiply_reduce_fusion
  487.4 74.5 %psum.7 = f32[3072]{0:T(1024)S(1)} all-reduce(f32[3072]{0:T(1024)S(1)} %multiply_reduce_fusion), channel_id=1, replica_groups=mesh['seq'=8,'tensor'=16] {'tensor'}, use_global_device_ids=true, to_apply=%region_11.12 | all-reduce | flops 3072 | bytes 24576 | tf_op jit(solution)/shard_map/psum | solution.py:162
  561.9 5.6 multiply_convert_fusion.1
  (372 shorter events, 169.1 us)
Async XLA Ops:
  6.5 111.3 %all-gather.5.cloned.1.call-start = ((), (), s32[]{:S(2)}) async-start(), calls=%async_computation | async-start | bytes 16711680 | tf_op jit(solution)/shard_map/all_gather | solution.py:91
  7.3 188.6 %all-gather.7.cloned.1.call-start = ((), (), s32[]{:S(2)}) async-start(), calls=%async_computation.1 | async-start | bytes 1474560 | tf_op jit(solution)/shard_map/all_gather | solution.py:18
  136.3 2.4 copy-start.3
  136.4 2.4 copy-start.14
  136.4 2.4 copy-start.16
  146.8 4.0 copy-start.11
  146.8 4.0 copy-start.15
  147.9 11.4 %copy-start.4 = (f32[3072]{0:T(1024)S(1)}, f32[3072]{0:T(1024)}, u32[]{:S(2)}) copy-start(f32[3072]{0:T(1024)} %get-tuple-element.271) | copy-start | bytes 36868
  147.9 11.4 %copy-start.5 = (f32[3072]{0:T(1024)S(1)}, f32[3072]{0:T(1024)}, u32[]{:S(2)}) copy-start(f32[3072]{0:T(1024)} %get-tuple-element.272) | copy-start | bytes 36868
  147.9 11.4 %copy-start.6 = (f32[3072]{0:T(1024)S(1)}, f32[3072]{0:T(1024)}, u32[]{:S(2)}) copy-start(f32[3072]{0:T(1024)} %get-tuple-element.273) | copy-start | bytes 36868
  147.9 11.4 %copy-start.7 = (f32[576]{0:T(1024)S(1)}, f32[576]{0:T(1024)}, u32[]{:S(2)}) copy-start(f32[576]{0:T(1024)} %get-tuple-element.222) | copy-start | bytes 6916
  147.9 11.4 %copy-start.8 = (f32[576]{0:T(1024)S(1)}, f32[576]{0:T(1024)}, u32[]{:S(2)}) copy-start(f32[576]{0:T(1024)} %get-tuple-element.223) | copy-start | bytes 6916
  148.0 11.4 %copy-start.9 = (f32[576]{0:T(1024)S(1)}, f32[576]{0:T(1024)}, u32[]{:S(2)}) copy-start(f32[576]{0:T(1024)} %get-tuple-element.224) | copy-start | bytes 6916
  148.0 11.4 %copy-start.10 = (f32[576]{0:T(1024)S(1)}, f32[576]{0:T(1024)}, u32[]{:S(2)}) copy-start(f32[576]{0:T(1024)} %get-tuple-element.225) | copy-start | bytes 6916
  148.0 6.5 %collective-permute-start = (bf16[3,576]{0,1:T(8,128)(2,1)S(1)}, bf16[3,576]{0,1:T(8,128)(2,1)S(1)}, u32[]{:S(2)}, u32[]{:S(2)}) collective-permute-start(bf16[3,576]{0,1:T(8,128)(2,1)S(1)} %fusion.66), channel_id=1, source_target_pairs={{0,16},{16,32},{32,48},{48,64},{64,80},{80,96},{96,112},{1,17},{17... | collective-permute-start | bytes 10376 | tf_op jit(solution)/shard_map/ppermute | solution.py:13
  167.7 1.8 copy-start.2
  168.2 2.5 copy-start.1
  168.2 5.4 copy-start.13
  195.8 5.4 copy-start.17
  482.4 1.9 copy-start
  482.4 79.5 %copy-start.12 = (f32[320]{0:T(512)S(1)}, f32[320]{0:T(512)}, u32[]{:S(2)}) copy-start(f32[320]{0:T(512)} %param.26) | copy-start | bytes 3844
Sparse Core Ops, SparseCore 0:
  9.5 108.2 all-gather.4
  173.5 22.2 all-gather.6
where the time goes:
time: 582 us; the launch traced here: 574 us
  local copies, waits for them, and re-layouts  195 us (34%)
  waiting for transfers between devices  109 us (19%)
  other arithmetic  89.8 us (15%)
  blocking collectives  82.8 us (14%)
  matrix products  79 us (14%)
  between operations  15.1 us (3%)
    dynamic_update_slice x24, local copies, waits for them, and re-layouts, on_device(): unused, outputs = lax.scan(advance, entering, inputs)  105 us
    all_gather x1, waiting for transfers between devices, on_device(): lax.all_gather(hidden_rows, 'tensor', axis=0, tiled=True)  101 us
    psum x1, blocking collectives, on_device(): squares_total = lax.psum(row_squares, 'tensor')  74.5 us
    dynamic_slice x36, local copies, waits for them, and re-layouts, on_device(): unused, outputs = lax.scan(advance, entering, inputs)  30.7 us
    another operation x28, other arithmetic  23.7 us
    dot_general x12, matrix products, block_update(): inner_part = jnp.einsum('ijh,jhp->ihp', mixing, values, precision=precise)  20.5 us
    dot_general x1, matrix products, on_device(): jnp.dot(lax.all_gather(hidden_rows, 'tensor', axis=0, tiled=True), joined...  18.5 us
    while x12, matrix products  16.1 us
  transfers between devices with their start and end apart: 3, of which 3 were waited for; matrix products, arithmetic and copies ran while one was open for 3% of the time, Pallas kernels for 0%

commit v1 on v0

v1 whole, which is shorter than its diff:
```python
import functools

import jax
import jax.numpy as jnp
from jax import lax
from jax.experimental import pallas as pl
from jax.experimental.pallas import tpu as pltpu
from jax.sharding import PartitionSpec as P

KCONV = 4
Q = 256
LANES = 128
SIDE = 4
REACH = 4
F32 = jnp.float32
BF16 = jnp.bfloat16


def dot(a, b, contract=((1,), (0,))):
    return lax.dot_general(a, b, (contract, ((), ())), preferred_element_type=F32)


def halves(a):
    high = a.astype(BF16)
    return high, (a - high.astype(F32)).astype(BF16)


def thirds(a):
    high = a.astype(BF16)
    rest = a - high.astype(F32)
    middle = rest.astype(BF16)
    return high, middle, (rest - middle.astype(F32)).astype(BF16)


def spread_heads(a, expand):
    high, low = halves(a)
    return dot(high, expand) + dot(low, expand)


def silu(v):
    half = 0.5 * v
    return half + half * jnp.tanh(half)


def ssd_kernel(
    heads,
    lane0,
    step_col,
    wide,
    proj_ref,
    rim_ref,
    seg_ref,
    taps_ref,
    vectors_ref,
    skip_ref,
    expand_ref,
    y_ref,
    reach_ref,
    map_ref,
    state_ref,
    rows,
    state,
    total,
):
    block = pl.program_id(0)
    raw_wide = wide + 2 * LANES

    @pl.when(block == 0)
    def _():
        rows[0:8, :] = rim_ref[...].astype(F32)
        state[...] = jnp.zeros_like(state)
        total[...] = jnp.zeros_like(total)

    rows[8:, :wide] = proj_ref[:, :wide].astype(F32)
    rows[8:, wide:] = proj_ref[:, 2 * wide : 2 * wide + 2 * LANES].astype(F32)
    first = block * Q
    seg = seg_ref[...] - first
    place = lax.broadcasted_iota(jnp.int32, (Q, LANES), 0)
    keep = [place - k >= seg for k in range(1, KCONV)]
    pieces = []
    for tile in range(raw_wide // LANES):
        at = slice(tile * LANES, (tile + 1) * LANES)
        sums = taps_ref[0:1, at] * rows[8:, at]
        for k in range(1, KCONV):
            sums = sums + jnp.where(keep[k - 1], taps_ref[k : k + 1, at] * rows[8 - k : 8 - k + Q, at], 0.0)
        pieces.append(silu(sums).astype(BF16))
    rows[0:8, :] = rows[Q : Q + 8, :]
    tiles = wide // LANES
    values = jnp.concatenate([p.astype(F32) for p in pieces[:tiles]], 1)
    input_map, output_map = pieces[tiles], pieces[tiles + 1]
    map_ref[...] = output_map

    v = proj_ref[:, step_col : step_col + LANES].astype(F32) + vectors_ref[0:1, :]
    step = jnp.maximum(v, 0.0) + jnp.log(1.0 + jnp.exp(-jnp.abs(v)))
    decay = vectors_ref[1:2, :] * step
    ii = lax.broadcasted_iota(jnp.int32, (Q, Q), 0)
    jj = lax.broadcasted_iota(jnp.int32, (Q, Q), 1)
    causal = (jj <= ii).astype(F32).astype(BF16)
    running = sum(dot(causal, part) for part in thirds(decay))
    running_t = running.T
    barred = jnp.where((jj <= ii) & (jj >= jnp.concatenate([seg, seg], 1)), 0.0, -1e30)
    last = running[Q - 1 : Q, :]
    last_seg = seg[Q - 1 : Q, :]
    carried = jnp.where(seg < 0, jnp.exp(running), 0.0)
    tail = jnp.where(place >= last_seg, jnp.exp(last - running), 0.0) * step
    reach_ref[...] = jnp.where(seg + first < 0, jnp.exp(total[0:1, :] + running), 0.0)
    total[0:1, :] = total[0:1, :] + last

    expand = expand_ref[...]
    carried_wide = spread_heads(carried, expand)
    stepped = values * spread_heads(step, expand)
    tailed = (values * spread_heads(tail, expand)).astype(BF16)
    scores = dot(output_map, input_map, ((1,), (1,)))
    left = lax.broadcasted_iota(jnp.int32, (Q, LANES), 1) < LANES // 2
    outs = []
    for tile in range(tiles):
        pair = stepped[:, tile * LANES : (tile + 1) * LANES]
        acc = None
        for side in range(2):
            head = 2 * tile + side
            if head >= heads:
                continue
            lane = lane0 + head
            factor = jnp.exp(running[:, lane : lane + 1] - running_t[lane : lane + 1, :] + barred)
            mixing = (scores * factor).astype(BF16)
            mine = jnp.where(left if side == 0 else ~left, pair, 0.0).astype(BF16)
            term = dot(mixing, mine)
            acc = term if acc is None else acc + term
        outs.append(acc)
    inner = jnp.concatenate(outs, 1)
    entering = dot(output_map, state[...].astype(BF16)) * carried_wide
    y_ref[...] = inner + entering + skip_ref[0:1, :] * values
    state[...] = carried_wide[Q - 1 : Q, :] * state[...] + dot(input_map, tailed, ((0,), (0,)))

    @pl.when(block == pl.num_programs(0) - 1)
    def _():
        state_ref[0:LANES, :] = state[...]
        whole = jnp.where(last_seg + first < 0, jnp.exp(total[0:1, :]), 0.0)
        state_ref[LANES:, :] = spread_heads(jnp.broadcast_to(whole, (8, LANES)), expand)


def ssd_pass(proj, rim, seg, taps, vectors, skip, expand, heads, lane0, step_col, wide):
    count = proj.shape[0]
    width = proj.shape[1]
    raw_wide = wide + 2 * LANES
    by_block = lambda w: pl.BlockSpec((Q, w), lambda i: (i, 0))
    whole = lambda a: pl.BlockSpec(a.shape, lambda i: (0,) * a.ndim)
    return pl.pallas_call(
        functools.partial(ssd_kernel, heads, lane0, step_col, wide),
        grid=(count // Q,),
        in_specs=[by_block(width), whole(rim), by_block(LANES), whole(taps), whole(vectors), whole(skip), whole(expand)],
        out_specs=[by_block(wide), by_block(LANES), by_block(LANES), pl.BlockSpec((LANES + 8, wide), lambda i: (0, 0))],
        out_shape=[
            jax.ShapeDtypeStruct((count, wide), F32),
            jax.ShapeDtypeStruct((count, LANES), F32),
            jax.ShapeDtypeStruct((count, LANES), BF16),
            jax.ShapeDtypeStruct((LANES + 8, wide), F32),
        ],
        scratch_shapes=[
            pltpu.VMEM((Q + 8, raw_wide), F32),
            pltpu.VMEM((LANES, wide), F32),
            pltpu.VMEM((8, LANES), F32),
        ],
        compiler_params=pltpu.CompilerParams(vmem_limit_bytes=48 * 1024 * 1024),
        name="ssd_pass",
    )(proj, rim, seg, taps, vectors, skip, expand)


def gate_kernel(*refs):
    parts = refs[:REACH]
    y_ref, reach_ref, map_ref, gate_ref, expand_ref, gated_ref, squares_ref, entering = refs[REACH:]

    @pl.when(pl.program_id(0) == 0)
    def _():
        sofar = parts[-1][0:LANES, :]
        for part in parts[-2::-1]:
            sofar = part[0:LANES, :] + part[LANES : LANES + 1, :] * sofar
        entering[...] = sofar.astype(BF16)

    y = y_ref[...] + dot(map_ref[...], entering[...]) * spread_heads(reach_ref[...], expand_ref[...])
    gated = y * silu(gate_ref[...].astype(F32))
    gated_ref[...] = gated
    ones = jnp.ones((8, gated.shape[1]), BF16)
    squares_ref[0] = sum(dot(ones, part, ((1,), (1,))) for part in halves(gated * gated))


def gate_pass(parts, y, reach, out_map, proj, expand):
    count, wide = y.shape
    by_block = lambda w, c=0: pl.BlockSpec((Q, w), lambda i: (i, c))
    whole = lambda a: pl.BlockSpec(a.shape, lambda i: (0,) * a.ndim)
    return pl.pallas_call(
        gate_kernel,
        grid=(count // Q,),
        in_specs=[whole(p) for p in parts] + [by_block(wide), by_block(LANES), by_block(LANES), by_block(wide, 1), whole(expand)],
        out_specs=[by_block(wide), pl.BlockSpec((1, 8, Q), lambda i: (i, 0, 0))],
        out_shape=[
            jax.ShapeDtypeStruct((count, wide), F32),
            jax.ShapeDtypeStruct((count // Q, 8, Q), F32),
        ],
        scratch_shapes=[pltpu.VMEM((LANES, wide), BF16)],
        compiler_params=pltpu.CompilerParams(vmem_limit_bytes=48 * 1024 * 1024),
        name="gate_pass",
    )(*parts, y, reach, out_map, proj, expand)


def norm_kernel(channels, parts, *refs):
    squares = refs[:parts]
    gated_ref, gain_ref, out_ref = refs[parts:]
    total = squares[0][0]
    for part in squares[1:]:
        total = total + part[0]
    scale = lax.rsqrt(total / channels + 1e-5)
    ones = jnp.ones((8, LANES), BF16)
    first = lax.broadcasted_iota(jnp.int32, (8, Q), 0) == 0
    scale = jnp.where(first, scale, 0.0)
    column = sum(dot(part, ones, ((0,), (0,))) for part in thirds(scale))
    width = out_ref.shape[1]
    for tile in range(0, width, LANES):
        w = min(LANES, width - tile)
        out_ref[:, tile : tile + w] = (
            gated_ref[:, tile : tile + w] * column[:, :w] * gain_ref[0:1, tile : tile + w]
        ).astype(BF16)


def norm_pass(squares, gated, gain, channels, width):
    count, wide = gated.shape
    whole = lambda a: pl.BlockSpec(a.shape, lambda i: (0,) * a.ndim)
    return pl.pallas_call(
        functools.partial(norm_kernel, channels, len(squares)),
        grid=(count // Q,),
        in_specs=[pl.BlockSpec((1, 8, Q), lambda i: (i, 0, 0)) for _ in squares]
        + [pl.BlockSpec((Q, wide), lambda i: (i, 0)), whole(gain)],
        out_specs=pl.BlockSpec((Q, width), lambda i: (i, 0)),
        out_shape=jax.ShapeDtypeStruct((count, width), BF16),
        compiler_params=pltpu.CompilerParams(vmem_limit_bytes=48 * 1024 * 1024),
        name="norm_pass",
    )(*squares, gated, gain)


def along_x(by):
    return [(z * SIDE + x, z * SIDE + (x + by) % SIDE) for z in range(SIDE) for x in range(SIDE)]


def along_z(by):
    return [(z * SIDE + x, (z + by) % SIDE * SIDE + x) for z in range(SIDE) for x in range(SIDE)]


def from_behind(array, by):
    length = lax.axis_size("seq")
    return lax.ppermute(array, "seq", [(i, i + by) for i in range(length - by)])


def padded(a, width):
    return jnp.pad(a, [(0, 0)] * (a.ndim - 1) + [(0, width - a.shape[-1])])


def on_device(
    hidden_rows,
    value_weight,
    gating_weight,
    state_weight,
    step_weight,
    value_kernel,
    state_kernel,
    step_bias,
    decay_log,
    skip_scale,
    norm_scale,
    document_lengths,
):
    members = lax.axis_size("tensor")
    count = hidden_rows.shape[0] * members
    inner = value_weight.shape[1]
    heads = step_weight.shape[1]
    head_width = inner // heads
    wide = -(-inner // LANES) * LANES
    lane0 = inner % LANES
    step_col = inner - lane0
    raw_wide = wide + 2 * LANES
    joined = jnp.concatenate(
        [
            padded(jnp.concatenate([value_weight, step_weight], 1), wide),
            padded(gating_weight, wide),
            state_weight,
        ],
        1,
    )
    taps = jnp.concatenate([padded(value_kernel, wide), state_kernel], 1)
    taps = jnp.pad(taps, ((0, 8 - KCONV), (0, 0)))
    at_lanes = lambda a: jnp.pad(a, (lane0, LANES - lane0 - heads))
    vectors = jnp.pad(jnp.stack([at_lanes(step_bias), at_lanes(-jnp.exp(decay_log))]), ((0, 6), (0, 0)))
    wide_rows = lambda a: jnp.broadcast_to(padded(a, wide), (8, wide))
    skip = wide_rows(jnp.repeat(skip_scale, head_width))
    gain = wide_rows(norm_scale)
    expand = (
        jnp.arange(LANES)[:, None] - lane0 == (jnp.arange(wide) // head_width)[None, :]
    ).astype(BF16)
    starts = jnp.cumsum(document_lengths) - document_lengths
    row_offset = lax.axis_index("seq") * count
    positions = row_offset + jnp.arange(count, dtype=jnp.int32)
    seg = jnp.max(jnp.where(positions[:, None] >= starts[None, :], starts[None, :], 0), axis=1) - row_offset
    seg = jnp.broadcast_to(seg[:, None], (count, LANES)).astype(jnp.int32)

    gathered = lax.all_gather(hidden_rows, "tensor", axis=0, tiled=True)
    project = lambda rows: jnp.dot(rows, joined, preferred_element_type=F32).astype(BF16)
    proj = project(gathered)
    ends = proj[count - 8 :]
    rim = from_behind(jnp.concatenate([ends[:, :wide], ends[:, 2 * wide :]], 1), 1)
    y, reach, out_map, summary = ssd_pass(
        proj, rim, seg, taps, vectors, skip, expand, heads, lane0, step_col, wide
    )
    parts = [from_behind(summary, by) for by in range(1, REACH + 1)]
    gated, squares = gate_pass(parts, y, reach, out_map, proj, expand)
    row_sum = squares + sum(lax.ppermute(squares, "tensor", along_x(by)) for by in range(1, SIDE))
    shares = [row_sum] + [lax.ppermute(row_sum, "tensor", along_z(by)) for by in range(1, SIDE)]
    return norm_pass(shares, gated, gain, inner * members, inner)


def solution(mesh):
    in_specs = (
        P(("seq", "tensor"), None),
        P(None, "tensor"),
        P(None, "tensor"),
        P(),
        P(None, "tensor"),
        P(None, "tensor"),
        P(),
        P("tensor"),
        P("tensor"),
        P("tensor"),
        P("tensor"),
        P(),
    )
    out_specs = P("seq", "tensor")
    return jax.shard_map(
        on_device, mesh=mesh, in_specs=in_specs, out_specs=out_specs, check_vma=False
    )
```

time: 582 us -> 236 us (0.41); the launches traced: 574 us -> 235 us
  local copies, waits for them, and re-layouts: 195 us -> 6.76 us
  other arithmetic: 89.8 us -> 4.04 us
  blocking collectives: 82.8 us -> 0 us
  matrix products: 79 us -> 19.8 us
  Pallas kernels: 0 us -> 43.7 us
  starting transfers between devices: 2.14 us -> 20.4 us
  waiting for transfers between devices: 109 us -> 127 us
    dynamic_update_slice x24 -> x0, local copies, waits for them, and re-layouts: 105 us -> none  [on_device(): unused, outputs = lax.scan(advance, entering, inputs)]
    psum x1 -> x0, blocking collectives: 74.5 us -> none  [on_device(): squares_total = lax.psum(row_squares, 'tensor')]
    pallas_call x0 -> x3, Pallas kernels: none -> 43.7 us  [the longest x1 23.9 us: ssd_pass(): pl.pallas_call(functools.partial(ssd_kernel, heads, lane0, step_col, wide...]
    dot_general x38 -> x1, matrix products: 62.9 us -> 19.8 us  [on_device(): jnp.dot(rows, joined, preferred_element_type=F32).astype(BF16)]
    dynamic_slice x44 -> x0, local copies, waits for them, and re-layouts: 35.1 us -> none  [the longest x36 30.7 us: on_device(): unused, outputs = lax.scan(advance, entering, inputs)]
    convert_element_type x15 -> x1, other arithmetic: 29.1 us -> 0.08 us  [on_device(): expand = (jnp.arange(LANES)[:, None] - lane0 == (jnp.arange(wide) // head...]
    another operation x28 -> x3, other arithmetic: 23.7 us -> 0.16 us
    slice x65 -> x2, local copies, waits for them, and re-layouts: 20.1 us -> 0.01 us  [the longest x1 0.01 us: on_device(): ends[:, :wide]]
  transfers between devices with their start and end apart: 3 -> 12, of which waited for: 3 -> 8; matrix products, arithmetic and copies ran while one was open for 3% -> 3% of each run, Pallas kernels for 0% -> 0%
where the time goes in v1:
time: 236 us; the launch traced here: 235 us
  waiting for transfers between devices  127 us (54%)
  Pallas kernels  43.7 us (19%)
  starting transfers between devices  20.4 us (9%)
  matrix products  19.8 us (8%)
  between operations  13.6 us (6%)
  local copies, waits for them, and re-layouts  6.76 us (3%)
  other arithmetic  4.04 us (2%)
    all_gather x1, waiting for transfers between devices, on_device(): gathered = lax.all_gather(hidden_rows, 'tensor', axis=0, tiled=True)  103 us
    pallas_call x1, Pallas kernels, ssd_pass(): pl.pallas_call(functools.partial(ssd_kernel, heads, lane0, step_col, wide...  23.9 us
    dot_general x1, matrix products, on_device(): jnp.dot(rows, joined, preferred_element_type=F32).astype(BF16)  19.8 us
    ppermute x5, waiting for transfers between devices, from_behind(): return lax.ppermute(array, 'seq', [(i, i + by) for i in range(length - by)])  14.4 us
    pallas_call x1, Pallas kernels, gate_pass(): pl.pallas_call(gate_kernel, grid=(count // Q,), in_specs=[whole(p) for p...  11.6 us
    ppermute x5, starting transfers between devices, from_behind(): return lax.ppermute(array, 'seq', [(i, i + by) for i in range(length - by)])  10.1 us
    pallas_call x1, Pallas kernels, norm_pass(): pl.pallas_call(functools.partial(norm_kernel, channels, len(squares)), gr...  8.16 us
    ppermute x3, starting transfers between devices, on_device(): lax.ppermute(squares, 'tensor', along_x(by))  5.58 us
  transfers between devices with their start and end apart: 12, of which 8 were waited for; matrix products, arithmetic and copies ran while one was open for 3% of the time, Pallas kernels for 0%

profile of v1, /device:TPU:16, one launch (start us, length us, event | category | flops | bytes accessed | tf_op | source)
XLA Modules:
  0.0 235.0 jit_solution(12205894569731638563)
XLA Ops:
  6.5 0.0 all-gather.2.cloned.1.call-start
  6.5 0.7 all-gather.2.cloned.1.call-update
  7.3 1.6 copy.21
  8.9 0.7 copy.23
  9.6 0.1 reduce
  9.8 0.7 sub.25
  10.4 0.7 exponential_negate_fusion
  11.1 0.7 pad_bitcast_fusion
  11.8 0.7 select_maximum_fusion
  12.5 0.1 select_reduce_fusion
  12.7 0.1 compare_convert_fusion.expand_ref.refs_8_
  12.8 1.6 fusion.13
  14.4 0.0 copy-start.2
  14.4 103.5 %all-gather.2.cloned.1.call-done = bf16[3072,2560]{1,0:T(8,128)(2,1)} async-done(((bf16[192,2560]{1,0:T(8,128)(2,1)}), bf16[3072,2560]{1,0:T(8,128)(2,1)}) %all-gather.2.cloned.1.call-update) | async-done | bytes 15728656 | tf_op jit(solution)/shard_map/all_gather | solution.py:304
  117.8 19.8 %convert_bitcast_fusion.proj_ref.refs_7_ = bf16[3072,1024]{1,0:T(8,128)(2,1)S(1)} fusion(bf16[3072,2560]{1,0:T(8,128)(2,1)} %all-gather.2.cloned.1.call-done, bf16[2560,320]{0,1:T(8,128)(2,1)} %param.14, bf16[2560,256]{0,1:T(8,128)(2,1)S(1)} %copy.21, bf16[2560,384]{0,1:T(8,128)(2,1)S(1)} %fusion.13), kind=kOutput, calls=%fused_computation.4 | convolution fusion | flops 16135487488 | bytes 26935296 | tf_op jit(solution)/shard_map/dot_general | solution.py:305
  137.7 0.0 copy-start
  137.7 1.9 collective-permute-start
  139.7 0.7 copy-done
  140.4 0.0 copy-done.2
  140.4 0.1 broadcast_in_dim.32
  140.4 0.1 reshape.57
  140.5 2.2 collective-permute-done.rim_ref
  142.7 0.5 broadcast_in_dim.19.seg_ref
  143.2 23.9 %ssd_pass.1 = (f32[3072,384]{1,0:T(8,128)}, f32[3072,128]{1,0:T(8,128)S(1)}, bf16[3072,128]{1,0:T(8,128)(2,1)S(1)}, f32[136,384]{1,0:T(8,128)S(1)}) custom-call(bf16[3072,1024]{1,0:T(8,128)(2,1)} %copy-done, bf16[8,640]{1,0:T(8,128)(2,1)S(1)} %collective-permute-done.rim_ref, s32[3072,128]{1,0:T(8,128)S(1)} %broadcast_in_dim.19.seg_ref, ...), custom_call_target="tpu_custom_call" | custom-call | tf_op jit(solution)/shard_map/ssd_pass/pallas_call | solution.py:148
  167.1 1.9 collective-permute-start.1
  169.1 3.1 %collective-permute-start.2 = (f32[136,384]{1,0:T(8,128)S(1)}, f32[136,384]{1,0:T(8,128)S(1)}, u32[]{:S(2)}, u32[]{:S(2)}) collective-permute-start(f32[136,384]{1,0:T(8,128)S(1)} %get-tuple-element.11), channel_id=1, source_target_pairs={{0,32},{16,48},{32,64},{48,80},{64,96},{80,112},{1,33},{17,49},{33... | collective-permute-start | bytes 626696 | tf_op jit(solution)/shard_map/ppermute | solution.py:250
  172.2 1.9 collective-permute-start.3
  174.1 1.3 collective-permute-start.4
  175.4 0.0 collective-permute-done.1.refs_0_
  175.4 3.3 %collective-permute-done.2.refs_1_ = f32[136,384]{1,0:T(8,128)S(1)} collective-permute-done((f32[136,384]{1,0:T(8,128)S(1)}, f32[136,384]{1,0:T(8,128)S(1)}, u32[]{:S(2)}, u32[]{:S(2)}) %collective-permute-start.2) | collective-permute-done | bytes 208928 | tf_op jit(solution)/shard_map/ppermute | solution.py:250
  178.7 5.2 %collective-permute-done.3.refs_2_ = f32[136,384]{1,0:T(8,128)S(1)} collective-permute-done((f32[136,384]{1,0:T(8,128)S(1)}, f32[136,384]{1,0:T(8,128)S(1)}, u32[]{:S(2)}, u32[]{:S(2)}) %collective-permute-start.3) | collective-permute-done | bytes 208928 | tf_op jit(solution)/shard_map/ppermute | solution.py:250
  183.9 3.7 %collective-permute-done.4.refs_3_ = f32[136,384]{1,0:T(8,128)S(1)} collective-permute-done((f32[136,384]{1,0:T(8,128)S(1)}, f32[136,384]{1,0:T(8,128)S(1)}, u32[]{:S(2)}, u32[]{:S(2)}) %collective-permute-start.4) | collective-permute-done | bytes 208928 | tf_op jit(solution)/shard_map/ppermute | solution.py:250
  187.6 11.6 %gate_pass.1 = (f32[3072,384]{1,0:T(8,128)}, f32[12,8,256]{2,1,0:T(8,128)S(1)}) custom-call(f32[136,384]{1,0:T(8,128)S(1)} %collective-permute-done.1.refs_0_, f32[136,384]{1,0:T(8,128)S(1)} %collective-permute-done.2.refs_1_, f32[136,384]{1,0:T(8,128)S(1)} %collective-permute-done.3.refs_2_, f32[136,384]{1,0:T(8,128)S(1)} %collective-permute-done.4.refs_3_, ...), custom_call_target="tpu_custom_call" | custom-call | tf_op jit(solution)/shard_map/gate_pass/pallas_call | solution.py:191
  199.2 1.4 collective-permute-start.5
  200.6 2.7 %collective-permute-start.6 = (f32[12,8,256]{2,1,0:T(8,128)S(1)}, f32[12,8,256]{2,1,0:T(8,128)S(1)}, u32[]{:S(2)}, u32[]{:S(2)}) collective-permute-start(f32[12,8,256]{2,1,0:T(8,128)S(1)} %get-tuple-element.15), channel_id=1, source_target_pairs={{0,2},{1,3},{2,0},{3,1},{4,6},{5,7},{6,4},{7,5},{8,10},{9,11},{10,... | collective-permute-start | bytes 294920 | tf_op jit(solution)/shard_map/ppermute | solution.py:314
  203.3 1.5 collective-permute-start.7
  204.7 0.5 collective-permute-done.5
  205.3 3.0 %collective-permute-done.6 = f32[12,8,256]{2,1,0:T(8,128)S(1)} collective-permute-done((f32[12,8,256]{2,1,0:T(8,128)S(1)}, f32[12,8,256]{2,1,0:T(8,128)S(1)}, u32[]{:S(2)}, u32[]{:S(2)}) %collective-permute-start.6) | collective-permute-done | bytes 98336 | tf_op jit(solution)/shard_map/ppermute | solution.py:314
  208.3 0.0 collective-permute-done.7
  208.3 2.5 %collective-permute-start.10 = (f32[12,8,256]{2,1,0:T(8,128)S(1)}, f32[12,8,256]{2,1,0:T(8,128)S(1)}, u32[]{:S(2)}, u32[]{:S(2)}) collective-permute-start(f32[12,8,256]{2,1,0:T(8,128)S(1)} %add_add_fusion.refs_0_), channel_id=1, source_target_pairs={{0,12},{1,13},{2,14},{3,15},{4,0},{5,1},{6,2},{7,3},{8,4},{9,5},{1... | collective-permute-start | bytes 294920 | tf_op jit(solution)/shard_map/ppermute | solution.py:315
  210.8 0.0 collective-permute-start.8
  210.8 2.2 collective-permute-start.9
  213.0 0.0 copy-done.1
  213.0 0.0 collective-permute-done.10.refs_3_
  213.0 4.6 %collective-permute-done.8.refs_1_ = f32[12,8,256]{2,1,0:T(8,128)S(1)} collective-permute-done((f32[12,8,256]{2,1,0:T(8,128)S(1)}, f32[12,8,256]{2,1,0:T(8,128)S(1)}, u32[]{:S(2)}, u32[]{:S(2)}) %collective-permute-start.8) | collective-permute-done | bytes 98336 | tf_op jit(solution)/shard_map/ppermute | solution.py:315
  217.6 0.0 collective-permute-done.9.refs_2_
  217.7 8.2 %norm_pass.1 = bf16[3072,320]{1,0:T(8,128)(2,1)S(1)} custom-call(f32[12,8,256]{2,1,0:T(8,128)S(1)} %add_add_fusion.refs_0_, f32[12,8,256]{2,1,0:T(8,128)S(1)} %collective-permute-done.8.refs_1_, f32[12,8,256]{2,1,0:T(8,128)S(1)} %collective-permute-done.9.refs_2_, f32[12,8,256]{2,1,0:T(8,128)S(1)} %collective-permute-done.10.refs_3_, ...), custom_call_target="tpu_custom_call" | custom-call | tf_op jit(solution)/shard_map/norm_pass/pallas_call | solution.py:228
  225.8 2.4 %copy.24 = bf16[3072,320]{0,1:T(8,128)(2,1)} copy(bf16[3072,320]{1,0:T(8,128)(2,1)S(1)} %norm_pass.1) | data formatting | bytes 3932160 | tf_op jit(solution)/shard_map/norm_pass/pallas_call | solution.py:228
  (16 shorter events, 0.1 us)
Async XLA Ops:
  6.5 111.3 %all-gather.2.cloned.1.call-start = ((), (), s32[]{:S(2)}) async-start(), calls=%async_computation | async-start | bytes 16711680 | tf_op jit(solution)/shard_map/all_gather | solution.py:304
  14.4 126.0 %copy-start.2 = (f32[5]{0:T(128)S(1)}, f32[5]{0:T(128)}, u32[]{:S(2)}) copy-start(f32[5]{0:T(128)} %param.21) | copy-start | bytes 64
  137.7 2.7 %copy-start = (bf16[3072,1024]{1,0:T(8,128)(2,1)}, bf16[3072,1024]{1,0:T(8,128)(2,1)S(1)}, u32[]{:S(2)}) copy-start(bf16[3072,1024]{1,0:T(8,128)(2,1)S(1)} %convert_bitcast_fusion.proj_ref.refs_7_) | copy-start | bytes 18874372
  137.7 5.0 %collective-permute-start = (bf16[8,640]{1,0:T(8,128)(2,1)S(1)}, bf16[8,640]{1,0:T(8,128)(2,1)S(1)}, u32[]{:S(2)}, u32[]{:S(2)}) collective-permute-start(bf16[8,640]{1,0:T(8,128)(2,1)S(1)} %pad_maximum_fusion), channel_id=1, source_target_pairs={{0,16},{16,32},{32,48},{48,64},{64,80},{80,96},{96,112},{1,17},{17... | collective-permute-start | bytes 30728 | tf_op jit(solution)/shard_map/ppermute | solution.py:250
  167.1 8.3 %collective-permute-start.1 = (f32[136,384]{1,0:T(8,128)S(1)}, f32[136,384]{1,0:T(8,128)S(1)}, u32[]{:S(2)}, u32[]{:S(2)}) collective-permute-start(f32[136,384]{1,0:T(8,128)S(1)} %get-tuple-element.11), channel_id=1, source_target_pairs={{0,16},{16,32},{32,48},{48,64},{64,80},{80,96},{96,112},{1,17},{17... | collective-permute-start | bytes 626696 | tf_op jit(solution)/shard_map/ppermute | solution.py:250
  169.1 9.6 %collective-permute-start.2 = (f32[136,384]{1,0:T(8,128)S(1)}, f32[136,384]{1,0:T(8,128)S(1)}, u32[]{:S(2)}, u32[]{:S(2)}) collective-permute-start(f32[136,384]{1,0:T(8,128)S(1)} %get-tuple-element.11), channel_id=1, source_target_pairs={{0,32},{16,48},{32,64},{48,80},{64,96},{80,112},{1,33},{17,49},{33... | collective-permute-start | bytes 626696 | tf_op jit(solution)/shard_map/ppermute | solution.py:250
  172.2 11.7 %collective-permute-start.3 = (f32[136,384]{1,0:T(8,128)S(1)}, f32[136,384]{1,0:T(8,128)S(1)}, u32[]{:S(2)}, u32[]{:S(2)}) collective-permute-start(f32[136,384]{1,0:T(8,128)S(1)} %get-tuple-element.11), channel_id=1, source_target_pairs={{0,48},{16,64},{32,80},{48,96},{64,112},{1,49},{17,65},{33,81},{49... | collective-permute-start | bytes 626696 | tf_op jit(solution)/shard_map/ppermute | solution.py:250
  174.1 13.5 %collective-permute-start.4 = (f32[136,384]{1,0:T(8,128)S(1)}, f32[136,384]{1,0:T(8,128)S(1)}, u32[]{:S(2)}, u32[]{:S(2)}) collective-permute-start(f32[136,384]{1,0:T(8,128)S(1)} %get-tuple-element.11), channel_id=1, source_target_pairs={{0,64},{16,80},{32,96},{48,112},{1,65},{17,81},{33,97},{49,113},{2... | collective-permute-start | bytes 626696 | tf_op jit(solution)/shard_map/ppermute | solution.py:250
  187.6 25.4 %copy-start.1 = (f32[320]{0:T(512)S(1)}, f32[320]{0:T(512)}, u32[]{:S(2)}) copy-start(f32[320]{0:T(512)} %param.22) | copy-start | bytes 3844
  199.2 6.1 %collective-permute-start.5 = (f32[12,8,256]{2,1,0:T(8,128)S(1)}, f32[12,8,256]{2,1,0:T(8,128)S(1)}, u32[]{:S(2)}, u32[]{:S(2)}) collective-permute-start(f32[12,8,256]{2,1,0:T(8,128)S(1)} %get-tuple-element.15), channel_id=1, source_target_pairs={{0,1},{1,2},{2,3},{3,0},{4,5},{5,6},{6,7},{7,4},{8,9},{9,10},{10,1... | collective-permute-start | bytes 294920 | tf_op jit(solution)/shard_map/ppermute | solution.py:314
  200.6 7.7 %collective-permute-start.6 = (f32[12,8,256]{2,1,0:T(8,128)S(1)}, f32[12,8,256]{2,1,0:T(8,128)S(1)}, u32[]{:S(2)}, u32[]{:S(2)}) collective-permute-start(f32[12,8,256]{2,1,0:T(8,128)S(1)} %get-tuple-element.15), channel_id=1, source_target_pairs={{0,2},{1,3},{2,0},{3,1},{4,6},{5,7},{6,4},{7,5},{8,10},{9,11},{10,... | collective-permute-start | bytes 294920 | tf_op jit(solution)/shard_map/ppermute | solution.py:314
  203.3 5.0 %collective-permute-start.7 = (f32[12,8,256]{2,1,0:T(8,128)S(1)}, f32[12,8,256]{2,1,0:T(8,128)S(1)}, u32[]{:S(2)}, u32[]{:S(2)}) collective-permute-start(f32[12,8,256]{2,1,0:T(8,128)S(1)} %get-tuple-element.15), channel_id=1, source_target_pairs={{0,3},{1,0},{2,1},{3,2},{4,7},{5,4},{6,5},{7,6},{8,11},{9,8},{10,9... | collective-permute-start | bytes 294920 | tf_op jit(solution)/shard_map/ppermute | solution.py:314
  208.3 4.7 %collective-permute-start.10 = (f32[12,8,256]{2,1,0:T(8,128)S(1)}, f32[12,8,256]{2,1,0:T(8,128)S(1)}, u32[]{:S(2)}, u32[]{:S(2)}) collective-permute-start(f32[12,8,256]{2,1,0:T(8,128)S(1)} %add_add_fusion.refs_0_), channel_id=1, source_target_pairs={{0,12},{1,13},{2,14},{3,15},{4,0},{5,1},{6,2},{7,3},{8,4},{9,5},{1... | collective-permute-start | bytes 294920 | tf_op jit(solution)/shard_map/ppermute | solution.py:315
  210.8 6.9 %collective-permute-start.8 = (f32[12,8,256]{2,1,0:T(8,128)S(1)}, f32[12,8,256]{2,1,0:T(8,128)S(1)}, u32[]{:S(2)}, u32[]{:S(2)}) collective-permute-start(f32[12,8,256]{2,1,0:T(8,128)S(1)} %add_add_fusion.refs_0_), channel_id=1, source_target_pairs={{0,4},{1,5},{2,6},{3,7},{4,8},{5,9},{6,10},{7,11},{8,12},{9,13},{1... | collective-permute-start | bytes 294920 | tf_op jit(solution)/shard_map/ppermute | solution.py:315
  210.8 6.9 %collective-permute-start.9 = (f32[12,8,256]{2,1,0:T(8,128)S(1)}, f32[12,8,256]{2,1,0:T(8,128)S(1)}, u32[]{:S(2)}, u32[]{:S(2)}) collective-permute-start(f32[12,8,256]{2,1,0:T(8,128)S(1)} %add_add_fusion.refs_0_), channel_id=1, source_target_pairs={{0,8},{1,9},{2,10},{3,11},{4,12},{5,13},{6,14},{7,15},{8,0},{9,1},... | collective-permute-start | bytes 294920 | tf_op jit(solution)/shard_map/ppermute | solution.py:315
Sparse Core Ops, SparseCore 0:
  9.5 108.2 all-gather.1

commit v2 on v1

v2 whole, which is shorter than its diff:
```python
import functools

import jax
import jax.numpy as jnp
from jax import lax
from jax.experimental import pallas as pl
from jax.experimental.pallas import tpu as pltpu
from jax.sharding import PartitionSpec as P

KCONV = 4
Q = 256
LANES = 128
SIDE = 4
REACH = 4
F32 = jnp.float32
BF16 = jnp.bfloat16


def dot(a, b, contract=((1,), (0,))):
    return lax.dot_general(a, b, (contract, ((), ())), preferred_element_type=F32)


def thirds(a):
    high = a.astype(BF16)
    rest = a - high.astype(F32)
    middle = rest.astype(BF16)
    return high, middle, (rest - middle.astype(F32)).astype(BF16)


def silu(v):
    half = 0.5 * v
    return half + half * jnp.tanh(half)


def ssd_kernel(
    heads,
    value_ref,
    in_ref,
    out_ref,
    step_ref,
    rim_ref,
    seg_ref,
    taps_ref,
    vectors_ref,
    skip_ref,
    y_ref,
    reach_ref,
    map_ref,
    state_ref,
    before,
    state,
    total,
):
    block = pl.program_id(0)
    inner = value_ref.shape[0]
    head_width = inner // heads

    @pl.when(block == 0)
    def _():
        before[...] = rim_ref[...].astype(F32)
        state[...] = jnp.zeros_like(state)
        total[...] = jnp.zeros_like(total)

    first = block * Q
    seg = seg_ref[...] - first
    place = lax.broadcasted_iota(jnp.int32, (1, Q), 1)
    keep = [jnp.broadcast_to(jnp.where(place - k >= seg, 1.0, 0.0), (8, Q)) for k in range(1, KCONV)]

    def convolved(ref, at, base):
        raw = ref[at : at + 8, :]
        rows = slice(base + at, base + at + 8)
        ext = jnp.concatenate([before[rows, :], raw], 1)
        taps = [jnp.concatenate([taps_ref[k, rows, :]] * (Q // LANES), 1) for k in range(KCONV)]
        sums = taps[0] * raw
        for k in range(1, KCONV):
            sums = sums + taps[k] * keep[k - 1] * pltpu.roll(ext, k, 1)[:, LANES:]
        before[rows, :] = raw[:, Q - LANES :]
        return silu(sums)

    def conv_all(ref, base):
        count = ref.shape[0]
        wide = ref[...].astype(F32)
        return jnp.concatenate([convolved(wide, at, base) for at in range(0, count, 8)], 0).astype(BF16)

    values = conv_all(value_ref, 0).astype(F32)
    input_map = conv_all(in_ref, inner)
    output_map = conv_all(out_ref, inner + LANES)
    map_ref[...] = output_map

    v = step_ref[...].astype(F32)[0:8, :] + vectors_ref[0, :, 0:1]
    step = jnp.maximum(v, 0.0) + jnp.log(1.0 + jnp.exp(-jnp.abs(v)))
    decay = vectors_ref[1, :, 0:1] * step
    jj = lax.broadcasted_iota(jnp.int32, (Q, Q), 0)
    ii = lax.broadcasted_iota(jnp.int32, (Q, Q), 1)
    causal = jj <= ii
    upper = jnp.where(causal, 1.0, 0.0).astype(BF16)
    running = sum(dot(part, upper) for part in thirds(decay))
    running_t = running.T
    barred = jnp.where(causal & (jj >= seg), 0.0, -1e30)
    last = running[:, Q - 1 : Q]
    last_seg = seg[:, Q - 1 : Q]
    carried = jnp.where(seg < 0, jnp.exp(running), 0.0)
    tail = jnp.where(place >= last_seg, jnp.exp(last - running), 0.0) * step
    reach_ref[...] = jnp.where(seg + first < 0, jnp.exp(total[:, 0:1] + running), 0.0)
    total[...] = total[...] + last
    scores = dot(input_map, output_map, ((0,), (0,)))
    entering = dot(state[...].astype(BF16), output_map)
    for head in range(heads):
        at = slice(head * head_width, (head + 1) * head_width)
        mine = values[at, :]
        factor = jnp.exp(running[head : head + 1, :] - running_t[:, head : head + 1] + barred)
        mixing = (scores * factor).astype(BF16)
        within = dot((mine * step[head : head + 1, :]).astype(BF16), mixing)
        skipped = jnp.concatenate([skip_ref[at, :]] * (Q // LANES), 1) * mine
        y_ref[at, :] = within + entering[at, :] * carried[head : head + 1, :] + skipped
        tailed = (mine * tail[head : head + 1, :]).astype(BF16)
        state[at, :] = carried[head : head + 1, Q - 1 : Q] * state[at, :] + dot(tailed, input_map, ((1,), (1,)))

    @pl.when(block == pl.num_programs(0) - 1)
    def _():
        state_ref[0:inner, :] = state[...]
        whole = jnp.where(last_seg + first < 0, jnp.exp(total[:, 0:1]), 0.0)
        state_ref[inner:, :] = jnp.broadcast_to(whole, (8, LANES))


def limits():
    return pltpu.CompilerParams(vmem_limit_bytes=48 * 1024 * 1024)


def whole(a):
    return pl.BlockSpec(a.shape, lambda i: (0,) * a.ndim)


def some(rows, columns, at=0):
    return pl.BlockSpec((rows, columns), lambda i: (at, i))


def ssd_pass(proj, rim, seg, taps, vectors, skip, heads, inner):
    count = proj.shape[1]
    maps = 2 * inner // LANES
    steps = 2 * inner + 2 * LANES
    return pl.pallas_call(
        functools.partial(ssd_kernel, heads),
        grid=(count // Q,),
        in_specs=[
            some(inner, Q),
            some(LANES, Q, maps),
            some(LANES, Q, maps + 1),
            some(16, Q, steps // 16),
            whole(rim),
            some(1, Q),
            whole(taps),
            whole(vectors),
            whole(skip),
        ],
        out_specs=[
            some(inner, Q),
            some(8, Q),
            some(LANES, Q),
            pl.BlockSpec((inner + 8, LANES), lambda i: (0, 0)),
        ],
        out_shape=[
            jax.ShapeDtypeStruct((inner, count), F32),
            jax.ShapeDtypeStruct((8, count), F32),
            jax.ShapeDtypeStruct((LANES, count), BF16),
            jax.ShapeDtypeStruct((inner + 8, LANES), F32),
        ],
        scratch_shapes=[
            pltpu.VMEM((inner + 2 * LANES, LANES), F32),
            pltpu.VMEM((inner, LANES), F32),
            pltpu.VMEM((8, LANES), F32),
        ],
        compiler_params=limits(),
        name="ssd_pass",
    )(proj, proj, proj, proj, rim, seg, taps, vectors, skip)


def gate_kernel(heads, *refs):
    parts = refs[:REACH]
    y_ref, reach_ref, map_ref, gate_ref, gated_ref, squares_ref, entering = refs[REACH:]
    inner = y_ref.shape[0]
    head_width = inner // heads

    @pl.when(pl.program_id(0) == 0)
    def _():
        for head in range(heads):
            at = slice(head * head_width, (head + 1) * head_width)
            sofar = parts[-1][at, :]
            for part in parts[-2::-1]:
                sofar = part[at, :] + part[inner + head : inner + head + 1, :] * sofar
            entering[at, :] = sofar.astype(BF16)

    carried = dot(entering[...], map_ref[...])
    squares = jnp.zeros((8, y_ref.shape[1]), F32)
    for head in range(heads):
        at = slice(head * head_width, (head + 1) * head_width)
        y = y_ref[at, :] + carried[at, :] * reach_ref[head : head + 1, :]
        gated = y * silu(gate_ref[at, :].astype(F32))
        gated_ref[at, :] = gated
        square = gated * gated
        squares = squares + sum(square[i : i + 8, :] for i in range(0, head_width, 8))
    squares_ref[...] = jnp.sum(squares, axis=0, keepdims=True)


def gate_pass(parts, y, reach, out_map, proj, heads):
    inner, count = y.shape
    step = 3 * Q
    return pl.pallas_call(
        functools.partial(gate_kernel, heads),
        grid=(count // step,),
        in_specs=[whole(p) for p in parts] + [some(inner, step), some(8, step), some(LANES, step), some(inner, step, 1)],
        out_specs=[some(inner, step), some(1, step)],
        out_shape=[
            jax.ShapeDtypeStruct((inner, count), F32),
            jax.ShapeDtypeStruct((1, count), F32),
        ],
        scratch_shapes=[pltpu.VMEM((inner, LANES), BF16)],
        compiler_params=limits(),
        name="gate_pass",
    )(*parts, y, reach, out_map, proj)


def norm_kernel(channels, parts, *refs):
    squares = refs[:parts]
    gated_ref, gain_ref, out_ref = refs[parts:]
    total = squares[0][...]
    for part in squares[1:]:
        total = total + part[...]
    scale = lax.rsqrt(total / channels + 1e-5)
    step = out_ref.shape[1]
    for at in range(0, out_ref.shape[0], 16):
        rows = slice(at, at + 16)
        gain = jnp.concatenate([gain_ref[rows, :]] * (step // LANES), 1)
        out_ref[rows, :] = (gated_ref[rows, :] * scale * gain).astype(BF16)


def norm_pass(squares, gated, gain, channels):
    inner, count = gated.shape
    step = 3 * Q
    return pl.pallas_call(
        functools.partial(norm_kernel, channels, len(squares)),
        grid=(count // step,),
        in_specs=[some(1, step) for _ in squares] + [some(inner, step), whole(gain)],
        out_specs=some(inner, step),
        out_shape=jax.ShapeDtypeStruct((inner, count), BF16),
        compiler_params=limits(),
        name="norm_pass",
    )(*squares, gated, gain)


def along_x(by):
    return [(z * SIDE + x, z * SIDE + (x + by) % SIDE) for z in range(SIDE) for x in range(SIDE)]


def along_z(by):
    return [(z * SIDE + x, (z + by) % SIDE * SIDE + x) for z in range(SIDE) for x in range(SIDE)]


def from_behind(array, by):
    length = lax.axis_size("seq")
    return lax.ppermute(array, "seq", [(i, i + by) for i in range(length - by)])


def on_device(
    hidden_rows,
    value_weight,
    gating_weight,
    state_weight,
    step_weight,
    value_kernel,
    state_kernel,
    step_bias,
    decay_log,
    skip_scale,
    norm_scale,
    document_lengths,
):
    members = lax.axis_size("tensor")
    count = hidden_rows.shape[0] * members
    inner = value_weight.shape[1]
    heads = step_weight.shape[1]
    head_width = inner // heads
    lanes = lambda a: jnp.broadcast_to(a[..., None], a.shape + (LANES,))
    joined = jnp.concatenate(
        [
            value_weight.T,
            gating_weight.T,
            state_weight.T,
            jnp.pad(step_weight.T, ((0, 16 - heads), (0, 0))),
        ],
        0,
    )
    taps = lanes(jnp.concatenate([value_kernel, state_kernel], 1))
    vectors = lanes(jnp.pad(jnp.stack([step_bias, -jnp.exp(decay_log)]), ((0, 0), (0, 8 - heads))))
    skip = lanes(jnp.repeat(skip_scale, head_width))
    gain = lanes(norm_scale)
    starts = jnp.cumsum(document_lengths) - document_lengths
    row_offset = lax.axis_index("seq") * count
    positions = row_offset + jnp.arange(count, dtype=jnp.int32)
    seg = jnp.max(jnp.where(positions[None, :] >= starts[:, None], starts[:, None], 0), axis=0) - row_offset
    seg = seg[None, :].astype(jnp.int32)

    gathered = lax.all_gather(hidden_rows, "tensor", axis=0, tiled=True)
    proj = dot(joined, gathered, ((1,), (1,))).astype(BF16)
    ends = proj[:, count - LANES :]
    rim = from_behind(jnp.concatenate([ends[:inner], ends[2 * inner : 2 * inner + 2 * LANES]], 0), 1)
    y, reach, out_map, summary = ssd_pass(proj, rim, seg, taps, vectors, skip, heads, inner)
    parts = [from_behind(summary, by) for by in range(1, REACH + 1)]
    gated, squares = gate_pass(parts, y, reach, out_map, proj, heads)
    row_sum = squares + sum(lax.ppermute(squares, "tensor", along_x(by)) for by in range(1, SIDE))
    shares = [row_sum] + [lax.ppermute(row_sum, "tensor", along_z(by)) for by in range(1, SIDE)]
    return norm_pass(shares, gated, gain, inner * members).T


def solution(mesh):
    in_specs = (
        P(("seq", "tensor"), None),
        P(None, "tensor"),
        P(None, "tensor"),
        P(),
        P(None, "tensor"),
        P(None, "tensor"),
        P(),
        P("tensor"),
        P("tensor"),
        P("tensor"),
        P("tensor"),
        P(),
    )
    out_specs = P("seq", "tensor")
    return jax.shard_map(
        on_device, mesh=mesh, in_specs=in_specs, out_specs=out_specs, check_vma=False
    )
```

time: 236 us -> 214 us (0.907)
  Pallas kernels: 43.7 us -> 25.1 us
    pallas_call x2, Pallas kernels: 35.5 us -> 22.9 us  [the longest x1 18.5 us: ssd_pass(): pl.pallas_call(functools.partial(ssd_kernel, heads), grid=(count // Q,),...]
    pallas_call x1, Pallas kernels: 8.16 us -> 2.14 us  [norm_pass(): pl.pallas_call(functools.partial(norm_kernel, channels, len(squares)), gr...]
    all_gather x1, waiting for transfers between devices: 103 us -> 107 us  [on_device(): gathered = lax.all_gather(hidden_rows, 'tensor', axis=0, tiled=True)]
    pallas_call x1 -> x0, local copies, waits for them, and re-layouts: 2.37 us -> none  [norm_pass(): pl.pallas_call(functools.partial(norm_kernel, channels, len(squares)), gr...]
  transfers between devices with their start and end apart: 12 -> 12, of which waited for: 8 -> 10; matrix products, arithmetic and copies ran while one was open for 3% -> 2% of each run, Pallas kernels for 0% -> 0%
where the time goes in v2:
time: 214 us; the launch traced here: 213 us
  waiting for transfers between devices  128 us (60%)
  Pallas kernels  25.1 us (12%)
  matrix products  20.7 us (10%)
  starting transfers between devices  19.4 us (9%)
  between operations  13.5 us (6%)
  local copies, waits for them, and re-layouts  4.86 us (2%)
    all_gather x1, waiting for transfers between devices, on_device(): gathered = lax.all_gather(hidden_rows, 'tensor', axis=0, tiled=True)  107 us
    dot_general x1, matrix products, dot(): lax.dot_general(a, b, (contract, ((), ())), preferred_element_type=F32)  20.7 us
    pallas_call x1, Pallas kernels, ssd_pass(): pl.pallas_call(functools.partial(ssd_kernel, heads), grid=(count // Q,),...  18.5 us
    ppermute x5, waiting for transfers between devices, from_behind(): return lax.ppermute(array, 'seq', [(i, i + by) for i in range(length - by)])  14.5 us
    ppermute x5, starting transfers between devices, from_behind(): return lax.ppermute(array, 'seq', [(i, i + by) for i in range(length - by)])  10.1 us
    ppermute x3, starting transfers between devices, on_device(): lax.ppermute(squares, 'tensor', along_x(by))  5.64 us
    pallas_call x1, Pallas kernels, gate_pass(): pl.pallas_call(functools.partial(gate_kernel, heads), grid=(count // step...  4.43 us
  transfers between devices with their start and end apart: 12, of which 10 were waited for; matrix products, arithmetic and copies ran while one was open for 2% of the time, Pallas kernels for 0%

profile of v2, /device:TPU:16, one launch (start us, length us, event | category | flops | bytes accessed | tf_op | source)
XLA Modules:
  0.0 213.1 jit_solution(6128103839053598459)
XLA Ops:
  6.5 0.0 all-gather.2.cloned.1.call-start
  6.5 0.7 all-gather.2.cloned.1.call-update
  7.3 1.6 copy.17
  8.9 0.7 copy.18
  9.6 0.1 reduce
  9.8 0.7 sub.17
  10.4 0.1 select_reduce_fusion
  10.6 0.7 negate_bitcast_fusion
  11.2 106.6 %all-gather.2.cloned.1.call-done = bf16[3072,2560]{1,0:T(8,128)(2,1)} async-done(((bf16[192,2560]{1,0:T(8,128)(2,1)}), bf16[3072,2560]{1,0:T(8,128)(2,1)}) %all-gather.2.cloned.1.call-update) | async-done | bytes 15728656 | tf_op jit(solution)/shard_map/all_gather | solution.py:303
  117.9 20.7 %convolution_convert_fusion.value_ref.in_ref.out_ref.step_ref.refs_7_ = bf16[912,3072]{1,0:T(8,128)(2,1)} fusion(bf16[3072,2560]{1,0:T(8,128)(2,1)} %all-gather.2.cloned.1.call-done, bf16[5,2560]{1,0:T(8,128)(2,1)} %bitcast.17, bf16[256,2560]{1,0:T(8,128)(2,1)S(1)} %copy.17, bf16[320,2560]{1,0:T(8,128)(2,1)} %bitcast.15, bf16[320,2560]{1,0:T(8,128)(2,1)} %bitcast.16), kind=kOutput, calls=%fused_computation.2 | convolution fusion | flops 14370668544 | bytes 25945088 | tf_op jit(solution)/shard_map/dot_general | solution.py:20
  138.6 0.9 slice.11
  139.5 0.8 slice.12
  140.3 1.9 collective-permute-start
  142.2 0.0 copy-done.4
  142.3 0.0 copy-done.3
  142.3 0.1 broadcast_in_dim.21
  142.4 0.1 broadcast_in_dim.22
  142.4 0.0 copy-done
  142.4 0.0 copy-done.1
  142.4 0.1 pad_maximum_fusion.1
  142.5 4.3 %collective-permute-done.rim_ref = bf16[576,128]{1,0:T(8,128)(2,1)S(1)} collective-permute-done((bf16[576,128]{1,0:T(8,128)(2,1)S(1)}, bf16[576,128]{1,0:T(8,128)(2,1)S(1)}, u32[]{:S(2)}, u32[]{:S(2)}) %collective-permute-start) | collective-permute-done | bytes 147488 | tf_op jit(solution)/shard_map/ppermute | solution.py:261
  146.8 0.4 broadcast_in_dim.19.taps_ref
  147.1 0.1 broadcast_in_dim.27.skip_ref
  147.3 0.1 broadcast_in_dim.20.vectors_ref
  147.3 18.5 %ssd_pass.1 = (f32[320,3072]{1,0:T(8,128)}, f32[8,3072]{1,0:T(8,128)S(1)}, bf16[128,3072]{1,0:T(8,128)(2,1)S(1)}, f32[328,128]{1,0:T(8,128)S(1)}) custom-call(bf16[912,3072]{1,0:T(8,128)(2,1)} %convolution_convert_fusion.value_ref.in_ref.out_ref.step_ref.refs_7_, bf16[912,3072]{1,0:T(8,128)(2,1)} %convolution_convert_fusion.value_ref.in_ref.out_ref.step_ref.refs_7_, ...), custom_call_target="tpu_custom_call" | custom-call | tf_op jit(solution)/shard_map/ssd_pass/pallas_call | solution.py:142
  165.8 1.9 collective-permute-start.1
  167.7 3.1 %collective-permute-start.2 = (f32[328,128]{1,0:T(8,128)S(1)}, f32[328,128]{1,0:T(8,128)S(1)}, u32[]{:S(2)}, u32[]{:S(2)}) collective-permute-start(f32[328,128]{1,0:T(8,128)S(1)} %get-tuple-element.11), channel_id=1, source_target_pairs={{0,32},{16,48},{32,64},{48,80},{64,96},{80,112},{1,33},{17,49},{33... | collective-permute-start | bytes 503816 | tf_op jit(solution)/shard_map/ppermute | solution.py:261
  170.9 1.9 collective-permute-start.3
  172.8 1.3 collective-permute-start.4
  174.1 0.0 collective-permute-done.1.refs_0_
  174.1 2.4 %collective-permute-done.2.refs_1_ = f32[328,128]{1,0:T(8,128)S(1)} collective-permute-done((f32[328,128]{1,0:T(8,128)S(1)}, f32[328,128]{1,0:T(8,128)S(1)}, u32[]{:S(2)}, u32[]{:S(2)}) %collective-permute-start.2) | collective-permute-done | bytes 167968 | tf_op jit(solution)/shard_map/ppermute | solution.py:261
  176.5 4.4 %collective-permute-done.3.refs_2_ = f32[328,128]{1,0:T(8,128)S(1)} collective-permute-done((f32[328,128]{1,0:T(8,128)S(1)}, f32[328,128]{1,0:T(8,128)S(1)}, u32[]{:S(2)}, u32[]{:S(2)}) %collective-permute-start.3) | collective-permute-done | bytes 167968 | tf_op jit(solution)/shard_map/ppermute | solution.py:261
  180.8 3.5 %collective-permute-done.4.refs_3_ = f32[328,128]{1,0:T(8,128)S(1)} collective-permute-done((f32[328,128]{1,0:T(8,128)S(1)}, f32[328,128]{1,0:T(8,128)S(1)}, u32[]{:S(2)}, u32[]{:S(2)}) %collective-permute-start.4) | collective-permute-done | bytes 167968 | tf_op jit(solution)/shard_map/ppermute | solution.py:261
  184.4 4.4 %gate_pass.1 = (f32[320,3072]{1,0:T(8,128)S(1)}, f32[1,3072]{1,0:T(1,128)S(1)}) custom-call(f32[328,128]{1,0:T(8,128)S(1)} %collective-permute-done.1.refs_0_, f32[328,128]{1,0:T(8,128)S(1)} %collective-permute-done.2.refs_1_, f32[328,128]{1,0:T(8,128)S(1)} %collective-permute-done.3.refs_2_, f32[328,128]{1,0:T(8,128)S(1)} %collective-permute-done.4.refs_3_, ...), custom_call_target="tpu_custom_call" | custom-call | tf_op jit(solution)/shard_map/gate_pass/pallas_call | solution.py:208
  188.8 1.5 collective-permute-start.5
  190.3 2.7 %collective-permute-start.6 = (f32[1,3072]{1,0:T(1,128)S(1)}, f32[1,3072]{1,0:T(1,128)S(1)}, u32[]{:S(2)}, u32[]{:S(2)}) collective-permute-start(f32[1,3072]{1,0:T(1,128)S(1)} %get-tuple-element.15), channel_id=1, source_target_pairs={{0,2},{1,3},{2,0},{3,1},{4,6},{5,7},{6,4},{7,5},{8,10},{9,11},{10,... | collective-permute-start | bytes 36872 | tf_op jit(solution)/shard_map/ppermute | solution.py:310
  193.0 1.5 collective-permute-start.7
  194.4 0.0 collective-permute-done.5
  194.4 1.1 collective-permute-done.6
  195.5 1.2 collective-permute-done.7
  196.7 1.0 collective-permute-start.10
  197.7 1.1 collective-permute-start.8
  198.8 1.5 collective-permute-start.9
  200.3 0.2 collective-permute-done.10.refs_3_
  200.5 2.1 collective-permute-done.8.refs_1_
  202.6 1.4 collective-permute-done.9.refs_2_
  204.0 0.1 broadcast_in_dim.48.refs_5_
  204.1 2.1 %norm_pass.1 = bf16[320,3072]{1,0:T(8,128)(2,1)} custom-call(f32[1,3072]{1,0:T(1,128)S(1)} %add_add_fusion.refs_0_, f32[1,3072]{1,0:T(1,128)S(1)} %collective-permute-done.8.refs_1_, f32[1,3072]{1,0:T(1,128)S(1)} %collective-permute-done.9.refs_2_, f32[1,3072]{1,0:T(1,128)S(1)} %collective-permute-done.10.refs_3_, ...), custom_call_target="tpu_custom_call" | custom-call | tf_op jit(solution)/shard_map/norm_pass/pallas_call | solution.py:240
  (12 shorter events, 0.1 us)
Async XLA Ops:
  6.5 111.3 %all-gather.2.cloned.1.call-start = ((), (), s32[]{:S(2)}) async-start(), calls=%async_computation | async-start | bytes 16711680 | tf_op jit(solution)/shard_map/all_gather | solution.py:303
  117.8 24.4 %copy-start.4 = (f32[5]{0:T(128)S(1)}, f32[5]{0:T(128)}, u32[]{:S(2)}) copy-start(f32[5]{0:T(128)} %param.19) | copy-start | bytes 64
  117.8 24.4 %copy-start.3 = (f32[5]{0:T(128)S(1)}, f32[5]{0:T(128)}, u32[]{:S(2)}) copy-start(f32[5]{0:T(128)} %param.21) | copy-start | bytes 64
  117.8 24.6 %copy-start = (f32[4,320]{1,0:T(4,128)S(1)}, f32[4,320]{1,0:T(4,128)}, u32[]{:S(2)}) copy-start(f32[4,320]{1,0:T(4,128)} %param.17) | copy-start | bytes 15364
  117.8 24.6 %copy-start.1 = (f32[4,256]{1,0:T(4,128)S(1)}, f32[4,256]{1,0:T(4,128)}, u32[]{:S(2)}) copy-start(f32[4,256]{1,0:T(4,128)} %param.18) | copy-start | bytes 12292
  140.3 6.5 %collective-permute-start = (bf16[576,128]{1,0:T(8,128)(2,1)S(1)}, bf16[576,128]{1,0:T(8,128)(2,1)S(1)}, u32[]{:S(2)}, u32[]{:S(2)}) collective-permute-start(bf16[576,128]{1,0:T(8,128)(2,1)S(1)} %pad_maximum_fusion), channel_id=1, source_target_pairs={{0,16},{16,32},{32,48},{48,64},{64,80},{80,96},{96,112},{1,17},{17... | collective-permute-start | bytes 442376 | tf_op jit(solution)/shard_map/ppermute | solution.py:261
  165.8 8.3 %collective-permute-start.1 = (f32[328,128]{1,0:T(8,128)S(1)}, f32[328,128]{1,0:T(8,128)S(1)}, u32[]{:S(2)}, u32[]{:S(2)}) collective-permute-start(f32[328,128]{1,0:T(8,128)S(1)} %get-tuple-element.11), channel_id=1, source_target_pairs={{0,16},{16,32},{32,48},{48,64},{64,80},{80,96},{96,112},{1,17},{17... | collective-permute-start | bytes 503816 | tf_op jit(solution)/shard_map/ppermute | solution.py:261
  167.7 8.7 %collective-permute-start.2 = (f32[328,128]{1,0:T(8,128)S(1)}, f32[328,128]{1,0:T(8,128)S(1)}, u32[]{:S(2)}, u32[]{:S(2)}) collective-permute-start(f32[328,128]{1,0:T(8,128)S(1)} %get-tuple-element.11), channel_id=1, source_target_pairs={{0,32},{16,48},{32,64},{48,80},{64,96},{80,112},{1,33},{17,49},{33... | collective-permute-start | bytes 503816 | tf_op jit(solution)/shard_map/ppermute | solution.py:261
  170.9 10.0 %collective-permute-start.3 = (f32[328,128]{1,0:T(8,128)S(1)}, f32[328,128]{1,0:T(8,128)S(1)}, u32[]{:S(2)}, u32[]{:S(2)}) collective-permute-start(f32[328,128]{1,0:T(8,128)S(1)} %get-tuple-element.11), channel_id=1, source_target_pairs={{0,48},{16,64},{32,80},{48,96},{64,112},{1,49},{17,65},{33,81},{49... | collective-permute-start | bytes 503816 | tf_op jit(solution)/shard_map/ppermute | solution.py:261
  172.8 11.6 %collective-permute-start.4 = (f32[328,128]{1,0:T(8,128)S(1)}, f32[328,128]{1,0:T(8,128)S(1)}, u32[]{:S(2)}, u32[]{:S(2)}) collective-permute-start(f32[328,128]{1,0:T(8,128)S(1)} %get-tuple-element.11), channel_id=1, source_target_pairs={{0,64},{16,80},{32,96},{48,112},{1,65},{17,81},{33,97},{49,113},{2... | collective-permute-start | bytes 503816 | tf_op jit(solution)/shard_map/ppermute | solution.py:261
  184.4 19.6 %copy-start.2 = (f32[320]{0:T(512)S(1)}, f32[320]{0:T(512)}, u32[]{:S(2)}) copy-start(f32[320]{0:T(512)} %param.22) | copy-start | bytes 3844
  188.8 5.6 %collective-permute-start.5 = (f32[1,3072]{1,0:T(1,128)S(1)}, f32[1,3072]{1,0:T(1,128)S(1)}, u32[]{:S(2)}, u32[]{:S(2)}) collective-permute-start(f32[1,3072]{1,0:T(1,128)S(1)} %get-tuple-element.15), channel_id=1, source_target_pairs={{0,1},{1,2},{2,3},{3,0},{4,5},{5,6},{6,7},{7,4},{8,9},{9,10},{10,1... | collective-permute-start | bytes 36872 | tf_op jit(solution)/shard_map/ppermute | solution.py:310
  190.3 5.2 %collective-permute-start.6 = (f32[1,3072]{1,0:T(1,128)S(1)}, f32[1,3072]{1,0:T(1,128)S(1)}, u32[]{:S(2)}, u32[]{:S(2)}) collective-permute-start(f32[1,3072]{1,0:T(1,128)S(1)} %get-tuple-element.15), channel_id=1, source_target_pairs={{0,2},{1,3},{2,0},{3,1},{4,6},{5,7},{6,4},{7,5},{8,10},{9,11},{10,... | collective-permute-start | bytes 36872 | tf_op jit(solution)/shard_map/ppermute | solution.py:310
  193.0 3.7 %collective-permute-start.7 = (f32[1,3072]{1,0:T(1,128)S(1)}, f32[1,3072]{1,0:T(1,128)S(1)}, u32[]{:S(2)}, u32[]{:S(2)}) collective-permute-start(f32[1,3072]{1,0:T(1,128)S(1)} %get-tuple-element.15), channel_id=1, source_target_pairs={{0,3},{1,0},{2,1},{3,2},{4,7},{5,4},{6,5},{7,6},{8,11},{9,8},{10,9... | collective-permute-start | bytes 36872 | tf_op jit(solution)/shard_map/ppermute | solution.py:310
  196.7 3.8 %collective-permute-start.10 = (f32[1,3072]{1,0:T(1,128)S(1)}, f32[1,3072]{1,0:T(1,128)S(1)}, u32[]{:S(2)}, u32[]{:S(2)}) collective-permute-start(f32[1,3072]{1,0:T(1,128)S(1)} %add_add_fusion.refs_0_), channel_id=1, source_target_pairs={{0,12},{1,13},{2,14},{3,15},{4,0},{5,1},{6,2},{7,3},{8,4},{9,5},{1... | collective-permute-start | bytes 36872 | tf_op jit(solution)/shard_map/ppermute | solution.py:311
  197.7 4.9 %collective-permute-start.8 = (f32[1,3072]{1,0:T(1,128)S(1)}, f32[1,3072]{1,0:T(1,128)S(1)}, u32[]{:S(2)}, u32[]{:S(2)}) collective-permute-start(f32[1,3072]{1,0:T(1,128)S(1)} %add_add_fusion.refs_0_), channel_id=1, source_target_pairs={{0,4},{1,5},{2,6},{3,7},{4,8},{5,9},{6,10},{7,11},{8,12},{9,13},{1... | collective-permute-start | bytes 36872 | tf_op jit(solution)/shard_map/ppermute | solution.py:311
  198.8 5.2 %collective-permute-start.9 = (f32[1,3072]{1,0:T(1,128)S(1)}, f32[1,3072]{1,0:T(1,128)S(1)}, u32[]{:S(2)}, u32[]{:S(2)}) collective-permute-start(f32[1,3072]{1,0:T(1,128)S(1)} %add_add_fusion.refs_0_), channel_id=1, source_target_pairs={{0,8},{1,9},{2,10},{3,11},{4,12},{5,13},{6,14},{7,15},{8,0},{9,1},... | collective-permute-start | bytes 36872 | tf_op jit(solution)/shard_map/ppermute | solution.py:311
Sparse Core Ops, SparseCore 0:
  9.5 108.2 all-gather.1

commit v3 on v2

v3 whole, which is shorter than its diff:
```python
import functools

import jax
import jax.numpy as jnp
from jax import lax
from jax.experimental import pallas as pl
from jax.experimental.pallas import tpu as pltpu
from jax.sharding import PartitionSpec as P

KCONV = 4
Q = 256
LANES = 128
SIDE = 4
LIMIT = 24 * 1024 * 1024
REACH = 4
F32 = jnp.float32
BF16 = jnp.bfloat16


def dot(a, b, contract=((1,), (0,))):
    return lax.dot_general(a, b, (contract, ((), ())), preferred_element_type=F32)


def thirds(a):
    high = a.astype(BF16)
    rest = a - high.astype(F32)
    middle = rest.astype(BF16)
    return high, middle, (rest - middle.astype(F32)).astype(BF16)


def silu(v):
    half = 0.5 * v
    return half + half * jnp.tanh(half)


def block_kernel(heads, by, moves, arrays, kept, where_ref, *refs):
    weight_ref = refs[0]
    pieces = refs[1 : 1 + arrays]
    seg_ref, taps_ref, vectors_ref, skip_ref = refs[1 + arrays : 5 + arrays]
    y_ref, reach_ref, map_ref, gate_ref, state_ref = refs[5 + arrays + kept : 10 + arrays + kept]
    rows, projected, before, state, total, sems = refs[10 + arrays + kept :]
    inner = y_ref.shape[0]
    count = y_ref.shape[1]
    head_width = inner // heads
    maps = inner
    steps = maps + 2 * LANES
    gates = steps + 16
    copies = []
    for number, (array, source, place, offset, size) in enumerate(moves):
        target = LANES - 16
        if place >= 0:
            slot = (where_ref[1] + (0, 3, 1, 2)[place]) % SIDE
            target = pl.multiple_of(LANES + slot * (count // SIDE) + offset, 16)
        copies.append(
            pltpu.make_async_copy(
                pieces[array].at[pl.ds(source, size)], rows.at[pl.ds(target, size)], sems.at[number]
            )
        )
    for copy in copies:
        copy.start()
    state[...] = jnp.zeros_like(state)
    total[...] = jnp.zeros_like(total)
    jj = lax.broadcasted_iota(jnp.int32, (Q, Q), 0)
    ii = lax.broadcasted_iota(jnp.int32, (Q, Q), 1)
    causal = jj <= ii
    upper = jnp.where(causal, 1.0, 0.0).astype(BF16)
    place = lax.broadcasted_iota(jnp.int32, (1, Q), 1)
    origin = (where_ref[0] + by + SIDE) % SIDE * count
    for copy in copies:
        copy.wait()
    conv_rows = inner + 2 * LANES
    before[...] = dot(weight_ref[0:conv_rows, :], rows[0:LANES, :], ((1,), (1,))).astype(BF16).astype(F32)

    def project(chunk):
        projected[chunk % 2] = dot(weight_ref[...], rows[LANES + chunk * Q : LANES + (chunk + 1) * Q, :], ((1,), (1,))).astype(BF16)

    def recur(chunk):
        raw_ref = projected.at[chunk % 2]
        columns = slice(chunk * Q, (chunk + 1) * Q)
        gate_ref[:, columns] = raw_ref[gates : gates + inner, :]
        seg = seg_ref[:, columns] - (origin + chunk * Q)
        keep = [jnp.broadcast_to(jnp.where(place - k >= seg, 1.0, 0.0), (8, Q)) for k in range(1, KCONV)]

        def convolved(raw, base):
            rows_at = slice(base, base + 8)
            ext = jnp.concatenate([before[rows_at, :], raw], 1)
            taps = [jnp.concatenate([taps_ref[k, rows_at, :]] * (Q // LANES), 1) for k in range(KCONV)]
            sums = taps[0] * raw
            for k in range(1, KCONV):
                sums = sums + taps[k] * keep[k - 1] * pltpu.roll(ext, k, 1)[:, LANES:]
            before[rows_at, :] = raw[:, Q - LANES :]
            return silu(sums)

        def conv_all(start, size, base):
            wide = raw_ref[start : start + size, :].astype(F32)
            return jnp.concatenate(
                [convolved(wide[at : at + 8, :], base + at) for at in range(0, size, 8)], 0
            ).astype(BF16)

        values = conv_all(0, inner, 0).astype(F32)
        input_map = conv_all(maps, LANES, inner)
        output_map = conv_all(maps + LANES, LANES, inner + LANES)
        map_ref[:, columns] = output_map
        v = raw_ref[steps : steps + 16, :].astype(F32)[0:8, :] + vectors_ref[0, :, 0:1]
        step = jnp.maximum(v, 0.0) + jnp.log(1.0 + jnp.exp(-jnp.abs(v)))
        decay = vectors_ref[1, :, 0:1] * step
        running = sum(dot(part, upper) for part in thirds(decay))
        running_t = running.T
        barred = jnp.where(causal & (jj >= seg), 0.0, -1e30)
        last = running[:, Q - 1 : Q]
        last_seg = seg[:, Q - 1 : Q]
        carried = jnp.where(seg < 0, jnp.exp(running), 0.0)
        tail = jnp.where(place >= last_seg, jnp.exp(last - running), 0.0) * step
        reach_ref[:, columns] = jnp.where(seg + chunk * Q < 0, jnp.exp(total[:, 0:1] + running), 0.0)
        total[...] = total[...] + last
        scores = dot(input_map, output_map, ((0,), (0,)))
        entering = dot(state[...].astype(BF16), output_map) if chunk else None
        for head in range(heads):
            at = slice(head * head_width, (head + 1) * head_width)
            mine = values[at, :]
            factor = jnp.exp(running[head : head + 1, :] - running_t[:, head : head + 1] + barred)
            mixing = (scores * factor).astype(BF16)
            y = dot((mine * step[head : head + 1, :]).astype(BF16), mixing)
            if chunk:
                y = y + entering[at, :] * carried[head : head + 1, :]
            y_ref[at, columns] = y + jnp.concatenate([skip_ref[at, :]] * (Q // LANES), 1) * mine
            tailed = (mine * tail[head : head + 1, :]).astype(BF16)
            added = dot(tailed, input_map, ((1,), (1,)))
            state[at, :] = carried[head : head + 1, Q - 1 : Q] * state[at, :] + added if chunk else added
        if (chunk + 1) * Q == count:
            state_ref[0, 0:inner, :] = state[...]
            whole_way = jnp.where(last_seg + chunk * Q < 0, jnp.exp(total[:, 0:1]), 0.0)
            state_ref[0, inner:, :] = jnp.broadcast_to(whole_way, (8, LANES))

    chunks = count // Q
    project(0)
    for chunk in range(chunks):
        if chunk + 1 < chunks:
            project(chunk + 1)
        recur(chunk)


def limits():
    return pltpu.CompilerParams(vmem_limit_bytes=LIMIT)


def whole(a):
    return pl.BlockSpec(a.shape, lambda i: (0,) * a.ndim)


def some(rows, columns, at=0):
    return pl.BlockSpec((rows, columns), lambda i: (at, i))


def block_pass(where, by, joined, pieces, moves, seg, taps, vectors, skip, earlier, heads, inner):
    count = seg.shape[1]
    size = count // SIDE
    anywhere = pl.BlockSpec(memory_space=pl.ANY)
    across = lambda r: pl.BlockSpec((r, size), lambda i, w: (0, (w[0] + by + SIDE) % SIDE))
    return pl.pallas_call(
        functools.partial(block_kernel, heads, by, moves, len(pieces), len(earlier)),
        grid_spec=pltpu.PrefetchScalarGridSpec(
            num_scalar_prefetch=1,
            grid=(1,),
            in_specs=[pl.BlockSpec(memory_space=pltpu.VMEM)] + [anywhere] * len(pieces)
            + [
                across(1),
                *[pl.BlockSpec(memory_space=pltpu.VMEM)] * 3,
            ]
            + [anywhere] * len(earlier),
            out_specs=[
                across(inner),
                across(8),
                across(LANES),
                across(inner),
                pl.BlockSpec((1, inner + 8, LANES), lambda i, w: ((w[0] + by + SIDE) % SIDE, 0, 0)),
            ],
            scratch_shapes=[
                pltpu.VMEM((LANES + size, joined.shape[1]), BF16),
                pltpu.VMEM((2, joined.shape[0], Q), BF16),
                pltpu.VMEM((inner + 2 * LANES, LANES), F32),
                pltpu.VMEM((inner, LANES), F32),
                pltpu.VMEM((8, LANES), F32),
                pltpu.SemaphoreType.DMA((len(moves),)),
            ],
        ),
        out_shape=[
            jax.ShapeDtypeStruct((inner, count), F32),
            jax.ShapeDtypeStruct((8, count), F32),
            jax.ShapeDtypeStruct((LANES, count), BF16),
            jax.ShapeDtypeStruct((inner, count), BF16),
            jax.ShapeDtypeStruct((SIDE, inner + 8, LANES), F32),
        ],
        input_output_aliases={6 + len(pieces) + i: i for i in range(len(earlier))},
        compiler_params=limits(),
        cost_estimate=pl.CostEstimate(
            flops=2 * size * joined.shape[0] * joined.shape[1] * 2, bytes_accessed=20 << 20, transcendentals=1 << 21
        ),
        name="block_pass",
    )(where, joined, *pieces, seg, taps, vectors, skip, *earlier)


def gate_kernel(heads, *refs):
    parts = refs[:REACH]
    state_ref, y_ref, reach_ref, map_ref, gate_ref, gated_ref, squares_ref, entering = refs[REACH:]
    inner = y_ref.shape[0]
    head_width = inner // heads
    block = pl.program_id(0)

    @pl.when(block == 0)
    def _():
        for head in range(heads):
            at = slice(head * head_width, (head + 1) * head_width)
            sofar = parts[-1][at, :].astype(F32)
            for part in parts[-2::-1]:
                sofar = part[at, :].astype(F32) + part[inner : inner + 16, :].astype(F32)[head : head + 1, :] * sofar
            entering[at, :] = sofar

    @pl.when(block > 0)
    def _():
        for head in range(heads):
            at = slice(head * head_width, (head + 1) * head_width)
            entering[at, :] = state_ref[0, at, :] + state_ref[0, inner + head : inner + head + 1, :] * entering[at, :]

    carried = dot(entering[...].astype(BF16), map_ref[...])
    squares = jnp.zeros((8, y_ref.shape[1]), F32)
    for head in range(heads):
        at = slice(head * head_width, (head + 1) * head_width)
        y = y_ref[at, :] + carried[at, :] * reach_ref[head : head + 1, :]
        gated = y * silu(gate_ref[at, :].astype(F32))
        gated_ref[at, :] = gated
        square = gated * gated
        squares = squares + sum(square[i : i + 8, :] for i in range(0, head_width, 8))
    squares_ref[...] = jnp.sum(squares, axis=0, keepdims=True)


def gate_pass(parts, states, y, reach, out_map, gating, heads):
    inner, count = y.shape
    step = count // SIDE
    return pl.pallas_call(
        functools.partial(gate_kernel, heads),
        grid=(SIDE,),
        in_specs=[whole(p) for p in parts]
        + [pl.BlockSpec((1,) + states.shape[1:], lambda i: (jnp.maximum(i - 1, 0), 0, 0))]
        + [some(inner, step), some(8, step), some(LANES, step), some(inner, step)],
        out_specs=[some(inner, step), some(1, step)],
        out_shape=[
            jax.ShapeDtypeStruct((inner, count), F32),
            jax.ShapeDtypeStruct((1, count), F32),
        ],
        scratch_shapes=[pltpu.VMEM((inner, LANES), F32)],
        compiler_params=limits(),
        name="gate_pass",
    )(*parts, states, y, reach, out_map, gating)


def norm_kernel(channels, squares_ref, gated_ref, gain_ref, out_ref):
    total = jnp.sum(squares_ref[...], axis=0, keepdims=True)
    scale = lax.rsqrt(total / channels + 1e-5)
    step = out_ref.shape[1]
    for at in range(0, out_ref.shape[0], 16):
        rows = slice(at, at + 16)
        gain = jnp.concatenate([gain_ref[rows, :]] * (step // LANES), 1)
        out_ref[rows, :] = (gated_ref[rows, :] * scale * gain).astype(BF16)


def norm_pass(squares, gated, gain, channels):
    inner, count = gated.shape
    step = 3 * Q
    return pl.pallas_call(
        functools.partial(norm_kernel, channels),
        grid=(count // step,),
        in_specs=[some(squares.shape[0], step), some(inner, step), whole(gain)],
        out_specs=some(inner, step),
        out_shape=jax.ShapeDtypeStruct((inner, count), BF16),
        compiler_params=limits(),
        name="norm_pass",
    )(squares, gated, gain)


def along_x(by):
    return [(z * SIDE + x, z * SIDE + (x + by) % SIDE) for z in range(SIDE) for x in range(SIDE)]


def along_z(by):
    return [(z * SIDE + x, (z + by) % SIDE * SIDE + x) for z in range(SIDE) for x in range(SIDE)]


def next_line(array, target):
    lines = lax.axis_size("seq") * SIDE
    pairs = [(i * SIDE + SIDE - 1, i * SIDE + SIDE + target) for i in range(lines - 1)]
    return lax.ppermute(array, ("seq", "tensor"), pairs)


def from_behind(array, by):
    length = lax.axis_size("seq")
    return lax.ppermute(array, "seq", [(i, i + by) for i in range(length - by)])


def on_device(
    hidden_rows,
    value_weight,
    gating_weight,
    state_weight,
    step_weight,
    value_kernel,
    state_kernel,
    step_bias,
    decay_log,
    skip_scale,
    norm_scale,
    document_lengths,
):
    members = lax.axis_size("tensor")
    count = hidden_rows.shape[0] * members
    inner = value_weight.shape[1]
    heads = step_weight.shape[1]
    head_width = inner // heads
    lanes = lambda a: jnp.broadcast_to(a[..., None], a.shape + (LANES,))
    joined = jnp.concatenate(
        [
            value_weight.T,
            state_weight.T,
            jnp.pad(step_weight.T, ((0, 16 - heads), (0, 0))),
            gating_weight.T,
        ],
        0,
    )
    taps = lanes(jnp.concatenate([value_kernel, state_kernel], 1))
    vectors = lanes(jnp.pad(jnp.stack([step_bias, -jnp.exp(decay_log)]), ((0, 0), (0, 8 - heads))))
    skip = lanes(jnp.repeat(skip_scale, head_width))
    gain = lanes(norm_scale)
    starts = jnp.cumsum(document_lengths) - document_lengths
    row_offset = lax.axis_index("seq") * count
    positions = row_offset + jnp.arange(count, dtype=jnp.int32)
    seg = jnp.max(jnp.where(positions[None, :] >= starts[:, None], starts[:, None], 0), axis=0) - row_offset
    seg = seg[None, :].astype(jnp.int32)

    own = hidden_rows
    size = own.shape[0]
    half = size // 2
    part_a, part_b = size * 5 // 12, size * 7 // 12
    cut = part_b * 4 // 7
    x_step = lambda a, by: lax.ppermute(a, "tensor", along_x(by))
    z_step = lambda a, by: lax.ppermute(a, "tensor", along_z(by))
    place = lax.axis_index("tensor")
    z, x = place // SIDE, place % SIDE

    x_back, x_ahead = x_step(own, 1), x_step(own, -1)
    z_back, z_ahead = z_step(own[part_a:], 1), z_step(own[part_a:], -1)
    tail = own[size - 16 :]
    rim_1, rim_3 = next_line(tail, 1), next_line(tail, 3)
    x_far_1 = x_step(jnp.concatenate([x_back[:half], rim_3], 0), 1)
    x_far_2 = x_step(jnp.concatenate([x_ahead[half:], rim_3], 0), -1)
    z_far_1, z_far_2 = z_step(z_back[:cut], 1), z_step(z_ahead[cut:], -1)
    first = jnp.concatenate([own[:part_a], x_back[:part_a], x_ahead[:part_a]], 0)
    first_back, first_ahead = z_step(first, 1), z_step(first, -1)
    x_far_1, x_far_2, z_back, z_ahead = lax.optimization_barrier((x_far_1, x_far_2, z_back, z_ahead))
    near = jnp.concatenate([z_back, z_ahead], 0)
    near_1, near_2 = x_step(near, 1), x_step(near, -1)
    rim = lax.select_n(x, x_far_1[half:], rim_1, x_far_2[half:], rim_3)
    where = jnp.stack([z, x]).astype(jnp.int32)

    def run(by, pieces, moves, earlier):
        return block_pass(where, by, joined, pieces, moves, seg, taps, vectors, skip, earlier, heads, inner)

    done = run(
        0,
        [own, x_back, x_ahead, x_far_1, x_far_2, rim],
        (
            (0, 0, 0, 0, size),
            (1, 0, 1, 0, size),
            (2, 0, 2, 0, size),
            (3, 0, 3, 0, half),
            (4, 0, 3, half, half),
            (5, 0, -1, 0, 16),
        ),
        [],
    )
    rim, done = lax.optimization_barrier((rim, done))
    second = jnp.concatenate([x_far_1[:part_a], rim], 0)
    second_back, second_ahead = z_step(second, 1), z_step(second, -1)
    near_far_1, near_far_2 = x_step(near_1[:part_b], 1), x_step(near_2[part_b:], -1)
    z_far_1, near_far_1, near_far_2 = lax.optimization_barrier((z_far_1, near_far_1, near_far_2))
    far = jnp.concatenate([z_far_1, z_far_2], 0)
    far_1, far_2 = x_step(far, 1), x_step(far, -1)
    last = jnp.concatenate([first_ahead[2 * part_a :], second_ahead], 0)
    line_far_1, line_far_2 = z_step(first_back[: 2 * part_a], 1), z_step(last, -1)
    far_far_1, far_far_2 = x_step(far_1[:cut], 1), x_step(far_2[cut:], -1)
    lines = tuple((0, part_a * i, i, 0, part_a) for i in range(3)) + ((1, 0, 3, 0, part_a), (1, part_a, -1, 0, 16))
    done = run(
        -1,
        [first_back, second_back, z_back, near_1, near_2, near_far_1],
        lines + tuple((2 + i, 0, i, part_a, part_b) for i in range(SIDE)),
        done,
    )
    done = run(
        1,
        [first_ahead, second_ahead, z_ahead, near_1, near_2, near_far_2],
        lines
        + (
            (2, 0, 0, part_a, part_b),
            (3, part_b, 1, part_a, part_b),
            (4, part_b, 2, part_a, part_b),
            (5, 0, 3, part_a, part_b),
        ),
        done,
    )
    y, reach, out_map, gating, states = run(
        2,
        [line_far_1, line_far_2, far, far_1, far_2, far_far_1, far_far_2],
        (
            (0, 0, 0, 0, part_a),
            (0, part_a, 1, 0, part_a),
            (1, 0, 2, 0, part_a),
            (1, part_a, 3, 0, part_a),
            (1, 2 * part_a, -1, 0, 16),
            (2, 0, 0, part_a, part_b),
            (3, 0, 1, part_a, part_b),
            (4, 0, 2, part_a, part_b),
            (5, 0, 3, part_a, cut),
            (6, 0, 3, part_a + cut, part_b - cut),
        ),
        done,
    )
    through, summary = states[0, inner:], states[0, :inner]
    for later in states[1:]:
        across = jnp.repeat(later[inner : inner + heads], head_width, axis=0)
        through, summary = through * later[inner:], later[:inner] + across * summary
    summary = jnp.concatenate([summary, through, jnp.zeros_like(through)], 0).astype(BF16)
    parts = [from_behind(summary, by) for by in range(1, REACH + 1)]
    gated, squares = gate_pass(parts, states, y, reach, out_map, gating, heads)
    shares = lax.all_to_all(jnp.broadcast_to(squares, (members, count)), "tensor", 0, 0, tiled=True)
    return norm_pass(shares, gated, gain, inner * members).T


def solution(mesh):
    in_specs = (
        P(("seq", "tensor"), None),
        P(None, "tensor"),
        P(None, "tensor"),
        P(),
        P(None, "tensor"),
        P(None, "tensor"),
        P(),
        P("tensor"),
        P("tensor"),
        P("tensor"),
        P("tensor"),
        P(),
    )
    out_specs = P("seq", "tensor")
    return jax.shard_map(
        on_device, mesh=mesh, in_specs=in_specs, out_specs=out_specs, check_vma=False
    )
```

time: 214 us -> 163 us (0.76)
  waiting for transfers between devices: 128 us -> 40.2 us
  starting transfers between devices: 19.4 us -> 50.1 us
  matrix products: 20.7 us -> 0 us
  Pallas kernels: 25.1 us -> 43.2 us
  between operations: 13.5 us -> 0.51 us
  blocking collectives: 0 us -> 11.5 us
  other arithmetic: 1.73 us -> 7.57 us
  local copies, waits for them, and re-layouts: 4.86 us -> 9.18 us
    all_gather x1 -> x0, waiting for transfers between devices: 107 us -> none  [on_device(): gathered = lax.all_gather(hidden_rows, 'tensor', axis=0, tiled=True)]
    ppermute x6 -> x24, starting transfers between devices: 9.23 us -> 43 us  [the longest x12 22.7 us: on_device(): x_step = lambda a, by: lax.ppermute(a, 'tensor', along_x(by))]
    ppermute x6 -> x24, waiting for transfers between devices: 5.94 us -> 33.4 us  [the longest x12 19.9 us: on_device(): x_step = lambda a, by: lax.ppermute(a, 'tensor', along_x(by))]
    dot_general x1 -> x0, matrix products: 20.7 us -> none  [dot(): lax.dot_general(a, b, (contract, ((), ())), preferred_element_type=F32)]
    pallas_call x3 -> x6, Pallas kernels: 25.1 us -> 43.2 us  [the longest x4 38.4 us: block_pass(): pl.pallas_call(functools.partial(block_kernel, heads, by, moves, len(piec...]
    all_to_all x0 -> x1, blocking collectives: none -> 11.5 us  [on_device(): lax.all_to_all(jnp.broadcast_to(squares, (members, count)), 'tensor', 0,...]
    ppermute x5 -> x4, waiting for transfers between devices: 14.5 us -> 6.84 us  [from_behind(): return lax.ppermute(array, 'seq', [(i, i + by) for i in range(length - by)])]
    concatenate x1 -> x6, other arithmetic: 0.01 us -> 3.76 us  [the longest x1 2.51 us: on_device(): jnp.concatenate([value_weight.T, state_weight.T, jnp.pad(step_weight.T, (...]
  transfers between devices with their start and end apart: 12 -> 28, of which waited for: 10 -> 8; matrix products, arithmetic and copies ran while one was open for 2% -> 10% of each run, Pallas kernels for 0% -> 18%
where the time goes in v3:
time: 163 us; the launch traced here: 162 us
  starting transfers between devices  50.1 us (31%)
  Pallas kernels  43.2 us (27%)
  waiting for transfers between devices  40.2 us (25%)
  blocking collectives  11.5 us (7%)
  local copies, waits for them, and re-layouts  9.18 us (6%)
  other arithmetic  7.57 us (5%)
    pallas_call x4, Pallas kernels, block_pass(): pl.pallas_call(functools.partial(block_kernel, heads, by, moves, len(piec...  38.4 us
    ppermute x12, starting transfers between devices, on_device(): x_step = lambda a, by: lax.ppermute(a, 'tensor', along_x(by))  22.7 us
    ppermute x12, waiting for transfers between devices, on_device(): x_step = lambda a, by: lax.ppermute(a, 'tensor', along_x(by))  19.9 us
    ppermute x10, starting transfers between devices, on_device(): z_step = lambda a, by: lax.ppermute(a, 'tensor', along_z(by))  18.4 us
    ppermute x10, waiting for transfers between devices, on_device(): z_step = lambda a, by: lax.ppermute(a, 'tensor', along_z(by))  13.4 us
    all_to_all x1, blocking collectives, on_device(): lax.all_to_all(jnp.broadcast_to(squares, (members, count)), 'tensor', 0,...  11.5 us
    ppermute x4, starting transfers between devices, from_behind(): return lax.ppermute(array, 'seq', [(i, i + by) for i in range(length - by)])  7.05 us
    ppermute x4, waiting for transfers between devices, from_behind(): return lax.ppermute(array, 'seq', [(i, i + by) for i in range(length - by)])  6.84 us
  transfers between devices with their start and end apart: 28, of which 8 were waited for; matrix products, arithmetic and copies ran while one was open for 10% of the time, Pallas kernels for 18%

profile of v3, /device:TPU:16, one launch (start us, length us, event | category | flops | bytes accessed | tf_op | source)
XLA Modules:
  0.0 162.3 jit_solution(6813535935309835073)
XLA Ops:
  0.0 1.5 collective-permute-start
  1.5 1.7 %collective-permute-start.1 = (bf16[192,2560]{1,0:T(8,128)(2,1)}, bf16[192,2560]{1,0:T(8,128)(2,1)S(1)}, u32[]{:S(2)}, u32[]{:S(2)}) collective-permute-start(bf16[192,2560]{1,0:T(8,128)(2,1)} %refs_1_.1), channel_id=1, source_target_pairs={{0,3},{1,0},{2,1},{3,2},{4,7},{5,4},{6,5},{7,6},{8,11},{9,8},{10,9... | collective-permute-start | bytes 2949128 | tf_op jit(solution)/shard_map/ppermute | solution.py:344
  3.2 2.0 %slice.130 = bf16[112,2560]{1,0:T(8,128)(2,1)} slice(bf16[192,2560]{1,0:T(8,128)(2,1)} %refs_1_.1), slice={[80:192], [0:2560]} | slice | bytes 1146880 | tf_op jit(solution)/shard_map/slice | solution.py:350
  5.2 1.9 %collective-permute-start.8 = (bf16[112,2560]{1,0:T(8,128)(2,1)}, bf16[112,2560]{1,0:T(8,128)(2,1)S(1)}, u32[]{:S(2)}, u32[]{:S(2)}) collective-permute-start(bf16[112,2560]{1,0:T(8,128)(2,1)} %slice.130), channel_id=1, source_target_pairs={{0,4},{1,5},{2,6},{3,7},{4,8},{5,9},{6,10},{7,11},{8,12},{9,13},{1... | collective-permute-start | bytes 1720328 | tf_op jit(solution)/shard_map/ppermute | solution.py:345
  7.1 2.1 %collective-permute-start.9 = (bf16[112,2560]{1,0:T(8,128)(2,1)}, bf16[112,2560]{1,0:T(8,128)(2,1)S(1)}, u32[]{:S(2)}, u32[]{:S(2)}) collective-permute-start(bf16[112,2560]{1,0:T(8,128)(2,1)} %slice.130), channel_id=1, source_target_pairs={{0,12},{1,13},{2,14},{3,15},{4,0},{5,1},{6,2},{7,3},{8,4},{9,5},{1... | collective-permute-start | bytes 1720328 | tf_op jit(solution)/shard_map/ppermute | solution.py:345
  9.2 1.5 slice.128
  10.8 1.3 collective-permute-start.5
  12.0 0.7 copy.35
  12.9 0.7 sub.22
  14.4 0.8 pad_maximum_fusion.5
  15.2 1.3 select_maximum_fusion
  16.4 1.0 slice.122
  17.5 2.4 %copy.34 = bf16[2560,256]{0,1:T(8,128)(2,1)} copy(bf16[2560,256]{1,0:T(8,128)(2,1)} %param.15) | data formatting | bytes 2621440 | tf_op args[3]
  20.1 2.5 %fusion.3.refs_0_ = bf16[912,2560]{1,0:T(8,128)(2,1)S(1)} fusion(bf16[5,2560]{1,0:T(8,128)(2,1)} %bitcast.59, bf16[320,2560]{1,0:T(8,128)(2,1)} %bitcast.57, bf16[256,2560]{1,0:T(8,128)(2,1)} %bitcast.56, bf16[320,2560]{1,0:T(8,128)(2,1)} %bitcast.58), kind=kLoop, calls=%fused_computation.5 | loop fusion | flops 28016640 | bytes 9282560 | tf_op jit(solution)/shard_map/concatenate | solution.py:320
  22.6 2.3 %collective-permute-done.refs_2_ = bf16[192,2560]{1,0:T(8,128)(2,1)S(1)} collective-permute-done((bf16[192,2560]{1,0:T(8,128)(2,1)}, bf16[192,2560]{1,0:T(8,128)(2,1)S(1)}, u32[]{:S(2)}, u32[]{:S(2)}) %collective-permute-start) | collective-permute-done | bytes 983072 | tf_op jit(solution)/shard_map/ppermute | solution.py:344
  25.7 1.0 pad_maximum_fusion.2
  26.7 1.0 collective-permute-start.6
  27.6 4.7 %collective-permute-start.7 = (bf16[112,2560]{1,0:T(8,128)(2,1)S(1)}, bf16[112,2560]{1,0:T(8,128)(2,1)S(1)}, u32[]{:S(2)}, u32[]{:S(2)}) collective-permute-start(bf16[112,2560]{1,0:T(8,128)(2,1)S(1)} %get-tuple-element.78), channel_id=1, source_target_pairs={{0,3},{1,0},{2,1},{3,2},{4,7},{5,4},{6,5},{7,6},{8,11},{9,8},{10,9... | collective-permute-start | bytes 1720328 | tf_op jit(solution)/shard_map/ppermute | solution.py:344
  32.5 2.0 %collective-permute-start.2 = (bf16[240,2560]{1,0:T(8,128)(2,1)S(1)}, bf16[240,2560]{1,0:T(8,128)(2,1)S(1)}, u32[]{:S(2)}, u32[]{:S(2)}) collective-permute-start(bf16[240,2560]{1,0:T(8,128)(2,1)S(1)} %pad_maximum_fusion), channel_id=1, source_target_pairs={{0,4},{1,5},{2,6},{3,7},{4,8},{5,9},{6,10},{7,11},{8,12},{9,13},{1... | collective-permute-start | bytes 3686408 | tf_op jit(solution)/shard_map/ppermute | solution.py:345
  34.5 1.3 collective-permute-start.4
  35.8 8.3 %collective-permute-done.6.refs_4_ = bf16[112,2560]{1,0:T(8,128)(2,1)S(1)} collective-permute-done((bf16[112,2560]{1,0:T(8,128)(2,1)S(1)}, bf16[112,2560]{1,0:T(8,128)(2,1)S(1)}, u32[]{:S(2)}, u32[]{:S(2)}) %collective-permute-start.6) | collective-permute-done | bytes 573472 | tf_op jit(solution)/shard_map/ppermute | solution.py:344
  44.2 2.1 %collective-permute-start.14 = (bf16[224,2560]{1,0:T(8,128)(2,1)S(1)}, bf16[224,2560]{1,0:T(8,128)(2,1)S(1)}, u32[]{:S(2)}, u32[]{:S(2)}) collective-permute-start(bf16[224,2560]{1,0:T(8,128)(2,1)S(1)} %constant_dynamic-update-slice_fusion), channel_id=1, source_target_pairs={{0,1},{1,2},{2,3},{3,0},{4,5},{5,6},{6,7},{7,4},{8,9},{9,10},{10,1... | collective-permute-start | bytes 3440648 | tf_op jit(solution)/shard_map/ppermute | solution.py:344
  46.3 1.2 collective-permute-start.16
  48.2 9.6 %block_pass.4 = (f32[320,3072]{1,0:T(8,128)S(1)}, f32[8,3072]{1,0:T(8,128)S(1)}, bf16[128,3072]{1,0:T(8,128)(2,1)S(1)}, bf16[320,3072]{1,0:T(8,128)(2,1)S(1)}, f32[4,328,128]{2,1,0:T(8,128)S(1)}) custom-call(s32[2]{0:T(128)S(1)} %pad_add_fusion.where_ref, bf16[912,2560]{1,0:T(8,128)(2,1)S(1)} %fusion.3.refs_0_, bf16[192,2560]{1,0:T(8,128)(2,1)S(1)} %copy-done, ...), custom_call_target="tpu_custom_call" | custom-call | flops 7172259840 | bytes 20971520 | tf_op jit(solution)/shard_map/block_pass/pallas_call | solution.py:160
  57.8 3.5 %collective-permute-start.11 = (bf16[96,2560]{1,0:T(8,128)(2,1)S(1)}, bf16[96,2560]{1,0:T(8,128)(2,1)S(1)}, u32[]{:S(2)}, u32[]{:S(2)}) collective-permute-start(bf16[96,2560]{1,0:T(8,128)(2,1)S(1)} %pad_maximum_fusion.4), channel_id=1, source_target_pairs={{0,12},{1,13},{2,14},{3,15},{4,0},{5,1},{6,2},{7,3},{8,4},{9,5},{1... | collective-permute-start | bytes 1474568 | tf_op jit(solution)/shard_map/ppermute | solution.py:345
  61.3 9.4 %collective-permute-done.14.refs_4_ = bf16[224,2560]{1,0:T(8,128)(2,1)S(1)} collective-permute-done((bf16[224,2560]{1,0:T(8,128)(2,1)S(1)}, bf16[224,2560]{1,0:T(8,128)(2,1)S(1)}, u32[]{:S(2)}, u32[]{:S(2)}) %collective-permute-start.14) | collective-permute-done | bytes 1146912 | tf_op jit(solution)/shard_map/ppermute | solution.py:344
  70.7 1.6 %collective-permute-start.15 = (bf16[112,2560]{1,0:T(8,128)(2,1)S(1)}, bf16[112,2560]{1,0:T(8,128)(2,1)S(1)}, u32[]{:S(2)}, u32[]{:S(2)}) collective-permute-start(bf16[112,2560]{1,0:T(8,128)(2,1)S(1)} %slice.164), channel_id=1, source_target_pairs={{0,1},{1,2},{2,3},{3,0},{4,5},{5,6},{6,7},{7,4},{8,9},{9,10},{10,1... | collective-permute-start | bytes 1720328 | tf_op jit(solution)/shard_map/ppermute | solution.py:344
  72.4 1.9 %collective-permute-start.17 = (bf16[112,2560]{1,0:T(8,128)(2,1)S(1)}, bf16[112,2560]{1,0:T(8,128)(2,1)S(1)}, u32[]{:S(2)}, u32[]{:S(2)}) collective-permute-start(bf16[112,2560]{1,0:T(8,128)(2,1)S(1)} %slice.165), channel_id=1, source_target_pairs={{0,3},{1,0},{2,1},{3,2},{4,7},{5,4},{6,5},{7,6},{8,11},{9,8},{10,9... | collective-permute-start | bytes 1720328 | tf_op jit(solution)/shard_map/ppermute | solution.py:344
  74.5 2.0 %collective-permute-start.13 = (bf16[64,2560]{1,0:T(8,128)(2,1)S(1)}, bf16[64,2560]{1,0:T(8,128)(2,1)S(1)}, u32[]{:S(2)}, u32[]{:S(2)}) collective-permute-start(bf16[64,2560]{1,0:T(8,128)(2,1)S(1)} %slice.163), channel_id=1, source_target_pairs={{0,4},{1,5},{2,6},{3,7},{4,8},{5,9},{6,10},{7,11},{8,12},{9,13},{1... | collective-permute-start | bytes 983048 | tf_op jit(solution)/shard_map/ppermute | solution.py:345
  76.5 3.5 %collective-permute-start.18 = (bf16[48,2560]{1,0:T(8,128)(2,1)S(1)}, bf16[48,2560]{1,0:T(8,128)(2,1)S(1)}, u32[]{:S(2)}, u32[]{:S(2)}) collective-permute-start(bf16[48,2560]{1,0:T(8,128)(2,1)S(1)} %slice.166), channel_id=1, source_target_pairs={{0,12},{1,13},{2,14},{3,15},{4,0},{5,1},{6,2},{7,3},{8,4},{9,5},{1... | collective-permute-start | bytes 737288 | tf_op jit(solution)/shard_map/ppermute | solution.py:345
  80.2 8.3 %collective-permute-done.13 = bf16[64,2560]{1,0:T(8,128)(2,1)S(1)} collective-permute-done((bf16[64,2560]{1,0:T(8,128)(2,1)S(1)}, bf16[64,2560]{1,0:T(8,128)(2,1)S(1)}, u32[]{:S(2)}, u32[]{:S(2)}) %collective-permute-start.13) | collective-permute-done | bytes 327712 | tf_op jit(solution)/shard_map/ppermute | solution.py:345
  88.5 2.0 %collective-permute-start.12 = (bf16[176,2560]{1,0:T(8,128)(2,1)S(1)}, bf16[176,2560]{1,0:T(8,128)(2,1)S(1)}, u32[]{:S(2)}, u32[]{:S(2)}) collective-permute-start(bf16[176,2560]{1,0:T(8,128)(2,1)S(1)} %pad_maximum_fusion.1), channel_id=1, source_target_pairs={{0,12},{1,13},{2,14},{3,15},{4,0},{5,1},{6,2},{7,3},{8,4},{9,5},{1... | collective-permute-start | bytes 2703368 | tf_op jit(solution)/shard_map/ppermute | solution.py:345
  90.7 3.2 %collective-permute-start.20 = (bf16[112,2560]{1,0:T(8,128)(2,1)S(1)}, bf16[112,2560]{1,0:T(8,128)(2,1)S(1)}, u32[]{:S(2)}, u32[]{:S(2)}) collective-permute-start(bf16[112,2560]{1,0:T(8,128)(2,1)S(1)} %constant_dynamic-update-slice_fusion.2.refs_3_), channel_id=1, source_target_pairs={{0,3},{1,0},{2,1},{3,2},{4,7},{5,4},{6,5},{7,6},{8,11},{9,8},{10,9... | collective-permute-start | bytes 1720328 | tf_op jit(solution)/shard_map/ppermute | solution.py:344
  93.9 5.1 %collective-permute-done.23.refs_2_ = bf16[96,2560]{1,0:T(8,128)(2,1)S(1)} collective-permute-done((bf16[96,2560]{1,0:T(8,128)(2,1)S(1)}, bf16[96,2560]{1,0:T(8,128)(2,1)S(1)}, u32[]{:S(2)}, u32[]{:S(2)}) %collective-permute-start.23) | collective-permute-done | bytes 491552 | tf_op jit(solution)/shard_map/ppermute | solution.py:345
  99.0 9.5 %block_pass.5 = (f32[320,3072]{1,0:T(8,128)S(1)}, f32[8,3072]{1,0:T(8,128)S(1)}, bf16[128,3072]{1,0:T(8,128)(2,1)S(1)}, bf16[320,3072]{1,0:T(8,128)(2,1)S(1)}, f32[4,328,128]{2,1,0:T(8,128)S(1)}) custom-call(s32[2]{0:T(128)S(1)} %pad_add_fusion.where_ref, ...), custom_call_target="tpu_custom_call", output_to_operand_aliasing={{0}: (12, {}), {1}: (13, {}), {2}: (14, {}), {3}: (15, {}),... | custom-call | flops 7172259840 | bytes 20971520 | tf_op jit(solution)/shard_map/block_pass/pallas_call | solution.py:160
  108.7 3.5 %collective-permute-start.22 = (bf16[48,2560]{1,0:T(8,128)(2,1)S(1)}, bf16[48,2560]{1,0:T(8,128)(2,1)S(1)}, u32[]{:S(2)}, u32[]{:S(2)}) collective-permute-start(bf16[48,2560]{1,0:T(8,128)(2,1)S(1)} %slice.168), channel_id=1, source_target_pairs={{0,3},{1,0},{2,1},{3,2},{4,7},{5,4},{6,5},{7,6},{8,11},{9,8},{10,9... | collective-permute-start | bytes 737288 | tf_op jit(solution)/shard_map/ppermute | solution.py:344
  112.2 9.5 %block_pass.6 = (f32[320,3072]{1,0:T(8,128)S(1)}, f32[8,3072]{1,0:T(8,128)S(1)}, bf16[128,3072]{1,0:T(8,128)(2,1)S(1)}, bf16[320,3072]{1,0:T(8,128)(2,1)S(1)}, f32[4,328,128]{2,1,0:T(8,128)S(1)}) custom-call(s32[2]{0:T(128)S(1)} %pad_add_fusion.where_ref, ...), custom_call_target="tpu_custom_call", output_to_operand_aliasing={{0}: (12, {}), {1}: (13, {}), {2}: (14, {}), {3}: (15, {}),... | custom-call | flops 7172259840 | bytes 20971520 | tf_op jit(solution)/shard_map/block_pass/pallas_call | solution.py:160
  121.7 9.8 %block_pass.7 = (f32[320,3072]{1,0:T(8,128)S(1)}, f32[8,3072]{1,0:T(8,128)S(1)}, bf16[128,3072]{1,0:T(8,128)(2,1)S(1)}, bf16[320,3072]{1,0:T(8,128)(2,1)S(1)}, f32[4,328,128]{2,1,0:T(8,128)S(1)}) custom-call(s32[2]{0:T(128)S(1)} %pad_add_fusion.where_ref, ...), custom_call_target="tpu_custom_call", output_to_operand_aliasing={{0}: (13, {}), {1}: (14, {}), {2}: (15, {}), {3}: (16, {}),... | custom-call | flops 7172259840 | bytes 20971520 | tf_op jit(solution)/shard_map/block_pass/pallas_call | solution.py:160
  131.8 1.9 %collective-permute-start.24 = (bf16[336,128]{1,0:T(8,128)(2,1)S(1)}, bf16[336,128]{1,0:T(8,128)(2,1)S(1)}, u32[]{:S(2)}, u32[]{:S(2)}) collective-permute-start(bf16[336,128]{1,0:T(8,128)(2,1)S(1)} %maximum_maximum_fusion), channel_id=1, source_target_pairs={{0,16},{16,32},{32,48},{48,64},{64,80},{80,96},{96,112},{1,17},{17... | collective-permute-start | bytes 258056 | tf_op jit(solution)/shard_map/ppermute | solution.py:297
  133.7 1.9 %collective-permute-start.25 = (bf16[336,128]{1,0:T(8,128)(2,1)S(1)}, bf16[336,128]{1,0:T(8,128)(2,1)S(1)}, u32[]{:S(2)}, u32[]{:S(2)}) collective-permute-start(bf16[336,128]{1,0:T(8,128)(2,1)S(1)} %maximum_maximum_fusion), channel_id=1, source_target_pairs={{0,32},{16,48},{32,64},{48,80},{64,96},{80,112},{1,33},{17,49},{33... | collective-permute-start | bytes 258056 | tf_op jit(solution)/shard_map/ppermute | solution.py:297
  135.6 1.9 %collective-permute-start.26 = (bf16[336,128]{1,0:T(8,128)(2,1)S(1)}, bf16[336,128]{1,0:T(8,128)(2,1)S(1)}, u32[]{:S(2)}, u32[]{:S(2)}) collective-permute-start(bf16[336,128]{1,0:T(8,128)(2,1)S(1)} %maximum_maximum_fusion), channel_id=1, source_target_pairs={{0,48},{16,64},{32,80},{48,96},{64,112},{1,49},{17,65},{33,81},{49... | collective-permute-start | bytes 258056 | tf_op jit(solution)/shard_map/ppermute | solution.py:297
  137.5 1.3 collective-permute-start.27
  138.9 1.6 collective-permute-done.25.refs_1_
  140.4 3.2 %collective-permute-done.26.refs_2_ = bf16[336,128]{1,0:T(8,128)(2,1)S(1)} collective-permute-done((bf16[336,128]{1,0:T(8,128)(2,1)S(1)}, bf16[336,128]{1,0:T(8,128)(2,1)S(1)}, u32[]{:S(2)}, u32[]{:S(2)}) %collective-permute-start.26) | collective-permute-done | bytes 86048 | tf_op jit(solution)/shard_map/ppermute | solution.py:297
  143.6 2.1 %collective-permute-done.27.refs_3_ = bf16[336,128]{1,0:T(8,128)(2,1)S(1)} collective-permute-done((bf16[336,128]{1,0:T(8,128)(2,1)S(1)}, bf16[336,128]{1,0:T(8,128)(2,1)S(1)}, u32[]{:S(2)}, u32[]{:S(2)}) %collective-permute-start.27) | collective-permute-done | bytes 86048 | tf_op jit(solution)/shard_map/ppermute | solution.py:297
  145.7 2.7 %gate_pass.1 = (f32[320,3072]{1,0:T(8,128)S(1)}, f32[1,3072]{1,0:T(1,128)S(1)}) custom-call(bf16[336,128]{1,0:T(8,128)(2,1)S(1)} %collective-permute-done.24.refs_0_, bf16[336,128]{1,0:T(8,128)(2,1)S(1)} %collective-permute-done.25.refs_1_, bf16[336,128]{1,0:T(8,128)(2,1)S(1)} %collective-permute-done.26.refs_2_, ...), custom_call_target="tpu_custom_call" | custom-call | tf_op jit(solution)/shard_map/gate_pass/pallas_call | solution.py:240
  148.5 11.5 %all_to_all.8 = f32[16,1,3072]{2,1,0:T(1,128)S(1)} all-to-all(f32[16,1,3072]{2,1,0:T(1,128)S(1)} %broadcast_in_dim.69), channel_id=1, replica_groups=mesh['seq'=8,'tensor'=16] {'tensor'}, dimensions={0} | all-to-all | bytes 393216 | tf_op jit(solution)/shard_map/all_to_all | solution.py:433
  160.2 2.2 %norm_pass.1 = bf16[320,3072]{1,0:T(8,128)(2,1)} custom-call(f32[16,3072]{1,0:T(8,128)S(1)} %bitcast.50, f32[320,3072]{1,0:T(8,128)S(1)} %get-tuple-element.74.gated_ref, f32[320,128]{1,0:T(8,128)S(1)} %broadcast_in_dim.70.gain_ref), custom_call_target="tpu_custom_call" | custom-call | tf_op jit(solution)/shard_map/norm_pass/pallas_call | solution.py:270
  (75 shorter events, 3.9 us)
Async XLA Ops:
  0.0 24.9 %collective-permute-start = (bf16[192,2560]{1,0:T(8,128)(2,1)}, bf16[192,2560]{1,0:T(8,128)(2,1)S(1)}, u32[]{:S(2)}, u32[]{:S(2)}) collective-permute-start(bf16[192,2560]{1,0:T(8,128)(2,1)} %refs_1_.1), channel_id=1, source_target_pairs={{0,1},{1,2},{2,3},{3,0},{4,5},{5,6},{6,7},{7,4},{8,9},{9,10},{10,1... | collective-permute-start | bytes 2949128 | tf_op jit(solution)/shard_map/ppermute | solution.py:344
  1.5 24.1 %collective-permute-start.1 = (bf16[192,2560]{1,0:T(8,128)(2,1)}, bf16[192,2560]{1,0:T(8,128)(2,1)S(1)}, u32[]{:S(2)}, u32[]{:S(2)}) collective-permute-start(bf16[192,2560]{1,0:T(8,128)(2,1)} %refs_1_.1), channel_id=1, source_target_pairs={{0,3},{1,0},{2,1},{3,2},{4,7},{5,4},{6,5},{7,6},{8,11},{9,8},{10,9... | collective-permute-start | bytes 2949128 | tf_op jit(solution)/shard_map/ppermute | solution.py:344
  5.2 14.7 %copy-start.3 = (f32[5]{0:T(128)S(1)}, f32[5]{0:T(128)}, u32[]{:S(2)}) copy-start(f32[5]{0:T(128)} %param.21) | copy-start | bytes 64
  5.2 27.3 %collective-permute-start.8 = (bf16[112,2560]{1,0:T(8,128)(2,1)}, bf16[112,2560]{1,0:T(8,128)(2,1)S(1)}, u32[]{:S(2)}, u32[]{:S(2)}) collective-permute-start(bf16[112,2560]{1,0:T(8,128)(2,1)} %slice.130), channel_id=1, source_target_pairs={{0,4},{1,5},{2,6},{3,7},{4,8},{5,9},{6,10},{7,11},{8,12},{9,13},{1... | collective-permute-start | bytes 1720328 | tf_op jit(solution)/shard_map/ppermute | solution.py:345
  7.1 27.4 %collective-permute-start.9 = (bf16[112,2560]{1,0:T(8,128)(2,1)}, bf16[112,2560]{1,0:T(8,128)(2,1)S(1)}, u32[]{:S(2)}, u32[]{:S(2)}) collective-permute-start(bf16[112,2560]{1,0:T(8,128)(2,1)} %slice.130), channel_id=1, source_target_pairs={{0,12},{1,13},{2,14},{3,15},{4,0},{5,1},{6,2},{7,3},{8,4},{9,5},{1... | collective-permute-start | bytes 1720328 | tf_op jit(solution)/shard_map/ppermute | solution.py:345
  10.8 14.9 %collective-permute-start.5 = (bf16[16,2560]{1,0:T(8,128)(2,1)}, bf16[16,2560]{1,0:T(8,128)(2,1)}, u32[]{:S(2)}, u32[]{:S(2)}) collective-permute-start(bf16[16,2560]{1,0:T(8,128)(2,1)} %slice.128), channel_id=1, source_target_pairs={{3,7},{7,11},{11,15},{15,19},{19,23},{23,27},{27,31},{31,35},{35,3... | collective-permute-start | bytes 245768 | tf_op jit(solution)/shard_map/ppermute | solution.py:292
  24.9 22.6 %collective-permute-start.10 = (bf16[16,2560]{1,0:T(8,128)(2,1)}, bf16[16,2560]{1,0:T(8,128)(2,1)S(1)}, u32[]{:S(2)}, u32[]{:S(2)}) collective-permute-start(bf16[16,2560]{1,0:T(8,128)(2,1)} %slice.128), channel_id=1, source_target_pairs={{3,5},{7,9},{11,13},{15,17},{19,21},{23,25},{27,29},{31,33},{35,37... | collective-permute-start | bytes 245768 | tf_op jit(solution)/shard_map/ppermute | solution.py:292
  26.7 17.4 %collective-permute-start.6 = (bf16[112,2560]{1,0:T(8,128)(2,1)S(1)}, bf16[112,2560]{1,0:T(8,128)(2,1)S(1)}, u32[]{:S(2)}, u32[]{:S(2)}) collective-permute-start(bf16[112,2560]{1,0:T(8,128)(2,1)S(1)} %get-tuple-element.79), channel_id=1, source_target_pairs={{0,1},{1,2},{2,3},{3,0},{4,5},{5,6},{6,7},{7,4},{8,9},{9,10},{10,1... | collective-permute-start | bytes 1720328 | tf_op jit(solution)/shard_map/ppermute | solution.py:344
  27.6 16.5 %collective-permute-start.7 = (bf16[112,2560]{1,0:T(8,128)(2,1)S(1)}, bf16[112,2560]{1,0:T(8,128)(2,1)S(1)}, u32[]{:S(2)}, u32[]{:S(2)}) collective-permute-start(bf16[112,2560]{1,0:T(8,128)(2,1)S(1)} %get-tuple-element.78), channel_id=1, source_target_pairs={{0,3},{1,0},{2,1},{3,2},{4,7},{5,4},{6,5},{7,6},{8,11},{9,8},{10,9... | collective-permute-start | bytes 1720328 | tf_op jit(solution)/shard_map/ppermute | solution.py:344
  32.5 44.0 %collective-permute-start.2 = (bf16[240,2560]{1,0:T(8,128)(2,1)S(1)}, bf16[240,2560]{1,0:T(8,128)(2,1)S(1)}, u32[]{:S(2)}, u32[]{:S(2)}) collective-permute-start(bf16[240,2560]{1,0:T(8,128)(2,1)S(1)} %pad_maximum_fusion), channel_id=1, source_target_pairs={{0,4},{1,5},{2,6},{3,7},{4,8},{5,9},{6,10},{7,11},{8,12},{9,13},{1... | collective-permute-start | bytes 3686408 | tf_op jit(solution)/shard_map/ppermute | solution.py:345
  34.5 40.0 %collective-permute-start.4 = (bf16[240,2560]{1,0:T(8,128)(2,1)S(1)}, bf16[240,2560]{1,0:T(8,128)(2,1)S(1)}, u32[]{:S(2)}, u32[]{:S(2)}) collective-permute-start(bf16[240,2560]{1,0:T(8,128)(2,1)S(1)} %pad_maximum_fusion), channel_id=1, source_target_pairs={{0,12},{1,13},{2,14},{3,15},{4,0},{5,1},{6,2},{7,3},{8,4},{9,5},{1... | collective-permute-start | bytes 3686408 | tf_op jit(solution)/shard_map/ppermute | solution.py:345
  44.1 3.9 %copy-start.1 = (f32[2,8]{1,0:T(2,128)S(1)}, f32[2,8]{1,0:T(2,128)}, u32[]{:S(2)}) copy-start(f32[2,8]{1,0:T(2,128)} %select_maximum_fusion) | copy-start | bytes 196
  44.2 4.0 %copy-start = (bf16[192,2560]{1,0:T(8,128)(2,1)S(1)}, bf16[192,2560]{1,0:T(8,128)(2,1)}, u32[]{:S(2)}) copy-start(bf16[192,2560]{1,0:T(8,128)(2,1)} %refs_1_.1) | copy-start | bytes 2949124
  44.2 26.5 %collective-permute-start.14 = (bf16[224,2560]{1,0:T(8,128)(2,1)S(1)}, bf16[224,2560]{1,0:T(8,128)(2,1)S(1)}, u32[]{:S(2)}, u32[]{:S(2)}) collective-permute-start(bf16[224,2560]{1,0:T(8,128)(2,1)S(1)} %constant_dynamic-update-slice_fusion), channel_id=1, source_target_pairs={{0,1},{1,2},{2,3},{3,0},{4,5},{5,6},{6,7},{7,4},{8,9},{9,10},{10,1... | collective-permute-start | bytes 3440648 | tf_op jit(solution)/shard_map/ppermute | solution.py:344
  46.3 26.1 %collective-permute-start.16 = (bf16[224,2560]{1,0:T(8,128)(2,1)S(1)}, bf16[224,2560]{1,0:T(8,128)(2,1)S(1)}, u32[]{:S(2)}, u32[]{:S(2)}) collective-permute-start(bf16[224,2560]{1,0:T(8,128)(2,1)S(1)} %constant_dynamic-update-slice_fusion), channel_id=1, source_target_pairs={{0,3},{1,0},{2,1},{3,2},{4,7},{5,4},{6,5},{7,6},{8,11},{9,8},{10,9... | collective-permute-start | bytes 3440648 | tf_op jit(solution)/shard_map/ppermute | solution.py:344
  57.8 22.2 %collective-permute-start.11 = (bf16[96,2560]{1,0:T(8,128)(2,1)S(1)}, bf16[96,2560]{1,0:T(8,128)(2,1)S(1)}, u32[]{:S(2)}, u32[]{:S(2)}) collective-permute-start(bf16[96,2560]{1,0:T(8,128)(2,1)S(1)} %pad_maximum_fusion.4), channel_id=1, source_target_pairs={{0,12},{1,13},{2,14},{3,15},{4,0},{5,1},{6,2},{7,3},{8,4},{9,5},{1... | collective-permute-start | bytes 1474568 | tf_op jit(solution)/shard_map/ppermute | solution.py:345
  70.7 19.7 %collective-permute-start.15 = (bf16[112,2560]{1,0:T(8,128)(2,1)S(1)}, bf16[112,2560]{1,0:T(8,128)(2,1)S(1)}, u32[]{:S(2)}, u32[]{:S(2)}) collective-permute-start(bf16[112,2560]{1,0:T(8,128)(2,1)S(1)} %slice.164), channel_id=1, source_target_pairs={{0,1},{1,2},{2,3},{3,0},{4,5},{5,6},{6,7},{7,4},{8,9},{9,10},{10,1... | collective-permute-start | bytes 1720328 | tf_op jit(solution)/shard_map/ppermute | solution.py:344
  72.4 18.1 %collective-permute-start.17 = (bf16[112,2560]{1,0:T(8,128)(2,1)S(1)}, bf16[112,2560]{1,0:T(8,128)(2,1)S(1)}, u32[]{:S(2)}, u32[]{:S(2)}) collective-permute-start(bf16[112,2560]{1,0:T(8,128)(2,1)S(1)} %slice.165), channel_id=1, source_target_pairs={{0,3},{1,0},{2,1},{3,2},{4,7},{5,4},{6,5},{7,6},{8,11},{9,8},{10,9... | collective-permute-start | bytes 1720328 | tf_op jit(solution)/shard_map/ppermute | solution.py:344
  74.5 14.0 %collective-permute-start.13 = (bf16[64,2560]{1,0:T(8,128)(2,1)S(1)}, bf16[64,2560]{1,0:T(8,128)(2,1)S(1)}, u32[]{:S(2)}, u32[]{:S(2)}) collective-permute-start(bf16[64,2560]{1,0:T(8,128)(2,1)S(1)} %slice.163), channel_id=1, source_target_pairs={{0,4},{1,5},{2,6},{3,7},{4,8},{5,9},{6,10},{7,11},{8,12},{9,13},{1... | collective-permute-start | bytes 983048 | tf_op jit(solution)/shard_map/ppermute | solution.py:345
  76.5 14.0 %collective-permute-start.18 = (bf16[48,2560]{1,0:T(8,128)(2,1)S(1)}, bf16[48,2560]{1,0:T(8,128)(2,1)S(1)}, u32[]{:S(2)}, u32[]{:S(2)}) collective-permute-start(bf16[48,2560]{1,0:T(8,128)(2,1)S(1)} %slice.166), channel_id=1, source_target_pairs={{0,12},{1,13},{2,14},{3,15},{4,0},{5,1},{6,2},{7,3},{8,4},{9,5},{1... | collective-permute-start | bytes 737288 | tf_op jit(solution)/shard_map/ppermute | solution.py:345
  80.0 19.0 %collective-permute-start.23 = (bf16[96,2560]{1,0:T(8,128)(2,1)S(1)}, bf16[96,2560]{1,0:T(8,128)(2,1)S(1)}, u32[]{:S(2)}, u32[]{:S(2)}) collective-permute-start(bf16[96,2560]{1,0:T(8,128)(2,1)S(1)} %pad_maximum_fusion.4), channel_id=1, source_target_pairs={{0,4},{1,5},{2,6},{3,7},{4,8},{5,9},{6,10},{7,11},{8,12},{9,13},{1... | collective-permute-start | bytes 1474568 | tf_op jit(solution)/shard_map/ppermute | solution.py:345
  88.5 33.2 %collective-permute-start.12 = (bf16[176,2560]{1,0:T(8,128)(2,1)S(1)}, bf16[176,2560]{1,0:T(8,128)(2,1)S(1)}, u32[]{:S(2)}, u32[]{:S(2)}) collective-permute-start(bf16[176,2560]{1,0:T(8,128)(2,1)S(1)} %pad_maximum_fusion.1), channel_id=1, source_target_pairs={{0,12},{1,13},{2,14},{3,15},{4,0},{5,1},{6,2},{7,3},{8,4},{9,5},{1... | collective-permute-start | bytes 2703368 | tf_op jit(solution)/shard_map/ppermute | solution.py:345
  90.5 31.2 %collective-permute-start.3 = (bf16[160,2560]{1,0:T(8,128)(2,1)S(1)}, bf16[160,2560]{1,0:T(8,128)(2,1)S(1)}, u32[]{:S(2)}, u32[]{:S(2)}) collective-permute-start(bf16[160,2560]{1,0:T(8,128)(2,1)S(1)} %slice.159), channel_id=1, source_target_pairs={{0,4},{1,5},{2,6},{3,7},{4,8},{5,9},{6,10},{7,11},{8,12},{9,13},{1... | collective-permute-start | bytes 2457608 | tf_op jit(solution)/shard_map/ppermute | solution.py:345
  90.6 17.9 %collective-permute-start.19 = (bf16[112,2560]{1,0:T(8,128)(2,1)S(1)}, bf16[112,2560]{1,0:T(8,128)(2,1)S(1)}, u32[]{:S(2)}, u32[]{:S(2)}) collective-permute-start(bf16[112,2560]{1,0:T(8,128)(2,1)S(1)} %constant_dynamic-update-slice_fusion.2.refs_3_), channel_id=1, source_target_pairs={{0,1},{1,2},{2,3},{3,0},{4,5},{5,6},{6,7},{7,4},{8,9},{9,10},{10,1... | collective-permute-start | bytes 1720328 | tf_op jit(solution)/shard_map/ppermute | solution.py:344
  90.7 18.0 %collective-permute-start.20 = (bf16[112,2560]{1,0:T(8,128)(2,1)S(1)}, bf16[112,2560]{1,0:T(8,128)(2,1)S(1)}, u32[]{:S(2)}, u32[]{:S(2)}) collective-permute-start(bf16[112,2560]{1,0:T(8,128)(2,1)S(1)} %constant_dynamic-update-slice_fusion.2.refs_3_), channel_id=1, source_target_pairs={{0,3},{1,0},{2,1},{3,2},{4,7},{5,4},{6,5},{7,6},{8,11},{9,8},{10,9... | collective-permute-start | bytes 1720328 | tf_op jit(solution)/shard_map/ppermute | solution.py:344
  108.5 13.2 %collective-permute-start.21 = (bf16[64,2560]{1,0:T(8,128)(2,1)S(1)}, bf16[64,2560]{1,0:T(8,128)(2,1)S(1)}, u32[]{:S(2)}, u32[]{:S(2)}) collective-permute-start(bf16[64,2560]{1,0:T(8,128)(2,1)S(1)} %slice.167), channel_id=1, source_target_pairs={{0,1},{1,2},{2,3},{3,0},{4,5},{5,6},{6,7},{7,4},{8,9},{9,10},{10,1... | collective-permute-start | bytes 983048 | tf_op jit(solution)/shard_map/ppermute | solution.py:344
  108.7 13.0 %collective-permute-start.22 = (bf16[48,2560]{1,0:T(8,128)(2,1)S(1)}, bf16[48,2560]{1,0:T(8,128)(2,1)S(1)}, u32[]{:S(2)}, u32[]{:S(2)}) collective-permute-start(bf16[48,2560]{1,0:T(8,128)(2,1)S(1)} %slice.168), channel_id=1, source_target_pairs={{0,3},{1,0},{2,1},{3,2},{4,7},{5,4},{6,5},{7,6},{8,11},{9,8},{10,9... | collective-permute-start | bytes 737288 | tf_op jit(solution)/shard_map/ppermute | solution.py:344
  131.8 7.1 %collective-permute-start.24 = (bf16[336,128]{1,0:T(8,128)(2,1)S(1)}, bf16[336,128]{1,0:T(8,128)(2,1)S(1)}, u32[]{:S(2)}, u32[]{:S(2)}) collective-permute-start(bf16[336,128]{1,0:T(8,128)(2,1)S(1)} %maximum_maximum_fusion), channel_id=1, source_target_pairs={{0,16},{16,32},{32,48},{48,64},{64,80},{80,96},{96,112},{1,17},{17... | collective-permute-start | bytes 258056 | tf_op jit(solution)/shard_map/ppermute | solution.py:297
  133.7 6.7 %collective-permute-start.25 = (bf16[336,128]{1,0:T(8,128)(2,1)S(1)}, bf16[336,128]{1,0:T(8,128)(2,1)S(1)}, u32[]{:S(2)}, u32[]{:S(2)}) collective-permute-start(bf16[336,128]{1,0:T(8,128)(2,1)S(1)} %maximum_maximum_fusion), channel_id=1, source_target_pairs={{0,32},{16,48},{32,64},{48,80},{64,96},{80,112},{1,33},{17,49},{33... | collective-permute-start | bytes 258056 | tf_op jit(solution)/shard_map/ppermute | solution.py:297
  135.6 8.0 %collective-permute-start.26 = (bf16[336,128]{1,0:T(8,128)(2,1)S(1)}, bf16[336,128]{1,0:T(8,128)(2,1)S(1)}, u32[]{:S(2)}, u32[]{:S(2)}) collective-permute-start(bf16[336,128]{1,0:T(8,128)(2,1)S(1)} %maximum_maximum_fusion), channel_id=1, source_target_pairs={{0,48},{16,64},{32,80},{48,96},{64,112},{1,49},{17,65},{33,81},{49... | collective-permute-start | bytes 258056 | tf_op jit(solution)/shard_map/ppermute | solution.py:297
  137.5 8.1 %collective-permute-start.27 = (bf16[336,128]{1,0:T(8,128)(2,1)S(1)}, bf16[336,128]{1,0:T(8,128)(2,1)S(1)}, u32[]{:S(2)}, u32[]{:S(2)}) collective-permute-start(bf16[336,128]{1,0:T(8,128)(2,1)S(1)} %maximum_maximum_fusion), channel_id=1, source_target_pairs={{0,64},{16,80},{32,96},{48,112},{1,65},{17,81},{33,97},{49,113},{2... | collective-permute-start | bytes 258056 | tf_op jit(solution)/shard_map/ppermute | solution.py:297
  145.7 14.4 %copy-start.2 = (f32[320]{0:T(512)S(1)}, f32[320]{0:T(512)}, u32[]{:S(2)}) copy-start(f32[320]{0:T(512)} %param.22) | copy-start | bytes 3844

commit v4 on v3

--- a/solution.py
+++ b/solution.py
@@ -71,10 +71,14 @@
     conv_rows = inner + 2 * LANES
     before[...] = dot(weight_ref[0:conv_rows, :], rows[0:LANES, :], ((1,), (1,))).astype(BF16).astype(F32)
 
-    def project(chunk):
-        projected[chunk % 2] = dot(weight_ref[...], rows[LANES + chunk * Q : LANES + (chunk + 1) * Q, :], ((1,), (1,))).astype(BF16)
+    def project(chunk, part=None):
+        ends = (0, inner, gates, gates + inner)
+        at = slice(0, gates + inner) if part is None else slice(ends[part], ends[part + 1])
+        now = rows[LANES + chunk * Q : LANES + (chunk + 1) * Q, :]
+        projected[chunk % 2, at, :] = dot(weight_ref[at, :], now, ((1,), (1,))).astype(BF16)
 
     def recur(chunk):
+        ahead = (lambda part: project(chunk + 1, part)) if (chunk + 1) * Q < count else (lambda part: None)
         raw_ref = projected.at[chunk % 2]
         columns = slice(chunk * Q, (chunk + 1) * Q)
         gate_ref[:, columns] = raw_ref[gates : gates + inner, :]
@@ -97,7 +101,9 @@
                 [convolved(wide[at : at + 8, :], base + at) for at in range(0, size, 8)], 0
             ).astype(BF16)
 
+        ahead(0)
         values = conv_all(0, inner, 0).astype(F32)
+        ahead(1)
         input_map = conv_all(maps, LANES, inner)
         output_map = conv_all(maps + LANES, LANES, inner + LANES)
         map_ref[:, columns] = output_map
@@ -115,6 +121,7 @@
         total[...] = total[...] + last
         scores = dot(input_map, output_map, ((0,), (0,)))
         entering = dot(state[...].astype(BF16), output_map) if chunk else None
+        ahead(2)
         for head in range(heads):
             at = slice(head * head_width, (head + 1) * head_width)
             mine = values[at, :]
@@ -135,8 +142,6 @@
     chunks = count // Q
     project(0)
     for chunk in range(chunks):
-        if chunk + 1 < chunks:
-            project(chunk + 1)
         recur(chunk)
 
 
@@ -383,10 +388,9 @@
     near_far_1, near_far_2 = x_step(near_1[:part_b], 1), x_step(near_2[part_b:], -1)
     z_far_1, near_far_1, near_far_2 = lax.optimization_barrier((z_far_1, near_far_1, near_far_2))
     far = jnp.concatenate([z_far_1, z_far_2], 0)
-    far_1, far_2 = x_step(far, 1), x_step(far, -1)
+    far_1, far_2, far_3 = x_step(far, 1), x_step(far, -1), x_step(far, 2)
     last = jnp.concatenate([first_ahead[2 * part_a :], second_ahead], 0)
     line_far_1, line_far_2 = z_step(first_back[: 2 * part_a], 1), z_step(last, -1)
-    far_far_1, far_far_2 = x_step(far_1[:cut], 1), x_step(far_2[cut:], -1)
     lines = tuple((0, part_a * i, i, 0, part_a) for i in range(3)) + ((1, 0, 3, 0, part_a), (1, part_a, -1, 0, 16))
     done = run(
         -1,
@@ -408,19 +412,15 @@
     )
     y, reach, out_map, gating, states = run(
         2,
-        [line_far_1, line_far_2, far, far_1, far_2, far_far_1, far_far_2],
+        [line_far_1, line_far_2, far, far_1, far_2, far_3],
         (
             (0, 0, 0, 0, part_a),
             (0, part_a, 1, 0, part_a),
             (1, 0, 2, 0, part_a),
             (1, part_a, 3, 0, part_a),
             (1, 2 * part_a, -1, 0, 16),
-            (2, 0, 0, part_a, part_b),
-            (3, 0, 1, part_a, part_b),
-            (4, 0, 2, part_a, part_b),
-            (5, 0, 3, part_a, cut),
-            (6, 0, 3, part_a + cut, part_b - cut),
-        ),
+        )
+        + tuple((2 + i, 0, i, part_a, part_b) for i in range(SIDE)),
         done,
     )
     through, summary = states[0, inner:], states[0, :inner]

time: 163 us -> 161 us (0.988)
  starting transfers between devices: 50.1 us -> 47.1 us
  blocking collectives: 11.5 us -> 13.9 us
    ppermute x12 -> x11, starting transfers between devices: 22.7 us -> 19.7 us  [on_device(): x_step = lambda a, by: lax.ppermute(a, 'tensor', along_x(by))]
    all_to_all x1, blocking collectives: 11.5 us -> 13.9 us  [on_device(): lax.all_to_all(jnp.broadcast_to(squares, (members, count)), 'tensor', 0,...]
    ppermute x12 -> x11, waiting for transfers between devices: 19.9 us -> 20.2 us  [on_device(): x_step = lambda a, by: lax.ppermute(a, 'tensor', along_x(by))]
  transfers between devices with their start and end apart: 28 -> 27, of which waited for: 8 -> 8; matrix products, arithmetic and copies ran while one was open for 10% -> 10% of each run, Pallas kernels for 18% -> 17%
where the time goes in v4:
time: 161 us
  starting transfers between devices  47.1 us (29%)
  Pallas kernels  42.2 us (26%)
  waiting for transfers between devices  40.5 us (25%)
  blocking collectives  13.9 us (9%)
  local copies, waits for them, and re-layouts  9.15 us (6%)
  other arithmetic  7.55 us (5%)
    pallas_call x4, Pallas kernels, block_pass(): pl.pallas_call(functools.partial(block_kernel, heads, by, moves, len(piec...  37.4 us
    ppermute x11, waiting for transfers between devices, on_device(): x_step = lambda a, by: lax.ppermute(a, 'tensor', along_x(by))  20.2 us
    ppermute x11, starting transfers between devices, on_device(): x_step = lambda a, by: lax.ppermute(a, 'tensor', along_x(by))  19.7 us
    ppermute x10, starting transfers between devices, on_device(): z_step = lambda a, by: lax.ppermute(a, 'tensor', along_z(by))  18.4 us
    all_to_all x1, blocking collectives, on_device(): lax.all_to_all(jnp.broadcast_to(squares, (members, count)), 'tensor', 0,...  13.9 us
    ppermute x10, waiting for transfers between devices, on_device(): z_step = lambda a, by: lax.ppermute(a, 'tensor', along_z(by))  13.4 us
    ppermute x4, starting transfers between devices, from_behind(): return lax.ppermute(array, 'seq', [(i, i + by) for i in range(length - by)])  7.05 us
    ppermute x4, waiting for transfers between devices, from_behind(): return lax.ppermute(array, 'seq', [(i, i + by) for i in range(length - by)])  6.84 us
  transfers between devices with their start and end apart: 27, of which 8 were waited for; matrix products, arithmetic and copies ran while one was open for 10% of the time, Pallas kernels for 17%

profile of v4, /device:TPU:16, one launch (start us, length us, event | category | flops | bytes accessed | tf_op | source)
XLA Modules:
  0.0 160.8 jit_solution(1001860109440406451)
XLA Ops:
  0.0 1.5 collective-permute-start
  1.5 1.7 %collective-permute-start.1 = (bf16[192,2560]{1,0:T(8,128)(2,1)}, bf16[192,2560]{1,0:T(8,128)(2,1)S(1)}, u32[]{:S(2)}, u32[]{:S(2)}) collective-permute-start(bf16[192,2560]{1,0:T(8,128)(2,1)} %refs_1_.1), channel_id=1, source_target_pairs={{0,3},{1,0},{2,1},{3,2},{4,7},{5,4},{6,5},{7,6},{8,11},{9,8},{10,9... | collective-permute-start | bytes 2949128 | tf_op jit(solution)/shard_map/ppermute | solution.py:349
  3.2 2.0 %slice.124 = bf16[112,2560]{1,0:T(8,128)(2,1)} slice(bf16[192,2560]{1,0:T(8,128)(2,1)} %refs_1_.1), slice={[80:192], [0:2560]} | slice | bytes 1146880 | tf_op jit(solution)/shard_map/slice | solution.py:355
  5.2 1.9 %collective-permute-start.8 = (bf16[112,2560]{1,0:T(8,128)(2,1)}, bf16[112,2560]{1,0:T(8,128)(2,1)S(1)}, u32[]{:S(2)}, u32[]{:S(2)}) collective-permute-start(bf16[112,2560]{1,0:T(8,128)(2,1)} %slice.124), channel_id=1, source_target_pairs={{0,4},{1,5},{2,6},{3,7},{4,8},{5,9},{6,10},{7,11},{8,12},{9,13},{1... | collective-permute-start | bytes 1720328 | tf_op jit(solution)/shard_map/ppermute | solution.py:350
  7.1 2.1 %collective-permute-start.9 = (bf16[112,2560]{1,0:T(8,128)(2,1)}, bf16[112,2560]{1,0:T(8,128)(2,1)S(1)}, u32[]{:S(2)}, u32[]{:S(2)}) collective-permute-start(bf16[112,2560]{1,0:T(8,128)(2,1)} %slice.124), channel_id=1, source_target_pairs={{0,12},{1,13},{2,14},{3,15},{4,0},{5,1},{6,2},{7,3},{8,4},{9,5},{1... | collective-permute-start | bytes 1720328 | tf_op jit(solution)/shard_map/ppermute | solution.py:350
  9.2 1.5 slice.122
  10.8 1.3 collective-permute-start.5
  12.1 0.7 copy.35
  12.9 0.7 sub.22
  13.6 0.7 negate_bitcast_fusion
  14.4 0.8 pad_maximum_fusion.5
  15.2 1.2 select_maximum_fusion
  16.4 1.0 slice.116
  17.5 2.4 %copy.34 = bf16[2560,256]{0,1:T(8,128)(2,1)} copy(bf16[2560,256]{1,0:T(8,128)(2,1)} %param.15) | data formatting | bytes 2621440 | tf_op args[3]
  20.0 2.5 %fusion.3.refs_0_ = bf16[912,2560]{1,0:T(8,128)(2,1)S(1)} fusion(bf16[5,2560]{1,0:T(8,128)(2,1)} %bitcast.59, bf16[320,2560]{1,0:T(8,128)(2,1)} %bitcast.57, bf16[256,2560]{1,0:T(8,128)(2,1)} %bitcast.56, bf16[320,2560]{1,0:T(8,128)(2,1)} %bitcast.58), kind=kLoop, calls=%fused_computation.5 | loop fusion | flops 28016640 | bytes 9282560 | tf_op jit(solution)/shard_map/concatenate | solution.py:325
  22.6 2.3 %collective-permute-done.refs_2_ = bf16[192,2560]{1,0:T(8,128)(2,1)S(1)} collective-permute-done((bf16[192,2560]{1,0:T(8,128)(2,1)}, bf16[192,2560]{1,0:T(8,128)(2,1)S(1)}, u32[]{:S(2)}, u32[]{:S(2)}) %collective-permute-start) | collective-permute-done | bytes 983072 | tf_op jit(solution)/shard_map/ppermute | solution.py:349
  25.7 1.0 pad_maximum_fusion.2
  26.7 1.0 collective-permute-start.6
  27.6 4.7 %collective-permute-start.7 = (bf16[112,2560]{1,0:T(8,128)(2,1)S(1)}, bf16[112,2560]{1,0:T(8,128)(2,1)S(1)}, u32[]{:S(2)}, u32[]{:S(2)}) collective-permute-start(bf16[112,2560]{1,0:T(8,128)(2,1)S(1)} %get-tuple-element.78), channel_id=1, source_target_pairs={{0,3},{1,0},{2,1},{3,2},{4,7},{5,4},{6,5},{7,6},{8,11},{9,8},{10,9... | collective-permute-start | bytes 1720328 | tf_op jit(solution)/shard_map/ppermute | solution.py:349
  32.5 2.0 %collective-permute-start.2 = (bf16[240,2560]{1,0:T(8,128)(2,1)S(1)}, bf16[240,2560]{1,0:T(8,128)(2,1)S(1)}, u32[]{:S(2)}, u32[]{:S(2)}) collective-permute-start(bf16[240,2560]{1,0:T(8,128)(2,1)S(1)} %pad_maximum_fusion), channel_id=1, source_target_pairs={{0,4},{1,5},{2,6},{3,7},{4,8},{5,9},{6,10},{7,11},{8,12},{9,13},{1... | collective-permute-start | bytes 3686408 | tf_op jit(solution)/shard_map/ppermute | solution.py:350
  34.5 1.3 collective-permute-start.4
  35.8 8.3 %collective-permute-done.6.refs_4_ = bf16[112,2560]{1,0:T(8,128)(2,1)S(1)} collective-permute-done((bf16[112,2560]{1,0:T(8,128)(2,1)S(1)}, bf16[112,2560]{1,0:T(8,128)(2,1)S(1)}, u32[]{:S(2)}, u32[]{:S(2)}) %collective-permute-start.6) | collective-permute-done | bytes 573472 | tf_op jit(solution)/shard_map/ppermute | solution.py:349
  44.2 2.1 %collective-permute-start.14 = (bf16[224,2560]{1,0:T(8,128)(2,1)S(1)}, bf16[224,2560]{1,0:T(8,128)(2,1)S(1)}, u32[]{:S(2)}, u32[]{:S(2)}) collective-permute-start(bf16[224,2560]{1,0:T(8,128)(2,1)S(1)} %constant_dynamic-update-slice_fusion), channel_id=1, source_target_pairs={{0,1},{1,2},{2,3},{3,0},{4,5},{5,6},{6,7},{7,4},{8,9},{9,10},{10,1... | collective-permute-start | bytes 3440648 | tf_op jit(solution)/shard_map/ppermute | solution.py:349
  46.3 1.2 collective-permute-start.16
  48.2 9.3 %block_pass.4 = (f32[320,3072]{1,0:T(8,128)S(1)}, f32[8,3072]{1,0:T(8,128)S(1)}, bf16[128,3072]{1,0:T(8,128)(2,1)S(1)}, bf16[320,3072]{1,0:T(8,128)(2,1)S(1)}, f32[4,328,128]{2,1,0:T(8,128)S(1)}) custom-call(s32[2]{0:T(128)S(1)} %pad_add_fusion.where_ref, bf16[912,2560]{1,0:T(8,128)(2,1)S(1)} %fusion.3.refs_0_, bf16[192,2560]{1,0:T(8,128)(2,1)S(1)} %copy-done, ...), custom_call_target="tpu_custom_call" | custom-call | flops 7172259840 | bytes 20971520 | tf_op jit(solution)/shard_map/block_pass/pallas_call | solution.py:165
  57.5 3.5 %collective-permute-start.11 = (bf16[96,2560]{1,0:T(8,128)(2,1)S(1)}, bf16[96,2560]{1,0:T(8,128)(2,1)S(1)}, u32[]{:S(2)}, u32[]{:S(2)}) collective-permute-start(bf16[96,2560]{1,0:T(8,128)(2,1)S(1)} %pad_maximum_fusion.4), channel_id=1, source_target_pairs={{0,12},{1,13},{2,14},{3,15},{4,0},{5,1},{6,2},{7,3},{8,4},{9,5},{1... | collective-permute-start | bytes 1474568 | tf_op jit(solution)/shard_map/ppermute | solution.py:350
  61.1 9.6 %collective-permute-done.14.refs_4_ = bf16[224,2560]{1,0:T(8,128)(2,1)S(1)} collective-permute-done((bf16[224,2560]{1,0:T(8,128)(2,1)S(1)}, bf16[224,2560]{1,0:T(8,128)(2,1)S(1)}, u32[]{:S(2)}, u32[]{:S(2)}) %collective-permute-start.14) | collective-permute-done | bytes 1146912 | tf_op jit(solution)/shard_map/ppermute | solution.py:349
  70.7 1.6 %collective-permute-start.15 = (bf16[112,2560]{1,0:T(8,128)(2,1)S(1)}, bf16[112,2560]{1,0:T(8,128)(2,1)S(1)}, u32[]{:S(2)}, u32[]{:S(2)}) collective-permute-start(bf16[112,2560]{1,0:T(8,128)(2,1)S(1)} %slice.156), channel_id=1, source_target_pairs={{0,1},{1,2},{2,3},{3,0},{4,5},{5,6},{6,7},{7,4},{8,9},{9,10},{10,1... | collective-permute-start | bytes 1720328 | tf_op jit(solution)/shard_map/ppermute | solution.py:349
  72.4 1.9 %collective-permute-start.17 = (bf16[112,2560]{1,0:T(8,128)(2,1)S(1)}, bf16[112,2560]{1,0:T(8,128)(2,1)S(1)}, u32[]{:S(2)}, u32[]{:S(2)}) collective-permute-start(bf16[112,2560]{1,0:T(8,128)(2,1)S(1)} %slice.157), channel_id=1, source_target_pairs={{0,3},{1,0},{2,1},{3,2},{4,7},{5,4},{6,5},{7,6},{8,11},{9,8},{10,9... | collective-permute-start | bytes 1720328 | tf_op jit(solution)/shard_map/ppermute | solution.py:349
  74.5 2.0 %collective-permute-start.13 = (bf16[64,2560]{1,0:T(8,128)(2,1)S(1)}, bf16[64,2560]{1,0:T(8,128)(2,1)S(1)}, u32[]{:S(2)}, u32[]{:S(2)}) collective-permute-start(bf16[64,2560]{1,0:T(8,128)(2,1)S(1)} %slice.155), channel_id=1, source_target_pairs={{0,4},{1,5},{2,6},{3,7},{4,8},{5,9},{6,10},{7,11},{8,12},{9,13},{1... | collective-permute-start | bytes 983048 | tf_op jit(solution)/shard_map/ppermute | solution.py:350
  76.5 3.5 %collective-permute-start.18 = (bf16[48,2560]{1,0:T(8,128)(2,1)S(1)}, bf16[48,2560]{1,0:T(8,128)(2,1)S(1)}, u32[]{:S(2)}, u32[]{:S(2)}) collective-permute-start(bf16[48,2560]{1,0:T(8,128)(2,1)S(1)} %slice.158), channel_id=1, source_target_pairs={{0,12},{1,13},{2,14},{3,15},{4,0},{5,1},{6,2},{7,3},{8,4},{9,5},{1... | collective-permute-start | bytes 737288 | tf_op jit(solution)/shard_map/ppermute | solution.py:350
  80.2 8.3 %collective-permute-done.13 = bf16[64,2560]{1,0:T(8,128)(2,1)S(1)} collective-permute-done((bf16[64,2560]{1,0:T(8,128)(2,1)S(1)}, bf16[64,2560]{1,0:T(8,128)(2,1)S(1)}, u32[]{:S(2)}, u32[]{:S(2)}) %collective-permute-start.13) | collective-permute-done | bytes 327712 | tf_op jit(solution)/shard_map/ppermute | solution.py:350
  88.5 2.0 %collective-permute-start.12 = (bf16[176,2560]{1,0:T(8,128)(2,1)S(1)}, bf16[176,2560]{1,0:T(8,128)(2,1)S(1)}, u32[]{:S(2)}, u32[]{:S(2)}) collective-permute-start(bf16[176,2560]{1,0:T(8,128)(2,1)S(1)} %pad_maximum_fusion.1), channel_id=1, source_target_pairs={{0,12},{1,13},{2,14},{3,15},{4,0},{5,1},{6,2},{7,3},{8,4},{9,5},{1... | collective-permute-start | bytes 2703368 | tf_op jit(solution)/shard_map/ppermute | solution.py:350
  90.7 3.2 %collective-permute-start.20 = (bf16[112,2560]{1,0:T(8,128)(2,1)S(1)}, bf16[112,2560]{1,0:T(8,128)(2,1)S(1)}, u32[]{:S(2)}, u32[]{:S(2)}) collective-permute-start(bf16[112,2560]{1,0:T(8,128)(2,1)S(1)} %constant_dynamic-update-slice_fusion.2.refs_3_), channel_id=1, source_target_pairs={{0,3},{1,0},{2,1},{3,2},{4,7},{5,4},{6,5},{7,6},{8,11},{9,8},{10,9... | collective-permute-start | bytes 1720328 | tf_op jit(solution)/shard_map/ppermute | solution.py:349
  93.9 5.1 %collective-permute-done.22.refs_2_ = bf16[96,2560]{1,0:T(8,128)(2,1)S(1)} collective-permute-done((bf16[96,2560]{1,0:T(8,128)(2,1)S(1)}, bf16[96,2560]{1,0:T(8,128)(2,1)S(1)}, u32[]{:S(2)}, u32[]{:S(2)}) %collective-permute-start.22) | collective-permute-done | bytes 491552 | tf_op jit(solution)/shard_map/ppermute | solution.py:350
  99.6 9.3 %block_pass.5 = (f32[320,3072]{1,0:T(8,128)S(1)}, f32[8,3072]{1,0:T(8,128)S(1)}, bf16[128,3072]{1,0:T(8,128)(2,1)S(1)}, bf16[320,3072]{1,0:T(8,128)(2,1)S(1)}, f32[4,328,128]{2,1,0:T(8,128)S(1)}) custom-call(s32[2]{0:T(128)S(1)} %pad_add_fusion.where_ref, ...), custom_call_target="tpu_custom_call", output_to_operand_aliasing={{0}: (12, {}), {1}: (13, {}), {2}: (14, {}), {3}: (15, {}),... | custom-call | flops 7172259840 | bytes 20971520 | tf_op jit(solution)/shard_map/block_pass/pallas_call | solution.py:165
  108.8 9.3 %block_pass.6 = (f32[320,3072]{1,0:T(8,128)S(1)}, f32[8,3072]{1,0:T(8,128)S(1)}, bf16[128,3072]{1,0:T(8,128)(2,1)S(1)}, bf16[320,3072]{1,0:T(8,128)(2,1)S(1)}, f32[4,328,128]{2,1,0:T(8,128)S(1)}) custom-call(s32[2]{0:T(128)S(1)} %pad_add_fusion.where_ref, ...), custom_call_target="tpu_custom_call", output_to_operand_aliasing={{0}: (12, {}), {1}: (13, {}), {2}: (14, {}), {3}: (15, {}),... | custom-call | flops 7172259840 | bytes 20971520 | tf_op jit(solution)/shard_map/block_pass/pallas_call | solution.py:165
  118.2 9.5 %block_pass.7 = (f32[320,3072]{1,0:T(8,128)S(1)}, f32[8,3072]{1,0:T(8,128)S(1)}, bf16[128,3072]{1,0:T(8,128)(2,1)S(1)}, bf16[320,3072]{1,0:T(8,128)(2,1)S(1)}, f32[4,328,128]{2,1,0:T(8,128)S(1)}) custom-call(s32[2]{0:T(128)S(1)} %pad_add_fusion.where_ref, ...), custom_call_target="tpu_custom_call", output_to_operand_aliasing={{0}: (12, {}), {1}: (13, {}), {2}: (14, {}), {3}: (15, {}),... | custom-call | flops 7172259840 | bytes 20971520 | tf_op jit(solution)/shard_map/block_pass/pallas_call | solution.py:165
  127.9 1.9 %collective-permute-start.23 = (bf16[336,128]{1,0:T(8,128)(2,1)S(1)}, bf16[336,128]{1,0:T(8,128)(2,1)S(1)}, u32[]{:S(2)}, u32[]{:S(2)}) collective-permute-start(bf16[336,128]{1,0:T(8,128)(2,1)S(1)} %maximum_maximum_fusion), channel_id=1, source_target_pairs={{0,16},{16,32},{32,48},{48,64},{64,80},{80,96},{96,112},{1,17},{17... | collective-permute-start | bytes 258056 | tf_op jit(solution)/shard_map/ppermute | solution.py:302
  129.8 1.9 %collective-permute-start.24 = (bf16[336,128]{1,0:T(8,128)(2,1)S(1)}, bf16[336,128]{1,0:T(8,128)(2,1)S(1)}, u32[]{:S(2)}, u32[]{:S(2)}) collective-permute-start(bf16[336,128]{1,0:T(8,128)(2,1)S(1)} %maximum_maximum_fusion), channel_id=1, source_target_pairs={{0,32},{16,48},{32,64},{48,80},{64,96},{80,112},{1,33},{17,49},{33... | collective-permute-start | bytes 258056 | tf_op jit(solution)/shard_map/ppermute | solution.py:302
  131.8 1.9 %collective-permute-start.25 = (bf16[336,128]{1,0:T(8,128)(2,1)S(1)}, bf16[336,128]{1,0:T(8,128)(2,1)S(1)}, u32[]{:S(2)}, u32[]{:S(2)}) collective-permute-start(bf16[336,128]{1,0:T(8,128)(2,1)S(1)} %maximum_maximum_fusion), channel_id=1, source_target_pairs={{0,48},{16,64},{32,80},{48,96},{64,112},{1,49},{17,65},{33,81},{49... | collective-permute-start | bytes 258056 | tf_op jit(solution)/shard_map/ppermute | solution.py:302
  133.7 1.3 collective-permute-start.26
  135.0 1.6 collective-permute-done.24.refs_1_
  136.6 3.2 %collective-permute-done.25.refs_2_ = bf16[336,128]{1,0:T(8,128)(2,1)S(1)} collective-permute-done((bf16[336,128]{1,0:T(8,128)(2,1)S(1)}, bf16[336,128]{1,0:T(8,128)(2,1)S(1)}, u32[]{:S(2)}, u32[]{:S(2)}) %collective-permute-start.25) | collective-permute-done | bytes 86048 | tf_op jit(solution)/shard_map/ppermute | solution.py:302
  139.7 2.1 %collective-permute-done.26.refs_3_ = bf16[336,128]{1,0:T(8,128)(2,1)S(1)} collective-permute-done((bf16[336,128]{1,0:T(8,128)(2,1)S(1)}, bf16[336,128]{1,0:T(8,128)(2,1)S(1)}, u32[]{:S(2)}, u32[]{:S(2)}) %collective-permute-start.26) | collective-permute-done | bytes 86048 | tf_op jit(solution)/shard_map/ppermute | solution.py:302
  141.8 2.7 %gate_pass.1 = (f32[320,3072]{1,0:T(8,128)S(1)}, f32[1,3072]{1,0:T(1,128)S(1)}) custom-call(bf16[336,128]{1,0:T(8,128)(2,1)S(1)} %collective-permute-done.23.refs_0_, bf16[336,128]{1,0:T(8,128)(2,1)S(1)} %collective-permute-done.24.refs_1_, bf16[336,128]{1,0:T(8,128)(2,1)S(1)} %collective-permute-done.25.refs_2_, ...), custom_call_target="tpu_custom_call" | custom-call | tf_op jit(solution)/shard_map/gate_pass/pallas_call | solution.py:245
  144.6 13.9 %all_to_all.8 = f32[16,1,3072]{2,1,0:T(1,128)S(1)} all-to-all(f32[16,1,3072]{2,1,0:T(1,128)S(1)} %broadcast_in_dim.69), channel_id=1, replica_groups=mesh['seq'=8,'tensor'=16] {'tensor'}, dimensions={0} | all-to-all | bytes 393216 | tf_op jit(solution)/shard_map/all_to_all | solution.py:433
  158.7 2.2 %norm_pass.1 = bf16[320,3072]{1,0:T(8,128)(2,1)} custom-call(f32[16,3072]{1,0:T(8,128)S(1)} %bitcast.50, f32[320,3072]{1,0:T(8,128)S(1)} %get-tuple-element.74.gated_ref, f32[320,128]{1,0:T(8,128)S(1)} %broadcast_in_dim.70.gain_ref), custom_call_target="tpu_custom_call" | custom-call | tf_op jit(solution)/shard_map/norm_pass/pallas_call | solution.py:275
  (71 shorter events, 3.7 us)
Async XLA Ops:
  0.0 24.9 %collective-permute-start = (bf16[192,2560]{1,0:T(8,128)(2,1)}, bf16[192,2560]{1,0:T(8,128)(2,1)S(1)}, u32[]{:S(2)}, u32[]{:S(2)}) collective-permute-start(bf16[192,2560]{1,0:T(8,128)(2,1)} %refs_1_.1), channel_id=1, source_target_pairs={{0,1},{1,2},{2,3},{3,0},{4,5},{5,6},{6,7},{7,4},{8,9},{9,10},{10,1... | collective-permute-start | bytes 2949128 | tf_op jit(solution)/shard_map/ppermute | solution.py:349
  1.5 24.1 %collective-permute-start.1 = (bf16[192,2560]{1,0:T(8,128)(2,1)}, bf16[192,2560]{1,0:T(8,128)(2,1)S(1)}, u32[]{:S(2)}, u32[]{:S(2)}) collective-permute-start(bf16[192,2560]{1,0:T(8,128)(2,1)} %refs_1_.1), channel_id=1, source_target_pairs={{0,3},{1,0},{2,1},{3,2},{4,7},{5,4},{6,5},{7,6},{8,11},{9,8},{10,9... | collective-permute-start | bytes 2949128 | tf_op jit(solution)/shard_map/ppermute | solution.py:349
  5.2 14.7 %copy-start.3 = (f32[5]{0:T(128)S(1)}, f32[5]{0:T(128)}, u32[]{:S(2)}) copy-start(f32[5]{0:T(128)} %param.21) | copy-start | bytes 64
  5.2 27.3 %collective-permute-start.8 = (bf16[112,2560]{1,0:T(8,128)(2,1)}, bf16[112,2560]{1,0:T(8,128)(2,1)S(1)}, u32[]{:S(2)}, u32[]{:S(2)}) collective-permute-start(bf16[112,2560]{1,0:T(8,128)(2,1)} %slice.124), channel_id=1, source_target_pairs={{0,4},{1,5},{2,6},{3,7},{4,8},{5,9},{6,10},{7,11},{8,12},{9,13},{1... | collective-permute-start | bytes 1720328 | tf_op jit(solution)/shard_map/ppermute | solution.py:350
  7.1 27.4 %collective-permute-start.9 = (bf16[112,2560]{1,0:T(8,128)(2,1)}, bf16[112,2560]{1,0:T(8,128)(2,1)S(1)}, u32[]{:S(2)}, u32[]{:S(2)}) collective-permute-start(bf16[112,2560]{1,0:T(8,128)(2,1)} %slice.124), channel_id=1, source_target_pairs={{0,12},{1,13},{2,14},{3,15},{4,0},{5,1},{6,2},{7,3},{8,4},{9,5},{1... | collective-permute-start | bytes 1720328 | tf_op jit(solution)/shard_map/ppermute | solution.py:350
  10.8 14.9 %collective-permute-start.5 = (bf16[16,2560]{1,0:T(8,128)(2,1)}, bf16[16,2560]{1,0:T(8,128)(2,1)}, u32[]{:S(2)}, u32[]{:S(2)}) collective-permute-start(bf16[16,2560]{1,0:T(8,128)(2,1)} %slice.122), channel_id=1, source_target_pairs={{3,7},{7,11},{11,15},{15,19},{19,23},{23,27},{27,31},{31,35},{35,3... | collective-permute-start | bytes 245768 | tf_op jit(solution)/shard_map/ppermute | solution.py:297
  24.9 22.6 %collective-permute-start.10 = (bf16[16,2560]{1,0:T(8,128)(2,1)}, bf16[16,2560]{1,0:T(8,128)(2,1)S(1)}, u32[]{:S(2)}, u32[]{:S(2)}) collective-permute-start(bf16[16,2560]{1,0:T(8,128)(2,1)} %slice.122), channel_id=1, source_target_pairs={{3,5},{7,9},{11,13},{15,17},{19,21},{23,25},{27,29},{31,33},{35,37... | collective-permute-start | bytes 245768 | tf_op jit(solution)/shard_map/ppermute | solution.py:297
  26.7 17.4 %collective-permute-start.6 = (bf16[112,2560]{1,0:T(8,128)(2,1)S(1)}, bf16[112,2560]{1,0:T(8,128)(2,1)S(1)}, u32[]{:S(2)}, u32[]{:S(2)}) collective-permute-start(bf16[112,2560]{1,0:T(8,128)(2,1)S(1)} %get-tuple-element.79), channel_id=1, source_target_pairs={{0,1},{1,2},{2,3},{3,0},{4,5},{5,6},{6,7},{7,4},{8,9},{9,10},{10,1... | collective-permute-start | bytes 1720328 | tf_op jit(solution)/shard_map/ppermute | solution.py:349
  27.6 16.5 %collective-permute-start.7 = (bf16[112,2560]{1,0:T(8,128)(2,1)S(1)}, bf16[112,2560]{1,0:T(8,128)(2,1)S(1)}, u32[]{:S(2)}, u32[]{:S(2)}) collective-permute-start(bf16[112,2560]{1,0:T(8,128)(2,1)S(1)} %get-tuple-element.78), channel_id=1, source_target_pairs={{0,3},{1,0},{2,1},{3,2},{4,7},{5,4},{6,5},{7,6},{8,11},{9,8},{10,9... | collective-permute-start | bytes 1720328 | tf_op jit(solution)/shard_map/ppermute | solution.py:349
  32.5 44.0 %collective-permute-start.2 = (bf16[240,2560]{1,0:T(8,128)(2,1)S(1)}, bf16[240,2560]{1,0:T(8,128)(2,1)S(1)}, u32[]{:S(2)}, u32[]{:S(2)}) collective-permute-start(bf16[240,2560]{1,0:T(8,128)(2,1)S(1)} %pad_maximum_fusion), channel_id=1, source_target_pairs={{0,4},{1,5},{2,6},{3,7},{4,8},{5,9},{6,10},{7,11},{8,12},{9,13},{1... | collective-permute-start | bytes 3686408 | tf_op jit(solution)/shard_map/ppermute | solution.py:350
  34.5 40.0 %collective-permute-start.4 = (bf16[240,2560]{1,0:T(8,128)(2,1)S(1)}, bf16[240,2560]{1,0:T(8,128)(2,1)S(1)}, u32[]{:S(2)}, u32[]{:S(2)}) collective-permute-start(bf16[240,2560]{1,0:T(8,128)(2,1)S(1)} %pad_maximum_fusion), channel_id=1, source_target_pairs={{0,12},{1,13},{2,14},{3,15},{4,0},{5,1},{6,2},{7,3},{8,4},{9,5},{1... | collective-permute-start | bytes 3686408 | tf_op jit(solution)/shard_map/ppermute | solution.py:350
  44.1 3.9 %copy-start.1 = (f32[2,8]{1,0:T(2,128)S(1)}, f32[2,8]{1,0:T(2,128)}, u32[]{:S(2)}) copy-start(f32[2,8]{1,0:T(2,128)} %select_maximum_fusion) | copy-start | bytes 196
  44.2 4.0 %copy-start = (bf16[192,2560]{1,0:T(8,128)(2,1)S(1)}, bf16[192,2560]{1,0:T(8,128)(2,1)}, u32[]{:S(2)}) copy-start(bf16[192,2560]{1,0:T(8,128)(2,1)} %refs_1_.1) | copy-start | bytes 2949124
  44.2 26.5 %collective-permute-start.14 = (bf16[224,2560]{1,0:T(8,128)(2,1)S(1)}, bf16[224,2560]{1,0:T(8,128)(2,1)S(1)}, u32[]{:S(2)}, u32[]{:S(2)}) collective-permute-start(bf16[224,2560]{1,0:T(8,128)(2,1)S(1)} %constant_dynamic-update-slice_fusion), channel_id=1, source_target_pairs={{0,1},{1,2},{2,3},{3,0},{4,5},{5,6},{6,7},{7,4},{8,9},{9,10},{10,1... | collective-permute-start | bytes 3440648 | tf_op jit(solution)/shard_map/ppermute | solution.py:349
  46.3 26.1 %collective-permute-start.16 = (bf16[224,2560]{1,0:T(8,128)(2,1)S(1)}, bf16[224,2560]{1,0:T(8,128)(2,1)S(1)}, u32[]{:S(2)}, u32[]{:S(2)}) collective-permute-start(bf16[224,2560]{1,0:T(8,128)(2,1)S(1)} %constant_dynamic-update-slice_fusion), channel_id=1, source_target_pairs={{0,3},{1,0},{2,1},{3,2},{4,7},{5,4},{6,5},{7,6},{8,11},{9,8},{10,9... | collective-permute-start | bytes 3440648 | tf_op jit(solution)/shard_map/ppermute | solution.py:349
  57.5 22.5 %collective-permute-start.11 = (bf16[96,2560]{1,0:T(8,128)(2,1)S(1)}, bf16[96,2560]{1,0:T(8,128)(2,1)S(1)}, u32[]{:S(2)}, u32[]{:S(2)}) collective-permute-start(bf16[96,2560]{1,0:T(8,128)(2,1)S(1)} %pad_maximum_fusion.4), channel_id=1, source_target_pairs={{0,12},{1,13},{2,14},{3,15},{4,0},{5,1},{6,2},{7,3},{8,4},{9,5},{1... | collective-permute-start | bytes 1474568 | tf_op jit(solution)/shard_map/ppermute | solution.py:350
  70.7 19.7 %collective-permute-start.15 = (bf16[112,2560]{1,0:T(8,128)(2,1)S(1)}, bf16[112,2560]{1,0:T(8,128)(2,1)S(1)}, u32[]{:S(2)}, u32[]{:S(2)}) collective-permute-start(bf16[112,2560]{1,0:T(8,128)(2,1)S(1)} %slice.156), channel_id=1, source_target_pairs={{0,1},{1,2},{2,3},{3,0},{4,5},{5,6},{6,7},{7,4},{8,9},{9,10},{10,1... | collective-permute-start | bytes 1720328 | tf_op jit(solution)/shard_map/ppermute | solution.py:349
  72.4 18.1 %collective-permute-start.17 = (bf16[112,2560]{1,0:T(8,128)(2,1)S(1)}, bf16[112,2560]{1,0:T(8,128)(2,1)S(1)}, u32[]{:S(2)}, u32[]{:S(2)}) collective-permute-start(bf16[112,2560]{1,0:T(8,128)(2,1)S(1)} %slice.157), channel_id=1, source_target_pairs={{0,3},{1,0},{2,1},{3,2},{4,7},{5,4},{6,5},{7,6},{8,11},{9,8},{10,9... | collective-permute-start | bytes 1720328 | tf_op jit(solution)/shard_map/ppermute | solution.py:349
  74.5 14.0 %collective-permute-start.13 = (bf16[64,2560]{1,0:T(8,128)(2,1)S(1)}, bf16[64,2560]{1,0:T(8,128)(2,1)S(1)}, u32[]{:S(2)}, u32[]{:S(2)}) collective-permute-start(bf16[64,2560]{1,0:T(8,128)(2,1)S(1)} %slice.155), channel_id=1, source_target_pairs={{0,4},{1,5},{2,6},{3,7},{4,8},{5,9},{6,10},{7,11},{8,12},{9,13},{1... | collective-permute-start | bytes 983048 | tf_op jit(solution)/shard_map/ppermute | solution.py:350
  76.5 14.0 %collective-permute-start.18 = (bf16[48,2560]{1,0:T(8,128)(2,1)S(1)}, bf16[48,2560]{1,0:T(8,128)(2,1)S(1)}, u32[]{:S(2)}, u32[]{:S(2)}) collective-permute-start(bf16[48,2560]{1,0:T(8,128)(2,1)S(1)} %slice.158), channel_id=1, source_target_pairs={{0,12},{1,13},{2,14},{3,15},{4,0},{5,1},{6,2},{7,3},{8,4},{9,5},{1... | collective-permute-start | bytes 737288 | tf_op jit(solution)/shard_map/ppermute | solution.py:350
  80.0 19.0 %collective-permute-start.22 = (bf16[96,2560]{1,0:T(8,128)(2,1)S(1)}, bf16[96,2560]{1,0:T(8,128)(2,1)S(1)}, u32[]{:S(2)}, u32[]{:S(2)}) collective-permute-start(bf16[96,2560]{1,0:T(8,128)(2,1)S(1)} %pad_maximum_fusion.4), channel_id=1, source_target_pairs={{0,4},{1,5},{2,6},{3,7},{4,8},{5,9},{6,10},{7,11},{8,12},{9,13},{1... | collective-permute-start | bytes 1474568 | tf_op jit(solution)/shard_map/ppermute | solution.py:350
  88.5 29.7 %collective-permute-start.12 = (bf16[176,2560]{1,0:T(8,128)(2,1)S(1)}, bf16[176,2560]{1,0:T(8,128)(2,1)S(1)}, u32[]{:S(2)}, u32[]{:S(2)}) collective-permute-start(bf16[176,2560]{1,0:T(8,128)(2,1)S(1)} %pad_maximum_fusion.1), channel_id=1, source_target_pairs={{0,12},{1,13},{2,14},{3,15},{4,0},{5,1},{6,2},{7,3},{8,4},{9,5},{1... | collective-permute-start | bytes 2703368 | tf_op jit(solution)/shard_map/ppermute | solution.py:350
  90.5 27.6 %collective-permute-start.3 = (bf16[160,2560]{1,0:T(8,128)(2,1)S(1)}, bf16[160,2560]{1,0:T(8,128)(2,1)S(1)}, u32[]{:S(2)}, u32[]{:S(2)}) collective-permute-start(bf16[160,2560]{1,0:T(8,128)(2,1)S(1)} %slice.151), channel_id=1, source_target_pairs={{0,4},{1,5},{2,6},{3,7},{4,8},{5,9},{6,10},{7,11},{8,12},{9,13},{1... | collective-permute-start | bytes 2457608 | tf_op jit(solution)/shard_map/ppermute | solution.py:350
  90.6 27.6 %collective-permute-start.19 = (bf16[112,2560]{1,0:T(8,128)(2,1)S(1)}, bf16[112,2560]{1,0:T(8,128)(2,1)S(1)}, u32[]{:S(2)}, u32[]{:S(2)}) collective-permute-start(bf16[112,2560]{1,0:T(8,128)(2,1)S(1)} %constant_dynamic-update-slice_fusion.2.refs_3_), channel_id=1, source_target_pairs={{0,1},{1,2},{2,3},{3,0},{4,5},{5,6},{6,7},{7,4},{8,9},{9,10},{10,1... | collective-permute-start | bytes 1720328 | tf_op jit(solution)/shard_map/ppermute | solution.py:349
  90.7 27.5 %collective-permute-start.20 = (bf16[112,2560]{1,0:T(8,128)(2,1)S(1)}, bf16[112,2560]{1,0:T(8,128)(2,1)S(1)}, u32[]{:S(2)}, u32[]{:S(2)}) collective-permute-start(bf16[112,2560]{1,0:T(8,128)(2,1)S(1)} %constant_dynamic-update-slice_fusion.2.refs_3_), channel_id=1, source_target_pairs={{0,3},{1,0},{2,1},{3,2},{4,7},{5,4},{6,5},{7,6},{8,11},{9,8},{10,9... | collective-permute-start | bytes 1720328 | tf_op jit(solution)/shard_map/ppermute | solution.py:349
  99.0 19.2 %collective-permute-start.21 = (bf16[112,2560]{1,0:T(8,128)(2,1)S(1)}, bf16[112,2560]{1,0:T(8,128)(2,1)S(1)}, u32[]{:S(2)}, u32[]{:S(2)}) collective-permute-start(bf16[112,2560]{1,0:T(8,128)(2,1)S(1)} %constant_dynamic-update-slice_fusion.2.refs_3_), channel_id=1, source_target_pairs={{0,2},{1,3},{2,0},{3,1},{4,6},{5,7},{6,4},{7,5},{8,10},{9,11},{10,... | collective-permute-start | bytes 1720328 | tf_op jit(solution)/shard_map/ppermute | solution.py:349
  127.9 7.1 %collective-permute-start.23 = (bf16[336,128]{1,0:T(8,128)(2,1)S(1)}, bf16[336,128]{1,0:T(8,128)(2,1)S(1)}, u32[]{:S(2)}, u32[]{:S(2)}) collective-permute-start(bf16[336,128]{1,0:T(8,128)(2,1)S(1)} %maximum_maximum_fusion), channel_id=1, source_target_pairs={{0,16},{16,32},{32,48},{48,64},{64,80},{80,96},{96,112},{1,17},{17... | collective-permute-start | bytes 258056 | tf_op jit(solution)/shard_map/ppermute | solution.py:302
  129.8 6.7 %collective-permute-start.24 = (bf16[336,128]{1,0:T(8,128)(2,1)S(1)}, bf16[336,128]{1,0:T(8,128)(2,1)S(1)}, u32[]{:S(2)}, u32[]{:S(2)}) collective-permute-start(bf16[336,128]{1,0:T(8,128)(2,1)S(1)} %maximum_maximum_fusion), channel_id=1, source_target_pairs={{0,32},{16,48},{32,64},{48,80},{64,96},{80,112},{1,33},{17,49},{33... | collective-permute-start | bytes 258056 | tf_op jit(solution)/shard_map/ppermute | solution.py:302
  131.8 8.0 %collective-permute-start.25 = (bf16[336,128]{1,0:T(8,128)(2,1)S(1)}, bf16[336,128]{1,0:T(8,128)(2,1)S(1)}, u32[]{:S(2)}, u32[]{:S(2)}) collective-permute-start(bf16[336,128]{1,0:T(8,128)(2,1)S(1)} %maximum_maximum_fusion), channel_id=1, source_target_pairs={{0,48},{16,64},{32,80},{48,96},{64,112},{1,49},{17,65},{33,81},{49... | collective-permute-start | bytes 258056 | tf_op jit(solution)/shard_map/ppermute | solution.py:302
  133.7 8.1 %collective-permute-start.26 = (bf16[336,128]{1,0:T(8,128)(2,1)S(1)}, bf16[336,128]{1,0:T(8,128)(2,1)S(1)}, u32[]{:S(2)}, u32[]{:S(2)}) collective-permute-start(bf16[336,128]{1,0:T(8,128)(2,1)S(1)} %maximum_maximum_fusion), channel_id=1, source_target_pairs={{0,64},{16,80},{32,96},{48,112},{1,65},{17,81},{33,97},{49,113},{2... | collective-permute-start | bytes 258056 | tf_op jit(solution)/shard_map/ppermute | solution.py:302
  141.8 16.7 %copy-start.2 = (f32[320]{0:T(512)S(1)}, f32[320]{0:T(512)}, u32[]{:S(2)}) copy-start(f32[320]{0:T(512)} %param.22) | copy-start | bytes 3844
